TPU v7x, 32 devices: a whole 2x2x4 slice. The times are simulated.
32 devices in a mesh: ctx: 4 (over y, core), exp: 8 (over z, x).
Axes of the slice: x: 2, y: 2, z: 4, core: 2. Of those that a mesh axis runs over, the one named last changes fastest.
Arguments:
- queries: bfloat16 [1024, 8192], P('exp', 'ctx'), may hold values from -180 to 180
- key_proj: bfloat16 [1024, 512], P('exp'), may hold values from -7 to 7
- value_matrix_rows: bfloat16 [1024, 512], P('exp'), may hold values from -6 to 6
- attn_grad: bfloat16 [1024, 8192], P('exp', 'ctx'), may hold values from -6 to 6
- moe_input: bfloat16 [1024, 4096], P('exp', 'ctx'), may hold values from -6 to 6
- moe_grad: bfloat16 [1024, 4096], P('exp', 'ctx'), may hold values from -6 to 6
- expert_ids: int32 [1024, 2], P('exp'), may hold values from 0 to 15, as said below
- route_weights: float32 [1024, 2], P('exp'), may hold values from 0.1 to 1
- gate_proj: bfloat16 [16, 4096, 768], P('exp', 'ctx'), may hold values from -0.09375 to 0.09375
- up_proj: bfloat16 [16, 4096, 768], P('exp', 'ctx'), may hold values from -0.09375 to 0.09375
- down_proj: bfloat16 [16, 768, 4096], P('exp', None, 'ctx'), may hold values from -0.21875 to 0.21875
Outputs:
- attn_out: bfloat16 [1024, 8192], P('exp', 'ctx')
- query_grad: bfloat16 [1024, 8192], P('exp', 'ctx')
- key_grad: bfloat16 [1024, 512], P('exp')
- value_grad: bfloat16 [1024, 512], P('exp')
- moe_out: bfloat16 [1024, 4096], P('exp', 'ctx')
- input_grad: bfloat16 [1024, 4096], P('exp', 'ctx')
Inputs may be any that keep to these rules, and one draw needn't show every extreme that they name: `expert_ids`: each row names 2 different experts. In each aligned block of 128 rows no expert is named more than 18 times, and one expert, the same in every block, is named exactly 18 times in every block.
All inputs are finite; a program needn't handle non-finite values.
Results may differ from a plain program's by a relative error of at most 0.019.
Values may be sent and summed in bfloat16 or wider, within the bound.
No kernel may reach another device: no remote copies, remote signals or barrier semaphores. Data moves between devices by JAX's collectives and lax.ppermute only.
A program may use at most 64 MiB of HBM per device.

v0:
```python
import jax
import jax.numpy as jnp
from jax import lax
from jax.sharding import PartitionSpec as P

HEAD_SIZE = 128


def gate_backward(hidden_grad, gate_full, up_full):
    sigmoid_gate = jax.nn.sigmoid(gate_full)
    activated = gate_full * sigmoid_gate
    gate_back = (
        hidden_grad * up_full * sigmoid_gate * (1.0 + gate_full * (1.0 - sigmoid_gate))
    ).astype(jnp.bfloat16)
    up_back = (hidden_grad * activated).astype(jnp.bfloat16)
    return (gate_back, up_back)


def activate(gate_full, up_full):
    return (jax.nn.silu(gate_full) * up_full).astype(jnp.bfloat16)


def body(
    queries,
    key_proj,
    value_matrix_rows,
    attn_grad,
    moe_input,
    moe_grad,
    expert_ids,
    route_weights,
    gate_proj,
    up_proj,
    down_proj,
):
    ctx_count = lax.axis_size("ctx")
    exp_count = lax.axis_size("exp")
    ctx_index = lax.axis_index("ctx")
    exp_index = lax.axis_index("exp")
    tok_count = queries.shape[0]
    head_dim = HEAD_SIZE
    heads_here = queries.shape[1] // head_dim
    kv_heads = key_proj.shape[1] // head_dim
    sharers = ctx_count // kv_heads
    kv_head = ctx_index // sharers
    seq_count = tok_count * exp_count
    score_scale = head_dim ** (-0.5)
    key_pick = lax.dynamic_slice_in_dim(key_proj, kv_head * head_dim, head_dim, 1)
    value_pick = lax.dynamic_slice_in_dim(value_matrix_rows, kv_head * head_dim, head_dim, 1)
    every_key, every_value = (
        lax.all_gather(key_pick, "exp", axis=0, tiled=True),
        lax.all_gather(value_pick, "exp", axis=0, tiled=True),
    )
    query_pos = exp_index * tok_count + jnp.arange(tok_count, dtype=jnp.int32)
    key_pos = jnp.arange(seq_count, dtype=jnp.int32)
    query_heads = queries.reshape(tok_count, heads_here, head_dim)
    cotan_heads = attn_grad.reshape(tok_count, heads_here, head_dim)
    scores = (
        jnp.einsum("rhd,kd->hrk", query_heads, every_key, preferred_element_type=jnp.float32)
        * score_scale
    )
    allowed = key_pos[None, :] <= query_pos[:, None]
    scores = jnp.where(allowed[None, :, :], scores, -jnp.inf)
    log_total = jax.nn.logsumexp(scores, axis=2, keepdims=True)
    attn_probs = jnp.exp(scores - log_total).astype(jnp.bfloat16)
    attended = jnp.einsum(
        "hrk,kd->rhd", attn_probs, every_value, preferred_element_type=jnp.float32
    ).astype(jnp.bfloat16)
    row_dot = jnp.sum(cotan_heads.astype(jnp.float32) * attended.astype(jnp.float32), axis=2)
    prob_grad = jnp.einsum(
        "rhd,kd->hrk", cotan_heads, every_value, preferred_element_type=jnp.float32
    )
    score_grad = (
        attn_probs.astype(jnp.float32) * (prob_grad - jnp.transpose(row_dot)[:, :, None])
    ).astype(jnp.bfloat16)
    query_back = (
        jnp.einsum("hrk,kd->rhd", score_grad, every_key, preferred_element_type=jnp.float32)
        * score_scale
    ).astype(jnp.bfloat16)
    key_term = (
        jnp.einsum("hrk,rhd->kd", score_grad, query_heads, preferred_element_type=jnp.float32)
        * score_scale
    )
    value_term = jnp.einsum(
        "hrk,rhd->kd", attn_probs, cotan_heads, preferred_element_type=jnp.float32
    )
    kv_term = jnp.concatenate([key_term, value_term], axis=1).reshape(
        exp_count, tok_count, 2 * head_dim
    )
    kv_pieces = lax.all_to_all(
        kv_term.astype(jnp.bfloat16), "exp", split_axis=0, concat_axis=0, tiled=True
    ).astype(kv_term.dtype)
    kv_summed = jnp.sum(kv_pieces, axis=0)
    kv_every = lax.all_gather(kv_summed.astype(jnp.bfloat16), "ctx", axis=1, tiled=True).astype(
        kv_summed.dtype
    )
    kv_every = kv_every.reshape(tok_count, kv_heads, sharers, 2, head_dim).sum(axis=2)
    key_grad = kv_every[:, :, 0, :].reshape(tok_count, kv_heads * head_dim).astype(jnp.bfloat16)
    value_grad = kv_every[:, :, 1, :].reshape(tok_count, kv_heads * head_dim).astype(jnp.bfloat16)
    width_here = moe_input.shape[1]
    local_experts = gate_proj.shape[0]
    top_count = expert_ids.shape[1]
    expert_total = local_experts * exp_count
    slot_count = 2 * ((tok_count + expert_total - 2) // (expert_total - 1))
    flat_ids = expert_ids.reshape(-1)
    flat_gain = route_weights.reshape(-1)
    targets = jnp.arange(expert_total, dtype=jnp.int32)
    chosen = flat_ids[None, :] == targets[:, None]

    def first_places(flags):
        return jnp.nonzero(flags, size=slot_count, fill_value=0)[0]

    places = jax.vmap(first_places)(chosen)
    filled = jnp.arange(slot_count)[None, :] < jnp.sum(chosen, axis=1)[:, None]
    slot_token = (places // top_count).astype(jnp.int32)
    picked_gain = flat_gain[places]
    slot_gain = jnp.where(filled, picked_gain, jnp.zeros_like(picked_gain))
    send_rows = moe_input[slot_token].reshape(exp_count, local_experts, slot_count, width_here)
    send_scaled = (moe_grad[slot_token].astype(jnp.float32) * slot_gain[:, :, None]).astype(
        jnp.bfloat16
    )
    send_scaled = send_scaled.reshape(exp_count, local_experts, slot_count, width_here)
    recv_rows, recv_scaled = (
        lax.all_to_all(send_rows, "exp", split_axis=0, concat_axis=0, tiled=True),
        lax.all_to_all(send_scaled, "exp", split_axis=0, concat_axis=0, tiled=True),
    )
    gate_part = jnp.einsum(
        "sacd,adf->sacf", recv_rows, gate_proj, preferred_element_type=jnp.float32
    )
    up_part = jnp.einsum("sacd,adf->sacf", recv_rows, up_proj, preferred_element_type=jnp.float32)
    hidden_part = jnp.einsum(
        "sacd,afd->sacf", recv_scaled, down_proj, preferred_element_type=jnp.float32
    )
    gate_full, up_full = lax.psum((gate_part, up_part), "ctx")
    hidden = activate(gate_full, up_full)
    hidden_grad = lax.psum(hidden_part, "ctx")
    gate_back, up_back = gate_backward(hidden_grad, gate_full, up_full)
    route_out = jnp.einsum(
        "sacf,afd->sacd", hidden, down_proj, preferred_element_type=jnp.float32
    ).astype(jnp.bfloat16)
    route_in = (
        jnp.einsum("sacf,adf->sacd", gate_back, gate_proj, preferred_element_type=jnp.float32)
        + jnp.einsum("sacf,adf->sacd", up_back, up_proj, preferred_element_type=jnp.float32)
    ).astype(jnp.bfloat16)
    back_out, back_in = (
        lax.all_to_all(route_out, "exp", split_axis=0, concat_axis=0, tiled=True),
        lax.all_to_all(route_in, "exp", split_axis=0, concat_axis=0, tiled=True),
    )
    slot_flat = slot_token.reshape(-1)
    member = (
        slot_flat[:, None] == jnp.arange(tok_count, dtype=jnp.int32)[None, :]
    ) & filled.reshape(-1)[:, None]
    weight_table = jnp.where(member, slot_gain.reshape(-1)[:, None], 0.0)
    moe_out = jnp.einsum(
        "pt,pd->td",
        weight_table,
        back_out.reshape(-1, width_here).astype(jnp.float32),
        precision=lax.Precision.HIGHEST,
        preferred_element_type=jnp.float32,
    ).astype(jnp.bfloat16)
    input_grad = jnp.einsum(
        "pt,pd->td",
        member.astype(jnp.bfloat16),
        back_in.reshape(-1, width_here),
        preferred_element_type=jnp.float32,
    ).astype(jnp.bfloat16)
    attn_out = attended.reshape(tok_count, heads_here * head_dim)
    query_grad = query_back.reshape(tok_count, heads_here * head_dim)
    return (attn_out, query_grad, key_grad, value_grad, moe_out, input_grad)


def solution(mesh):
    placed = (
        P("exp", "ctx"),
        P("exp", None),
        P("exp", None),
        P("exp", "ctx"),
        P("exp", "ctx"),
        P("exp", "ctx"),
        P("exp", None),
        P("exp", None),
        P("exp", "ctx", None),
        P("exp", "ctx", None),
        P("exp", None, "ctx"),
    )
    return jax.shard_map(
        body,
        mesh=mesh,
        in_specs=placed,
        out_specs=(
            P("exp", "ctx"),
            P("exp", "ctx"),
            P("exp", None),
            P("exp", None),
            P("exp", "ctx"),
            P("exp", "ctx"),
        ),
        check_vma=False,
    )
```

profile of v0, /device:TPU:0, one launch (start us, length us, event | category | flops | bytes accessed | tf_op | source)
XLA Modules:
  0.0 283.8 jit_solution(5348176369824208283)
XLA Ops:
  10.9 28.4 %scatter_custom_fusion = s32[288]{0:T(512)S(1)} fusion(s32[4096]{0:T(1024)S(1)} %bitcast.139, s32[4096]{0:T(1024)S(1)} %broadcast.386, s32[]{:T(128)} %constant.84.clone.1), kind=kCustom, calls=%fused_computation.114 | custom fusion | flops 4096 | bytes 1156
  39.9 2.6 gather_fusion.1
  42.5 2.1 reshape.404
  44.7 2.6 copy.100
  47.3 7.2 %all-to-all-start.1 = ((bf16[8,2,18,1024]{3,1,2,0:T(2,128)(2,1)}), bf16[8,2,18,1024]{3,1,2,0:T(2,128)(2,1)}, u32[]{:S(2)}, u32[]{:S(2)}) async-start(bf16[8,2,18,1024]{3,1,2,0:T(2,128)(2,1)} %copy.100), calls=%async_computation.1 | async-start | bytes 1179648 | tf_op jit(solution)/shard_map/all_to_all | solution.py:124
  55.6 2.5 gather_fusion
  58.7 2.6 gather_fusion.2
  61.3 2.4 reshape.411
  64.5 31.3 %all_gather.10 = bf16[1024,128]{1,0:T(8,128)(2,1)S(1)} all-gather(bf16[128,128]{1,0:T(8,128)(2,1)S(1)} %constant_dynamic-slice_fusion), channel_id=1, replica_groups=mesh['ctx'=4,'exp'=8] {'exp'}, dimensions={0}, use_global_device_ids=true | all-gather | bytes 294912 | tf_op jit(solution)/shard_map/all_gather | solution.py:51
  97.9 2.3 fusion.2
  100.3 2.8 %exponential_reduce_fusion = f32[16,128]{1,0:T(8,128)} fusion(f32[1024,128,16]{1,0,2:T(8,128)S(1)} %get-tuple-element.40, f32[16,128]{1,0:T(8,128)S(1)} %is-finite_select_fusion, pred[128,1024]{0,1:T(8,128)(4,1)S(1)} %iota_compare_fusion), kind=kLoop, calls=%fused_computation.9 | loop fusion | flops 8386560 | bytes 8536064 | tf_op jit(solution)/shard_map/reduce_sum | solution.py:64
  110.8 7.2 %exponential_convert_fusion = bf16[16,128,1024]{1,2,0:T(8,128)(2,1)} fusion(f32[1024,128,16]{1,0,2:T(8,128)} %copy-done.3, f32[16,128]{1,0:T(8,128)S(1)} %log_add_fusion, pred[128,1024]{0,1:T(8,128)(4,1)S(1)} %iota_compare_fusion), kind=kLoop, calls=%fused_computation.8 | loop fusion | flops 8388608 | bytes 12722176 | tf_op jit(solution)/shard_map/convert_element_type | solution.py:65
  117.9 5.4 %all-to-all-start.3 = ((bf16[8,2,18,1024]{3,1,2,0:T(2,128)(2,1)}), bf16[8,2,18,1024]{3,1,2,0:T(2,128)(2,1)}, u32[]{:S(2)}, u32[]{:S(2)}) async-start(bf16[8,2,18,1024]{3,1,2,0:T(2,128)(2,1)} %copy.105), calls=%async_computation.3 | async-start | bytes 1179648 | tf_op jit(solution)/shard_map/all_to_all | solution.py:125
  123.4 4.6 %fusion.37 = bf16[1024,128]{0,1:T(8,128)(2,1)} fusion(bf16[16,128,1024]{1,2,0:T(8,128)(2,1)} %exponential_convert_fusion, bf16[128,16,128]{0,2,1:T(8,128)(2,1)} %bitcast.129), kind=kOutput, calls=%fused_computation.37 | convolution fusion | flops 537001984 | bytes 4980736 | tf_op jit(solution)/shard_map/hrk,rhd->kd/dot_general | solution.py:84
  128.1 3.0 %fusion.20 = f32[8,2,18,768]{3,2,0,1:T(8,128)} fusion(bf16[2,1024,768]{2,1,0:T(8,128)(2,1)S(1)} %copy-done.9, bf16[8,2,18,1024]{3,1,2,0:T(2,128)(2,1)} %all-to-all-done.1), kind=kOutput, calls=%fused_computation.26 | convolution fusion | flops 452984832 | bytes 4620288 | tf_op jit(solution)/shard_map/sacd,adf->sacf/dot_general | solution.py:127
  131.1 3.1 %fusion.23 = f32[8,2,18,768]{3,2,0,1:T(8,128)} fusion(bf16[2,1024,768]{2,1,0:T(8,128)(2,1)S(1)} %copy-done, bf16[8,2,18,1024]{3,1,2,0:T(2,128)(2,1)} %all-to-all-done.1), kind=kOutput, calls=%fused_computation.27 | convolution fusion | flops 452984832 | bytes 4620288 | tf_op jit(solution)/shard_map/sacd,adf->sacf/dot_general | solution.py:130
  134.5 4.3 %fusion.17 = f32[8,2,18,768]{3,2,0,1:T(8,128)} fusion(bf16[2,768,1024]{2,1,0:T(8,128)(2,1)} %param.21, bf16[8,2,18,1024]{3,1,2,0:T(2,128)(2,1)} %all-to-all-done.3), kind=kOutput, calls=%fused_computation.25 | convolution fusion | flops 452984832 | bytes 4620288 | tf_op jit(solution)/shard_map/sacd,afd->sacf/dot_general | solution.py:131
  138.8 26.8 %all_gather.9 = bf16[1024,128]{0,1:T(8,128)(2,1)S(1)} all-gather(bf16[128,128]{0,1:T(8,128)(2,1)S(1)} %copy-done.12), channel_id=1, replica_groups=mesh['ctx'=4,'exp'=8] {'exp'}, dimensions={0}, use_global_device_ids=true | all-gather | bytes 294912 | tf_op jit(solution)/shard_map/all_gather | solution.py:52
  165.6 3.8 %multiply_reduce_fusion = (f32[128,16]{0,1:T(8,128)S(1)}, bf16[128,16,128]{2,0,1:T(8,128)(2,1)}) fusion(bf16[128,2048]{0,1:T(8,128)(2,1)} %copy.87, bf16[16,128,1024]{1,2,0:T(8,128)(2,1)} %exponential_convert_fusion, bf16[1024,128]{0,1:T(8,128)(2,1)S(1)} %all_gather.9), kind=kOutput, calls=%fused_computation.46 | convolution fusion | flops 538179584 | bytes 5513216 | tf_op jit(solution)/shard_map/hrk,kd->rhd/dot_general | solution.py:66
  173.6 4.1 %all-to-all-start = ((bf16[8,128,256]{1,2,0:T(8,128)(2,1)}), bf16[8,128,256]{1,2,0:T(8,128)(2,1)}, u32[]{:S(2)}, u32[]{:S(2)}) async-start(bf16[8,128,256]{1,2,0:T(8,128)(2,1)} %copy_bitcast_fusion), calls=%async_computation | async-start | bytes 1048576 | tf_op jit(solution)/shard_map/all_to_all | solution.py:90
  177.8 37.5 %all-reduce.3.cloned.1.call-done = (f32[8,2,18,768]{3,2,0,1:T(8,128)}, f32[8,2,18,768]{3,2,0,1:T(8,128)}, f32[8,2,18,768]{3,2,0,1:T(8,128)}) async-done(((f32[8,2,18,768]{3,2,0,1:T(8,128)}, f32[8,2,18,768]{3,2,0,1:T(8,128)}, f32[8,2,18,768]{3,2,0,1:T(8,128)}), (f32[8,2,18,768]{3,2,0,1:T(8,128)}, f32[8,2,18,768]{3,2,0,1:T(8,128)}, f32[8,2,18,768]{3,2,0,1:T(8,128)})) %all-reduce.3.cloned.1.call-update) | async-done | bytes 2654224 | tf_op jit(solution)/shard_map/psum | solution.py:134
  215.3 3.0 %fusion.3 = f32[2,8,18,1024]{3,2,1,0:T(8,128)S(1)} fusion(bf16[2,1024,768]{2,1,0:T(8,128)(2,1)S(1)} %copy-done, f32[8,2,18,768]{3,2,0,1:T(8,128)} %get-tuple-element.32, f32[8,2,18,768]{3,2,0,1:T(8,128)} %get-tuple-element.31), kind=kOutput, calls=%fused_computation.11 | convolution fusion | flops 454311936 | bytes 6094848 | tf_op jit(solution)/shard_map/sacf,adf->sacd/dot_general | solution.py:143
  221.6 5.5 %all-to-all-start.4 = ((bf16[8,2,18,1024]{3,1,2,0:T(2,128)(2,1)}), bf16[8,2,18,1024]{3,1,2,0:T(2,128)(2,1)}, u32[]{:S(2)}, u32[]{:S(2)}) async-start(bf16[8,2,18,1024]{3,1,2,0:T(2,128)(2,1)} %copy.107), calls=%async_computation.4 | async-start | bytes 1179648 | tf_op jit(solution)/shard_map/all_to_all | solution.py:147
  227.5 3.5 %fusion.33 = bf16[8,2,18,1024]{3,2,0,1:T(8,128)(2,1)S(1)} fusion(bf16[2,768,1024]{2,1,0:T(8,128)(2,1)} %param.21, f32[8,2,18,768]{3,2,0,1:T(8,128)} %get-tuple-element.30, f32[8,2,18,768]{3,2,0,1:T(8,128)} %get-tuple-element.31), kind=kOutput, calls=%fused_computation.33 | convolution fusion | flops 454606848 | bytes 5505024 | tf_op jit(solution)/shard_map/sacf,afd->sacd/dot_general | solution.py:138
  232.4 10.6 %all-to-all-done.4 = bf16[8,2,18,1024]{3,1,2,0:T(2,128)(2,1)} async-done(((bf16[8,2,18,1024]{3,1,2,0:T(2,128)(2,1)}), bf16[8,2,18,1024]{3,1,2,0:T(2,128)(2,1)}, u32[]{:S(2)}, u32[]{:S(2)}) %all-to-all-start.4) | async-done | bytes 589856 | tf_op jit(solution)/shard_map/all_to_all | solution.py:147
  243.0 4.2 %all-to-all-start.2 = ((bf16[8,2,18,1024]{3,1,2,0:T(2,128)(2,1)}), bf16[8,2,18,1024]{3,1,2,0:T(2,128)(2,1)}, u32[]{:S(2)}, u32[]{:S(2)}) async-start(bf16[8,2,18,1024]{3,1,2,0:T(2,128)(2,1)} %copy.103), calls=%async_computation.2 | async-start | bytes 1179648 | tf_op jit(solution)/shard_map/all_to_all | solution.py:146
  247.2 3.7 %fusion.32 = bf16[128,16,128]{2,0,1:T(8,128)(2,1)} fusion(bf16[16,128,1024]{1,2,0:T(8,128)(2,1)} %copy-done.5, bf16[1024,128]{1,0:T(8,128)(2,1)S(1)} %all_gather.10), kind=kOutput, calls=%fused_computation.31 | convolution fusion | flops 537395200 | bytes 4980736 | tf_op jit(solution)/shard_map/hrk,kd->rhd/dot_general | solution.py:77
  256.2 5.8 %all_gather.11 = bf16[128,1024]{0,1:T(8,128)(2,1)S(1)} all-gather(bf16[128,256]{0,1:T(8,128)(2,1)S(1)} %reduce_sum.51), channel_id=1, replica_groups=mesh['ctx'=4,'exp'=8] {'ctx'}, dimensions={1}, use_global_device_ids=true | all-gather | bytes 327680 | tf_op jit(solution)/shard_map/all_gather | solution.py:94
  265.7 2.1 reshape.406
  270.0 2.1 reshape.405
  272.1 2.3 convolution_convert_fusion.1
  274.4 2.6 convolution_convert_fusion.2
  (114 shorter events, 37.2 us)
Async XLA Ops:
  7.2 124.0 %copy-start = (bf16[2,1024,768]{2,1,0:T(8,128)(2,1)S(1)}, bf16[2,1024,768]{2,1,0:T(8,128)(2,1)}, u32[]{:S(2)}) copy-start(bf16[2,1024,768]{2,1,0:T(8,128)(2,1)} %param.20) | copy-start | bytes 9437188
  7.2 32.7 %copy-start.1 = (bf16[128,1024]{1,0:T(8,128)(2,1)S(1)}, bf16[128,1024]{1,0:T(8,128)(2,1)}, u32[]{:S(2)}) copy-start(bf16[128,1024]{1,0:T(8,128)(2,1)} %param.15) | copy-start | bytes 786436
  39.7 14.8 %copy-start.17 = (s32[16]{0:T(128)}, s32[16]{0:T(128)S(1)}, u32[]{:S(2)}) copy-start(s32[16]{0:T(128)S(1)} %convert_reduce_fusion) | copy-start | bytes 196
  42.5 12.8 %copy-start.19 = (f32[128,2]{0,1:T(2,128)S(1)}, f32[128,2]{0,1:T(2,128)}, u32[]{:S(2)}) copy-start(f32[128,2]{0,1:T(2,128)} %param.18) | copy-start | bytes 3076
  47.3 70.7 %all-to-all-start.1 = ((bf16[8,2,18,1024]{3,1,2,0:T(2,128)(2,1)}), bf16[8,2,18,1024]{3,1,2,0:T(2,128)(2,1)}, u32[]{:S(2)}, u32[]{:S(2)}) async-start(bf16[8,2,18,1024]{3,1,2,0:T(2,128)(2,1)} %copy.100), calls=%async_computation.1 | async-start | bytes 1179648 | tf_op jit(solution)/shard_map/all_to_all | solution.py:124
  55.6 3.2 %copy-start.2 = (bf16[128,1024]{1,0:T(8,128)(2,1)S(1)}, bf16[128,1024]{1,0:T(8,128)(2,1)}, u32[]{:S(2)}) copy-start(bf16[128,1024]{1,0:T(8,128)(2,1)} %param.16) | copy-start | bytes 786436
  58.0 3.3 %copy-start.13 = (f32[288]{0:T(512)}, f32[288]{0:T(512)S(1)}, u32[]{:S(2)}) copy-start(f32[288]{0:T(512)S(1)} %gather_fusion) | copy-start | bytes 3460
  97.9 2.4 copy-start.15
  97.9 2.4 copy-start.16
  100.2 3.4 %copy-start.3 = (f32[1024,128,16]{1,0,2:T(8,128)}, f32[1024,128,16]{1,0,2:T(8,128)S(1)}, u32[]{:S(2)}) copy-start(f32[1024,128,16]{1,0,2:T(8,128)S(1)} %get-tuple-element.40) | copy-start | bytes 25165828
  100.3 3.3 %copy-start.6 = (f32[8,2,18,1024]{3,2,1,0:T(8,128)S(1)}, f32[8,2,18,1024]{3,2,1,0:T(8,128)}, u32[]{:S(2)}) copy-start(f32[8,2,18,1024]{3,2,1,0:T(8,128)} %reshape.411) | copy-start | bytes 3538948
  117.9 16.5 %all-to-all-start.3 = ((bf16[8,2,18,1024]{3,1,2,0:T(2,128)(2,1)}), bf16[8,2,18,1024]{3,1,2,0:T(2,128)(2,1)}, u32[]{:S(2)}, u32[]{:S(2)}) async-start(bf16[8,2,18,1024]{3,1,2,0:T(2,128)(2,1)} %copy.105), calls=%async_computation.3 | async-start | bytes 1179648 | tf_op jit(solution)/shard_map/all_to_all | solution.py:125
  123.4 91.9 %all-reduce.3.cloned.1.call-start = ((), (), s32[]{:S(2)}) async-start(), calls=%async_computation.5 | async-start | bytes 7077888 | tf_op jit(solution)/shard_map/psum | solution.py:134
  123.4 4.6 %copy-start.9 = (bf16[2,1024,768]{2,1,0:T(8,128)(2,1)S(1)}, bf16[2,1024,768]{2,1,0:T(8,128)(2,1)}, u32[]{:S(2)}) copy-start(bf16[2,1024,768]{2,1,0:T(8,128)(2,1)} %param.19) | copy-start | bytes 9437188
  134.2 4.6 %copy-start.12 = (bf16[128,128]{0,1:T(8,128)(2,1)S(1)}, bf16[128,128]{0,1:T(8,128)(2,1)}, u32[]{:S(2)}) copy-start(bf16[128,128]{0,1:T(8,128)(2,1)} %copy.125) | copy-start | bytes 98308
  138.8 30.7 %copy-start.4 = (bf16[16,128,1024]{1,2,0:T(8,128)(2,1)S(1)}, bf16[16,128,1024]{1,2,0:T(8,128)(2,1)}, u32[]{:S(2)}) copy-start(bf16[16,128,1024]{1,2,0:T(8,128)(2,1)} %exponential_convert_fusion) | copy-start | bytes 12582916
  138.8 30.7 %copy-start.7 = (bf16[128,2048]{0,1:T(8,128)(2,1)S(1)}, bf16[128,2048]{0,1:T(8,128)(2,1)}, u32[]{:S(2)}) copy-start(bf16[128,2048]{0,1:T(8,128)(2,1)} %copy.87) | copy-start | bytes 1572868
  169.5 1.3 copy-start.8
  170.8 2.0 copy-start.5
  170.8 2.0 copy-start.11
  173.6 48.0 %all-to-all-start = ((bf16[8,128,256]{1,2,0:T(8,128)(2,1)}), bf16[8,128,256]{1,2,0:T(8,128)(2,1)}, u32[]{:S(2)}, u32[]{:S(2)}) async-start(bf16[8,128,256]{1,2,0:T(8,128)(2,1)} %copy_bitcast_fusion), calls=%async_computation | async-start | bytes 1048576 | tf_op jit(solution)/shard_map/all_to_all | solution.py:90
  215.3 3.0 %copy-start.10 = (bf16[2,1024,768]{2,1,0:T(8,128)(2,1)S(1)}, bf16[2,1024,768]{2,1,0:T(8,128)(2,1)}, u32[]{:S(2)}) copy-start(bf16[2,1024,768]{2,1,0:T(8,128)(2,1)} %param.19) | copy-start | bytes 9437188
  215.3 3.0 %copy-start.20 = (f32[8,2,18,768]{3,2,0,1:T(8,128)S(1)}, f32[8,2,18,768]{3,2,0,1:T(8,128)}, u32[]{:S(2)}) copy-start(f32[8,2,18,768]{3,2,0,1:T(8,128)} %get-tuple-element.30) | copy-start | bytes 2654212
  215.3 3.3 %copy-start.21 = (f32[8,2,18,768]{3,2,0,1:T(8,128)S(1)}, f32[8,2,18,768]{3,2,0,1:T(8,128)}, u32[]{:S(2)}) copy-start(f32[8,2,18,768]{3,2,0,1:T(8,128)} %get-tuple-element.31) | copy-start | bytes 2654212
  215.3 3.6 %copy-start.22 = (f32[8,2,18,768]{3,2,0,1:T(8,128)S(1)}, f32[8,2,18,768]{3,2,0,1:T(8,128)}, u32[]{:S(2)}) copy-start(f32[8,2,18,768]{3,2,0,1:T(8,128)} %get-tuple-element.32) | copy-start | bytes 2654212
  218.9 8.3 %copy-start.18 = (s32[16]{0:T(128)S(1)}, s32[16]{0:T(128)}, u32[]{:S(2)}) copy-start(s32[16]{0:T(128)} %copy-done.17) | copy-start | bytes 196
  221.6 21.4 %all-to-all-start.4 = ((bf16[8,2,18,1024]{3,1,2,0:T(2,128)(2,1)}), bf16[8,2,18,1024]{3,1,2,0:T(2,128)(2,1)}, u32[]{:S(2)}, u32[]{:S(2)}) async-start(bf16[8,2,18,1024]{3,1,2,0:T(2,128)(2,1)} %copy.107), calls=%async_computation.4 | async-start | bytes 1179648 | tf_op jit(solution)/shard_map/all_to_all | solution.py:147
  243.0 24.8 %all-to-all-start.2 = ((bf16[8,2,18,1024]{3,1,2,0:T(2,128)(2,1)}), bf16[8,2,18,1024]{3,1,2,0:T(2,128)(2,1)}, u32[]{:S(2)}, u32[]{:S(2)}) async-start(bf16[8,2,18,1024]{3,1,2,0:T(2,128)(2,1)} %copy.103), calls=%async_computation.2 | async-start | bytes 1179648 | tf_op jit(solution)/shard_map/all_to_all | solution.py:146
  247.2 7.8 %copy-start.14 = (f32[288]{0:T(512)S(1)}, f32[288]{0:T(512)}, u32[]{:S(2)}) copy-start(f32[288]{0:T(512)} %copy-done.13) | copy-start | bytes 3460
Sparse Core Ops, SparseCore 0:
  138.9 76.3 all-reduce.2
where the time goes:
time: 285 us; the launch traced here: 284 us
  blocking collectives  63.9 us (22%)
  waiting for transfers between devices  48.4 us (17%)
  local copies, waits for them, and re-layouts  46.2 us (16%)
  other arithmetic  44.1 us (15%)
  matrix products  40.2 us (14%)
  starting transfers between devices  26.6 us (9%)
  between operations  14.4 us (5%)
    psum x1, waiting for transfers between devices, body(): gate_full, up_full = lax.psum((gate_part, up_part), 'ctx')  37.5 us
    all_gather x1, blocking collectives, body(): lax.all_gather(key_pick, 'exp', axis=0, tiled=True)  31.3 us
    unnamed x4, other arithmetic  29.9 us
    all_gather x1, blocking collectives, body(): lax.all_gather(value_pick, 'exp', axis=0, tiled=True)  26.8 us
    unnamed x56, local copies, waits for them, and re-layouts  11.8 us
    all_to_all x1, waiting for transfers between devices, body(): lax.all_to_all(route_in, 'exp', split_axis=0, concat_axis=0, tiled=True)  10.6 us
    all_to_all x1, starting transfers between devices, body(): lax.all_to_all(send_rows, 'exp', split_axis=0, concat_axis=0, tiled=True)  7.24 us
    convert_element_type x1, other arithmetic, body(): attn_probs = jnp.exp(scores - log_total).astype(jnp.bfloat16)  7.16 us
  transfers between devices with their start and end apart: 6, of which 3 were waited for; matrix products, arithmetic and copies ran while one was open for 27% of the time, Pallas kernels for 0%

commit v1 on v0

v1 whole, which is shorter than its diff:
```python
import functools
import math

import jax
import jax.numpy as jnp
from jax import lax
from jax.experimental import pallas as pl
from jax.experimental.pallas import tpu as pltpu
from jax.sharding import PartitionSpec as P

HEAD_SIZE = 128
LANES = 128
ROW_TILE = 16
VMEM_BYTES = 48 * 1024 * 1024
BF16 = jnp.bfloat16
F32 = jnp.float32


def dot(a, b, a_dim=1, b_dim=0):
    return lax.dot_general(a, b, (((a_dim,), (b_dim,)), ((), ())), preferred_element_type=F32)


def iota(shape, dim):
    return lax.broadcasted_iota(jnp.int32, shape, dim)


def params(steps=1):
    return pltpu.CompilerParams(
        vmem_limit_bytes=VMEM_BYTES, dimension_semantics=("arbitrary",) * steps
    )


def cost(flops, bytes_accessed, transcendentals=0):
    return pl.CostEstimate(
        flops=int(flops), bytes_accessed=int(bytes_accessed), transcendentals=int(transcendentals)
    )


def power_of_two(value):
    return value > 0 and value & (value - 1) == 0


class Slots:
    def __init__(self, slot_count, width, exp_count, local_experts):
        whole = slot_count // ROW_TILE * ROW_TILE
        rem = slot_count - whole
        blocks = width // LANES
        self.fold = (
            whole > 0
            and rem > 0
            and power_of_two(rem)
            and power_of_two(exp_count)
            and rem * blocks <= whole
            and (rem * exp_count) % ROW_TILE == 0
        )
        self.rows = whole if self.fold or rem == 0 else whole + ROW_TILE
        self.rem = rem if self.fold else 0
        self.blocks = blocks
        self.width = width
        self.columns = width + (LANES if self.fold else 0)
        self.exp_count = exp_count
        self.local = local_experts
        self.experts = exp_count * local_experts
        self.total = self.experts * self.rows
        self.per_expert = exp_count * (self.rows + self.rem)


def route_places(ids, slots):
    tokens, top = ids.shape
    lanes = -(-slots.experts // LANES) * LANES
    expert = iota((tokens, lanes), 1)
    hits = [(ids[:, r : r + 1] == expert).astype(F32) for r in range(top)]
    earlier = (iota((tokens, tokens), 0) > iota((tokens, tokens), 1)).astype(BF16)
    before = dot(earlier, sum(hits).astype(BF16))
    found = []
    for r in range(top):
        rank = jnp.sum(hits[r] * before, axis=1, keepdims=True)
        base = ids[:, r : r + 1].astype(F32) * slots.rows
        inside = rank < slots.rows
        main = jnp.where(inside, base + rank, -1.0)
        folded = jnp.where(inside, -65536.0, base + rank - slots.rows)
        found.append((main, folded))
    return found


def as_row(column):
    tokens = column.shape[0]
    return jnp.transpose(jnp.broadcast_to(column, (tokens, LANES)))[0:1, :]


def dispatch_kernel(slots, weighted, ids_ref, gain_ref, rows_ref, out_ref):
    tokens, top = ids_ref.shape
    places = route_places(ids_ref[...], slots)
    mains = [as_row(main) for main, _ in places]
    folds = [as_row(folded) for _, folded in places]
    gains = [as_row(gain_ref[:, r : r + 1]) for r in range(top)]
    slot = iota((slots.total, tokens), 0).astype(F32)
    rows = rows_ref[...]

    def picks(wanted):
        pick = jnp.zeros((slots.total, tokens), F32)
        gain = pick
        for r in range(top):
            here = slot == wanted[r]
            pick = jnp.where(here, 1.0, pick)
            gain = jnp.where(here, gains[r], gain)
        return pick.astype(BF16), gain

    pick, gain = picks(mains)
    taken = dot(pick, rows)
    if weighted:
        taken = taken * jnp.sum(gain, axis=1, keepdims=True)
    out_ref[:, : slots.width] = taken.astype(BF16)
    if slots.fold:
        taken = jnp.zeros((slots.total, LANES), F32)
        total_gain = jnp.zeros((slots.total, tokens), F32)
        for f in range(slots.blocks):
            pick, gain = picks([fold + float(f * slots.rem) for fold in folds])
            taken = taken + dot(pick, rows[:, f * LANES : (f + 1) * LANES])
            total_gain = total_gain + gain
        if weighted:
            taken = taken * jnp.sum(total_gain, axis=1, keepdims=True)
        out_ref[:, slots.width :] = taken.astype(BF16)


def dispatch(slots, weighted, ids, gains, rows):
    return pl.pallas_call(
        functools.partial(dispatch_kernel, slots, weighted),
        out_shape=jax.ShapeDtypeStruct((slots.total, slots.columns), BF16),
        compiler_params=pltpu.CompilerParams(vmem_limit_bytes=VMEM_BYTES),
        cost_estimate=cost(4 * slots.total * LANES * slots.width, 4 * slots.total * slots.columns),
        name="dispatch_scaled" if weighted else "dispatch_rows",
    )(ids, gains, rows)


def combine_kernel(slots, weighted, ids_ref, gain_ref, back_ref, out_ref):
    tokens, top = ids_ref.shape
    places = route_places(ids_ref[...], slots)
    slot = iota((tokens, slots.total), 1).astype(F32)

    def table(wanted):
        found = jnp.zeros((tokens, slots.total), F32)
        for r in range(top):
            value = gain_ref[:, r : r + 1] if weighted else 1.0
            found = jnp.where(slot == wanted[r], value, found)
        return found

    def apply(found, rows):
        high = found.astype(BF16)
        result = dot(high, rows)
        if weighted:
            result = result + dot((found - high.astype(F32)).astype(BF16), rows)
        return result

    result = apply(table([main for main, _ in places]), back_ref[:, : slots.width])
    if slots.fold:
        folded = back_ref[:, slots.width :]
        extra = [
            apply(table([start + float(f * slots.rem) for _, start in places]), folded)
            for f in range(slots.blocks)
        ]
        result = result + jnp.concatenate(extra, axis=1)
    out_ref[...] = result.astype(BF16)


def combine(slots, weighted, ids, gains, back):
    tokens = ids.shape[0]
    return pl.pallas_call(
        functools.partial(combine_kernel, slots, weighted),
        out_shape=jax.ShapeDtypeStruct((tokens, slots.width), BF16),
        compiler_params=pltpu.CompilerParams(vmem_limit_bytes=VMEM_BYTES),
        cost_estimate=cost(8 * slots.total * LANES * slots.width, 4 * slots.total * slots.columns),
        name="combine_out" if weighted else "combine_in",
    )(ids, gains, back)


def fold_table(slots, shape, folded_dim):
    folded = iota(shape, folded_dim)
    plain = iota(shape, 1 - folded_dim)
    rem_bits = int(math.log2(slots.rem))
    exp_bits = int(math.log2(slots.exp_count))
    j = plain & (slots.rem - 1)
    source = (plain >> rem_bits) & (slots.exp_count - 1)
    f = plain >> (rem_bits + exp_bits)
    return (folded == source * slots.rows + f * slots.rem + j).astype(F32).astype(BF16)


def unpack_rows(slots, block):
    flat = block.reshape(slots.exp_count * slots.rows, slots.columns)
    if not slots.fold:
        return flat
    each = slots.exp_count * slots.rem
    plain = dot(
        fold_table(slots, (slots.blocks * each, slots.exp_count * slots.rows), 1),
        flat[:, slots.width :],
    ).astype(BF16)
    extra = jnp.concatenate(
        [plain[f * each : (f + 1) * each] for f in range(slots.blocks)], axis=1
    )
    return jnp.concatenate([flat[:, : slots.width], extra], axis=0)


def pack_rows(slots, rows, out_ref):
    count = slots.exp_count * slots.rows
    main = rows[:count].reshape(slots.exp_count, 1, slots.rows, slots.width)
    out_ref[:, :, :, : slots.width] = main
    if slots.fold:
        each = slots.exp_count * slots.rem
        stacked = jnp.concatenate(
            [rows[count:, f * LANES : (f + 1) * LANES] for f in range(slots.blocks)], axis=0
        )
        folded = dot(fold_table(slots, (count, slots.blocks * each), 0), stacked).astype(BF16)
        out_ref[:, :, :, slots.width :] = folded.reshape(
            slots.exp_count, 1, slots.rows, LANES
        )


def ff_tile(width):
    return 256 if width % 256 == 0 else width


def gate_up_kernel(slots, pick_ref, recv_ref, gate_ref, up_ref, out_ref, rows_ref):
    @pl.when(pl.program_id(0) == 0)
    def _():
        rows_ref[...] = unpack_rows(slots, recv_ref[...])

    rows = rows_ref[...]
    out_ref[0] = dot(rows, gate_ref[0]).astype(out_ref.dtype)
    out_ref[1] = dot(rows, up_ref[0]).astype(out_ref.dtype)


def gate_up(slots, expert, recv, gate_proj, up_proj, dtype):
    local, width, ff = gate_proj.shape
    tile = ff_tile(ff)
    weights = pl.BlockSpec((1, width, tile), lambda i, e: (e[0], 0, i))
    return pl.pallas_call(
        functools.partial(gate_up_kernel, slots),
        grid_spec=pltpu.PrefetchScalarGridSpec(
            num_scalar_prefetch=1,
            grid=(ff // tile,),
            in_specs=[
                pl.BlockSpec(
                    (slots.exp_count, 1, slots.rows, slots.columns), lambda i, e: (0, e[0], 0, 0)
                ),
                weights,
                weights,
            ],
            out_specs=pl.BlockSpec((2, slots.per_expert, tile), lambda i, e: (0, 0, i)),
            scratch_shapes=[pltpu.VMEM((slots.per_expert, width), BF16)],
        ),
        out_shape=jax.ShapeDtypeStruct((2, slots.per_expert, ff), dtype),
        compiler_params=params(),
        cost_estimate=cost(4 * slots.per_expert * width * ff, 4 * width * ff),
        name="gate_up",
    )(expert, recv, gate_proj, up_proj)


def hidden_grad_kernel(slots, pick_ref, recv_ref, down_ref, out_ref, rows_ref):
    @pl.when(pl.program_id(0) == 0)
    def _():
        rows_ref[...] = unpack_rows(slots, recv_ref[...])

    out_ref[...] = dot(rows_ref[...], down_ref[0], 1, 1).astype(out_ref.dtype)


def hidden_grad_part(slots, expert, recv, down_proj, dtype):
    local, ff, width = down_proj.shape
    tile = ff_tile(ff)
    return pl.pallas_call(
        functools.partial(hidden_grad_kernel, slots),
        grid_spec=pltpu.PrefetchScalarGridSpec(
            num_scalar_prefetch=1,
            grid=(ff // tile,),
            in_specs=[
                pl.BlockSpec(
                    (slots.exp_count, 1, slots.rows, slots.columns), lambda i, e: (0, e[0], 0, 0)
                ),
                pl.BlockSpec((1, tile, width), lambda i, e: (e[0], i, 0)),
            ],
            out_specs=pl.BlockSpec((slots.per_expert, tile), lambda i, e: (0, i)),
            scratch_shapes=[pltpu.VMEM((slots.per_expert, width), BF16)],
        ),
        out_shape=jax.ShapeDtypeStruct((slots.per_expert, ff), dtype),
        compiler_params=params(),
        cost_estimate=cost(2 * slots.per_expert * width * ff, 2 * width * ff),
        name="hidden_grad",
    )(expert, recv, down_proj)


def route_out_kernel(slots, pick_ref, mine_ref, other_ref, down_ref, out_ref):
    hidden = jnp.where(pl.program_id(0) == 0, mine_ref[...], other_ref[...])
    pack_rows(slots, dot(hidden, down_ref[0]).astype(BF16), out_ref)


def route_out(slots, order, mine, other, down_proj):
    local, ff, width = down_proj.shape
    whole = pl.BlockSpec(mine.shape, lambda i, e: (0, 0))
    return pl.pallas_call(
        functools.partial(route_out_kernel, slots),
        grid_spec=pltpu.PrefetchScalarGridSpec(
            num_scalar_prefetch=1,
            grid=(local,),
            in_specs=[whole, whole, pl.BlockSpec((1, ff, width), lambda i, e: (e[i], 0, 0))],
            out_specs=pl.BlockSpec(
                (slots.exp_count, 1, slots.rows, slots.columns), lambda i, e: (0, e[i], 0, 0)
            ),
        ),
        out_shape=jax.ShapeDtypeStruct((slots.exp_count, local, slots.rows, slots.columns), BF16),
        compiler_params=params(),
        cost_estimate=cost(4 * slots.per_expert * width * ff, 4 * width * ff),
        name="route_out",
    )(order, mine, other, down_proj)


def route_in_kernel(slots, pick_ref, mine_ref, other_ref, gate_ref, up_ref, out_ref):
    first = pl.program_id(0) == 0
    gate_back = jnp.where(first, mine_ref[0], other_ref[0])
    up_back = jnp.where(first, mine_ref[1], other_ref[1])
    total = dot(gate_back, gate_ref[0], 1, 1) + dot(up_back, up_ref[0], 1, 1)
    pack_rows(slots, total.astype(BF16), out_ref)


def route_in(slots, order, mine, other, gate_proj, up_proj):
    local, width, ff = gate_proj.shape
    whole = pl.BlockSpec(mine.shape, lambda i, e: (0, 0, 0))
    weights = pl.BlockSpec((1, width, ff), lambda i, e: (e[i], 0, 0))
    return pl.pallas_call(
        functools.partial(route_in_kernel, slots),
        grid_spec=pltpu.PrefetchScalarGridSpec(
            num_scalar_prefetch=1,
            grid=(local,),
            in_specs=[whole, whole, weights, weights],
            out_specs=pl.BlockSpec(
                (slots.exp_count, 1, slots.rows, slots.columns), lambda i, e: (0, e[i], 0, 0)
            ),
        ),
        out_shape=jax.ShapeDtypeStruct((slots.exp_count, local, slots.rows, slots.columns), BF16),
        compiler_params=params(),
        cost_estimate=cost(8 * slots.per_expert * width * ff, 8 * width * ff),
        name="route_in",
    )(order, mine, other, gate_proj, up_proj)


def attention_kernel(
    offsets, tokens, chunk, me_ref, q_ref, g_ref, kv_ref, kv_far_ref,
    out_ref, qgrad_ref, keep_ref, send_ref,
    probs_ref, low_ref, key_t, value_t, key_acc, value_acc,
):
    d = HEAD_SIZE
    step = pl.program_id(0)
    me = me_ref[0]
    half = kv_ref.shape[0]
    seq = 2 * half
    scale = d ** (-0.5)
    to_base2 = scale * math.log2(math.e)

    @pl.when(step == 0)
    def _():
        for start, ref in ((0, kv_ref), (half, kv_far_ref)):
            for at in range(0, half, tokens):
                both = jnp.transpose(ref[at : at + tokens, :].astype(F32)).astype(BF16)
                key_t[:, start + at : start + at + tokens] = both[:d]
                value_t[:, start + at : start + at + tokens] = both[d:]
        key_acc[...] = jnp.zeros_like(key_acc)
        value_acc[...] = jnp.zeros_like(value_acc)

    def piece(at, first):
        ref, start = (kv_ref, at) if at < half else (kv_far_ref, at - half)
        return ref[start : start + chunk, first : first + d]

    heads = q_ref.shape[1] // d
    lanes = heads * tokens
    q = jnp.concatenate([q_ref[:, h * d : (h + 1) * d] for h in range(heads)], axis=0)
    g = jnp.concatenate([g_ref[:, h * d : (h + 1) * d] for h in range(heads)], axis=0)
    q_t = jnp.transpose(q.astype(F32)).astype(BF16)
    g_t32 = jnp.transpose(g.astype(F32))
    g_t = g_t32.astype(BF16)
    query_token = iota((tokens, lanes), 1) & (tokens - 1)
    key_token = iota((tokens, lanes), 0)
    ahead = key_token - query_token

    top = jnp.full((1, lanes), -jnp.inf, F32)
    for at in range(0, seq, chunk):
        scores = dot(piece(at, 0), q_t)
        for part in range(0, chunk, tokens):
            block = me ^ offsets[(at + part) // tokens]
            allowed = ahead <= (me - block) * tokens
            some = jnp.where(allowed, scores[part : part + tokens], -jnp.inf)
            probs_ref[at + part : at + part + tokens, :] = some
            top = jnp.maximum(top, jnp.max(some, axis=0, keepdims=True))
    top = top * to_base2
    total = jnp.zeros((1, lanes), F32)
    for at in range(0, seq, chunk):
        raised = jnp.exp2(probs_ref[at : at + chunk, :] * to_base2 - top)
        probs_ref[at : at + chunk, :] = raised
        total = total + jnp.sum(raised, axis=0, keepdims=True)
    inverse = 1.0 / total
    attended = jnp.zeros((d, lanes), F32)
    for at in range(0, seq, chunk):
        low = (probs_ref[at : at + chunk, :] * inverse).astype(BF16)
        low_ref[at : at + chunk, :] = low
        attended = attended + dot(value_t[:, at : at + chunk], low)
        value_acc[at : at + chunk, :] += dot(low, g)
    attended = attended.astype(BF16).astype(F32)
    row_dot = jnp.sum(g_t32 * attended, axis=0, keepdims=True)
    query_back = jnp.zeros((d, lanes), F32)
    for at in range(0, seq, chunk):
        prob_grad = dot(piece(at, d), g_t)
        score_grad = (low_ref[at : at + chunk, :].astype(F32) * (prob_grad - row_dot)).astype(BF16)
        query_back = query_back + dot(key_t[:, at : at + chunk], score_grad)
        key_acc[at : at + chunk, :] += dot(score_grad, q)
    for h in range(heads):
        rows = slice(h * tokens, (h + 1) * tokens)
        out_ref[:, h * d : (h + 1) * d] = jnp.transpose(attended[:, rows]).astype(BF16)
        qgrad_ref[:, h * d : (h + 1) * d] = jnp.transpose(query_back[:, rows] * scale).astype(BF16)

    @pl.when(step == pl.num_programs(0) - 1)
    def _():
        keep_ref[:, :d] = key_acc[:half, :] * scale
        keep_ref[:, d:] = value_acc[:half, :]
        send_ref[:, :d] = (key_acc[half:, :] * scale).astype(BF16)
        send_ref[:, d:] = value_acc[half:, :].astype(BF16)


def attention(me, offsets, queries, attn_grad, kv_near, kv_far):
    tokens, columns = queries.shape
    half, both = kv_near.shape
    seq = 2 * half
    heads = columns // HEAD_SIZE
    group = 2 if heads % 2 == 0 else 1
    lanes = group * tokens
    chunk = min(256, half)
    tile = pl.BlockSpec((tokens, group * HEAD_SIZE), lambda i, m: (0, i))
    whole = pl.BlockSpec((half, both), lambda i, m: (0, 0))
    return pl.pallas_call(
        functools.partial(attention_kernel, offsets, tokens, chunk),
        grid_spec=pltpu.PrefetchScalarGridSpec(
            num_scalar_prefetch=1,
            grid=(heads // group,),
            in_specs=[tile, tile, whole, whole],
            out_specs=[tile, tile, whole, whole],
            scratch_shapes=[
                pltpu.VMEM((seq, lanes), F32),
                pltpu.VMEM((seq, lanes), BF16),
                pltpu.VMEM((HEAD_SIZE, seq), BF16),
                pltpu.VMEM((HEAD_SIZE, seq), BF16),
                pltpu.VMEM((seq, HEAD_SIZE), F32),
                pltpu.VMEM((seq, HEAD_SIZE), F32),
            ],
        ),
        out_shape=[
            jax.ShapeDtypeStruct(queries.shape, BF16),
            jax.ShapeDtypeStruct(queries.shape, BF16),
            jax.ShapeDtypeStruct((half, both), F32),
            jax.ShapeDtypeStruct((half, both), BF16),
        ],
        compiler_params=params(),
        cost_estimate=cost(12 * tokens * columns * seq, 8 * tokens * columns, tokens * heads * seq),
        name="attention",
    )(me, queries, attn_grad, kv_near, kv_far)


def swap(value, axis, bit):
    count = lax.axis_size(axis)
    return lax.ppermute(value, axis, [(i, i ^ bit) for i in range(count)])


def far_bits(count):
    bits = []
    bit = count // 2
    while bit >= 1:
        bits.append(bit)
        bit //= 2
    return bits


def spread_sum(part, ctx_count):
    bit = 2
    while bit < ctx_count:
        part = part + swap(part.astype(BF16), "ctx", bit).astype(F32)
        bit *= 2
    return part


def activate(gate, up):
    return (jax.nn.silu(gate) * up).astype(BF16)


def gate_backward(hidden_grad, gate, up):
    s = jax.nn.sigmoid(gate)
    gate_back = (hidden_grad * up * s * (1.0 + gate * (1.0 - s))).astype(BF16)
    up_back = (hidden_grad * (gate * s)).astype(BF16)
    return jnp.stack([gate_back, up_back])


def body(
    queries, key_proj, value_matrix_rows, attn_grad, moe_input, moe_grad,
    expert_ids, route_weights, gate_proj, up_proj, down_proj,
):
    ctx_count = lax.axis_size("ctx")
    exp_count = lax.axis_size("exp")
    ctx_index = lax.axis_index("ctx")
    exp_index = lax.axis_index("exp")
    tokens = queries.shape[0]
    d = HEAD_SIZE
    kv_heads = key_proj.shape[1] // d
    sharers = ctx_count // kv_heads
    kv_head = ctx_index // sharers
    width = moe_input.shape[1]
    local = gate_proj.shape[0]
    expert_total = local * exp_count
    slot_count = 2 * ((tokens + expert_total - 2) // (expert_total - 1))
    slots = Slots(slot_count, width, exp_count, local)
    core = ctx_index % 2
    mine = core.astype(jnp.int32).reshape(1)
    other = 1 - mine
    order = jnp.concatenate([mine, other])
    shape = (exp_count, local, slots.rows, slots.columns)

    def exchange(rows):
        flat = rows.reshape(exp_count, local * slots.rows, slots.columns)
        return lax.all_to_all(flat, "exp", split_axis=0, concat_axis=0, tiled=True)

    kv = jnp.concatenate(
        [
            lax.dynamic_slice_in_dim(key_proj, kv_head * d, d, 1),
            lax.dynamic_slice_in_dim(value_matrix_rows, kv_head * d, d, 1),
        ],
        axis=1,
    )
    offsets = [0]
    kv_far = None
    for bit in far_bits(exp_count):
        if kv_far is not None:
            kv = jnp.concatenate([kv, kv_far], axis=0)
        kv_far = swap(kv, "exp", bit)
        offsets = offsets + [o ^ bit for o in offsets]

    send_rows = dispatch(slots, False, expert_ids, route_weights, moe_input)
    recv_rows = exchange(send_rows).reshape(shape)
    send_scaled = dispatch(slots, True, expert_ids, route_weights, moe_grad)
    recv_scaled = exchange(send_scaled).reshape(shape)

    attn_out, query_grad, kv_keep, kv_send = attention(
        exp_index.astype(jnp.int32).reshape(1), tuple(offsets), queries, attn_grad, kv, kv_far
    )

    gu_send = gate_up(slots, other, recv_rows, gate_proj, up_proj, BF16)
    gu_recv = swap(gu_send, "ctx", 1)
    gu_keep = gate_up(slots, mine, recv_rows, gate_proj, up_proj, F32)
    gate_full, up_full = spread_sum(gu_keep + gu_recv.astype(F32), ctx_count)
    hidden = activate(gate_full, up_full)
    hidden_other = swap(hidden, "ctx", 1)
    out_rows = route_out(slots, order, hidden, hidden_other, down_proj)
    back_out = exchange(out_rows).reshape(slots.total, slots.columns)

    hg_send = hidden_grad_part(slots, other, recv_scaled, down_proj, BF16)
    hg_recv = swap(hg_send, "ctx", 1)
    hg_keep = hidden_grad_part(slots, mine, recv_scaled, down_proj, F32)
    hg_full = spread_sum(hg_keep + hg_recv.astype(F32), ctx_count)
    back = gate_backward(hg_full, gate_full, up_full)
    back_other = swap(back, "ctx", 1)
    in_rows = route_in(slots, order, back, back_other, gate_proj, up_proj)
    back_in = exchange(in_rows).reshape(slots.total, slots.columns)

    moe_out = combine(slots, True, expert_ids, route_weights, back_out)
    input_grad = combine(slots, False, expert_ids, route_weights, back_in)

    kv_sum = kv_keep
    for bit in reversed(far_bits(exp_count)):
        kv_sum = kv_sum + swap(kv_send, "exp", bit).astype(F32)
        half = kv_sum.shape[0] // 2
        if bit != exp_count // 2:
            kv_send = kv_sum[half:].astype(BF16)
            kv_sum = kv_sum[:half]
    kv_every = lax.all_gather(kv_sum.astype(BF16), "ctx", axis=0, tiled=False)
    if sharers > 1:
        kv_every = kv_every.astype(F32).reshape(kv_heads, sharers, tokens, 2 * d).sum(axis=1)
    kv_every = kv_every.astype(BF16)
    key_grad = jnp.concatenate([kv_every[h, :, :d] for h in range(kv_heads)], axis=1)
    value_grad = jnp.concatenate([kv_every[h, :, d:] for h in range(kv_heads)], axis=1)
    return (attn_out, query_grad, key_grad, value_grad, moe_out, input_grad)


def solution(mesh):
    placed = (
        P("exp", "ctx"),
        P("exp", None),
        P("exp", None),
        P("exp", "ctx"),
        P("exp", "ctx"),
        P("exp", "ctx"),
        P("exp", None),
        P("exp", None),
        P("exp", "ctx", None),
        P("exp", "ctx", None),
        P("exp", None, "ctx"),
    )
    return jax.shard_map(
        body,
        mesh=mesh,
        in_specs=placed,
        out_specs=(
            P("exp", "ctx"),
            P("exp", "ctx"),
            P("exp", None),
            P("exp", None),
            P("exp", "ctx"),
            P("exp", "ctx"),
        ),
        check_vma=False,
    )
```

time: 285 us -> 152 us (0.53)
  blocking collectives: 63.9 us -> 5.79 us
  Pallas kernels: 0 us -> 42.2 us
  matrix products: 40.2 us -> 0 us
  other arithmetic: 44.1 us -> 5.78 us
  local copies, waits for them, and re-layouts: 46.2 us -> 10.2 us
  between operations: 14.4 us -> 0.94 us
  waiting for transfers between devices: 48.4 us -> 54 us
  starting transfers between devices: 26.6 us -> 31.9 us
    all_gather x3 -> x1, blocking collectives: 63.9 us -> 5.79 us  [body(): kv_every = lax.all_gather(kv_sum.astype(BF16), 'ctx', axis=0, tiled=False)]
    pallas_call x0 -> x11, Pallas kernels: none -> 42.2 us  [the longest x1 16.8 us: attention(): pl.pallas_call(functools.partial(attention_kernel, offsets, tokens, chunk...]
    dot_general x14 -> x0, matrix products: 40.2 us -> none  [the longest x1 4.63 us: body(): jnp.einsum('hrk,rhd->kd', attn_probs, cotan_heads, preferred_element_type...]
    psum x1 -> x0, waiting for transfers between devices: 37.5 us -> none  [body(): gate_full, up_full = lax.psum((gate_part, up_part), 'ctx')]
    ppermute x0 -> x12, waiting for transfers between devices: none -> 33.7 us  [swap(): return lax.ppermute(value, axis, [(i, i ^ bit) for i in range(count)])]
    unnamed x4 -> x0, other arithmetic: 29.9 us -> none
    ppermute x0 -> x12, starting transfers between devices: none -> 12.4 us  [swap(): return lax.ppermute(value, axis, [(i, i ^ bit) for i in range(count)])]
    reshape x6 -> x0, local copies, waits for them, and re-layouts: 11.2 us -> none  [the longest x2 4.74 us: body(): moe_input[slot_token]]
  transfers between devices with their start and end apart: 6 -> 16, of which waited for: 3 -> 7; matrix products, arithmetic and copies ran while one was open for 27% -> 4% of each run, Pallas kernels for 0% -> 26%
where the time goes in v1:
time: 152 us; the launch traced here: 151 us
  waiting for transfers between devices  54 us (36%)
  Pallas kernels  42.2 us (28%)
  starting transfers between devices  31.9 us (21%)
  local copies, waits for them, and re-layouts  10.2 us (7%)
  blocking collectives  5.79 us (4%)
  other arithmetic  5.78 us (4%)
    ppermute x12, waiting for transfers between devices, swap(): return lax.ppermute(value, axis, [(i, i ^ bit) for i in range(count)])  33.7 us
    all_to_all x4, waiting for transfers between devices, exchange(): return lax.all_to_all(flat, 'exp', split_axis=0, concat_axis=0, tiled=True)  20.3 us
    all_to_all x4, starting transfers between devices, exchange(): return lax.all_to_all(flat, 'exp', split_axis=0, concat_axis=0, tiled=True)  19.5 us
    pallas_call x1, Pallas kernels, attention(): pl.pallas_call(functools.partial(attention_kernel, offsets, tokens, chunk...  16.8 us
    ppermute x12, starting transfers between devices, swap(): return lax.ppermute(value, axis, [(i, i ^ bit) for i in range(count)])  12.4 us
    unnamed x40, local copies, waits for them, and re-layouts  9.37 us
    pallas_call x2, Pallas kernels, gate_up(): pl.pallas_call(functools.partial(gate_up_kernel, slots), grid_spec=pltpu....  6.9 us
    all_gather x1, blocking collectives, body(): kv_every = lax.all_gather(kv_sum.astype(BF16), 'ctx', axis=0, tiled=False)  5.79 us
  transfers between devices with their start and end apart: 16, of which 7 were waited for; matrix products, arithmetic and copies ran while one was open for 4% of the time, Pallas kernels for 26%

profile of v1, /device:TPU:0, one launch (start us, length us, event | category | flops | bytes accessed | tf_op | source)
XLA Modules:
  0.0 150.9 jit_solution(198357636289217291)
XLA Ops:
  3.2 1.8 %dispatch_rows.1 = bf16[256,1152]{1,0:T(8,128)(2,1)} custom-call(s32[128,2]{1,0:T(8,128)S(1)} %copy.19.ids_ref, f32[128,2]{1,0:T(8,128)S(1)} %copy.20.gain_ref, bf16[128,1024]{1,0:T(8,128)(2,1)S(1)} %copy-done.8), custom_call_target="tpu_custom_call" | custom-call | flops 134217728 | bytes 1179648 | tf_op jit(solution)/shard_map/dispatch_rows/pallas_call | solution.py:127
  5.0 7.3 %all-to-all-start = ((bf16[8,32,1152]{2,1,0:T(8,128)(2,1)}), bf16[8,32,1152]{2,1,0:T(8,128)(2,1)S(1)}, u32[]{:S(2)}, u32[]{:S(2)}) async-start(bf16[8,32,1152]{2,1,0:T(8,128)(2,1)} %bitcast.11), calls=%async_computation | async-start | bytes 1179648 | tf_op jit(solution)/shard_map/all_to_all | solution.py:522
  13.2 1.9 %dispatch_scaled.1 = bf16[256,1152]{1,0:T(8,128)(2,1)} custom-call(s32[128,2]{1,0:T(8,128)S(1)} %copy.19.ids_ref, f32[128,2]{1,0:T(8,128)S(1)} %copy.20.gain_ref, bf16[128,1024]{1,0:T(8,128)(2,1)S(1)} %copy-done.9), custom_call_target="tpu_custom_call" | custom-call | flops 134217728 | bytes 1179648 | tf_op jit(solution)/shard_map/dispatch_scaled/pallas_call | solution.py:127
  15.1 13.0 %all-to-all-done = bf16[8,32,1152]{2,1,0:T(8,128)(2,1)S(1)} async-done(((bf16[8,32,1152]{2,1,0:T(8,128)(2,1)}), bf16[8,32,1152]{2,1,0:T(8,128)(2,1)S(1)}, u32[]{:S(2)}, u32[]{:S(2)}) %all-to-all-start) | async-done | bytes 589856 | tf_op jit(solution)/shard_map/all_to_all | solution.py:522
  28.1 4.2 %all-to-all-start.2 = ((bf16[8,32,1152]{2,1,0:T(8,128)(2,1)}), bf16[8,32,1152]{2,1,0:T(8,128)(2,1)}, u32[]{:S(2)}, u32[]{:S(2)}) async-start(bf16[8,32,1152]{2,1,0:T(8,128)(2,1)} %bitcast.17), calls=%async_computation.2 | async-start | bytes 1179648 | tf_op jit(solution)/shard_map/all_to_all | solution.py:522
  32.3 1.9 %copy-done.1 = bf16[2,1024,768]{2,1,0:T(8,128)(2,1)S(1)} copy-done((bf16[2,1024,768]{2,1,0:T(8,128)(2,1)S(1)}, bf16[2,1024,768]{2,1,0:T(8,128)(2,1)}, u32[]{:S(2)}) %copy-start.1) | copy-done | bytes 3145752
  34.2 1.1 copy-done.5
  35.3 3.8 %gate_up.3 = bf16[2,144,768]{2,1,0:T(8,128)(2,1)} custom-call(s32[1]{0:T(128)S(6)} %sub.8.pick_ref, bf16[8,2,16,1152]{3,2,1,0:T(8,128)(2,1)S(1)} %bitcast.51, bf16[2,1024,768]{2,1,0:T(8,128)(2,1)S(1)} %copy-done.1, bf16[2,1024,768]{2,1,0:T(8,128)(2,1)} %up_ref.5), custom_call_target="tpu_custom_call" | custom-call | flops 452984832 | bytes 3145728 | tf_op jit(solution)/shard_map/gate_up/pallas_call | solution.py:236
  39.9 2.9 %collective-permute-start = (bf16[128,256]{1,0:T(8,128)(2,1)S(1)}, bf16[128,256]{1,0:T(8,128)(2,1)S(1)}, u32[]{:S(2)}, u32[]{:S(2)}) collective-permute-start(bf16[128,256]{1,0:T(8,128)(2,1)S(1)} %pad_maximum_fusion.5), channel_id=1, source_target_pairs={{0,4},{1,5},{2,6},{3,7},{4,0},{5,1},{6,2},{7,3},{8,12},{9,13},{10,... | collective-permute-start | bytes 196616 | tf_op jit(solution)/shard_map/ppermute | solution.py:465
  42.8 7.3 %all-to-all-done.2 = bf16[8,32,1152]{2,1,0:T(8,128)(2,1)} async-done(((bf16[8,32,1152]{2,1,0:T(8,128)(2,1)}), bf16[8,32,1152]{2,1,0:T(8,128)(2,1)}, u32[]{:S(2)}, u32[]{:S(2)}) %all-to-all-start.2) | async-done | bytes 589856 | tf_op jit(solution)/shard_map/all_to_all | solution.py:522
  50.0 2.3 %hidden_grad.3 = bf16[144,768]{1,0:T(8,128)(2,1)S(1)} custom-call(s32[1]{0:T(128)S(6)} %sub.8.pick_ref, bf16[8,2,16,1152]{3,2,1,0:T(8,128)(2,1)} %bitcast.18.recv_ref, bf16[2,768,1024]{2,1,0:T(8,128)(2,1)S(1)} %copy-done), custom_call_target="tpu_custom_call" | custom-call | flops 226492416 | bytes 1572864 | tf_op jit(solution)/shard_map/hidden_grad/pallas_call | solution.py:269
  52.5 3.1 %gate_up.2 = f32[2,144,768]{2,1,0:T(8,128)S(1)} custom-call(s32[1]{0:T(128)} %bitcast.10.pick_ref, bf16[8,2,16,1152]{3,2,1,0:T(8,128)(2,1)S(1)} %bitcast.52, bf16[2,1024,768]{2,1,0:T(8,128)(2,1)S(1)} %copy-done.2, bf16[2,1024,768]{2,1,0:T(8,128)(2,1)} %up_ref.5), custom_call_target="tpu_custom_call" | custom-call | flops 452984832 | bytes 3145728 | tf_op jit(solution)/shard_map/gate_up/pallas_call | solution.py:236
  55.6 1.1 fusion
  56.7 1.6 %collective-permute-start.7 = (bf16[2,144,768]{2,1,0:T(8,128)(2,1)S(1)}, bf16[2,144,768]{2,1,0:T(8,128)(2,1)S(1)}, u32[]{:S(2)}, u32[]{:S(2)}) collective-permute-start(bf16[2,144,768]{2,1,0:T(8,128)(2,1)S(1)} %fusion), channel_id=1, source_target_pairs={{0,16},{8,24},{16,0},{24,8},{1,17},{9,25},{17,1},{25,9},{2,18},{10... | collective-permute-start | bytes 1327112 | tf_op jit(solution)/shard_map/ppermute | solution.py:465
  58.6 2.1 %hidden_grad.2 = f32[144,768]{1,0:T(8,128)S(1)} custom-call(s32[1]{0:T(128)} %bitcast.10.pick_ref, bf16[8,2,16,1152]{3,2,1,0:T(8,128)(2,1)} %bitcast.18.recv_ref, bf16[2,768,1024]{2,1,0:T(8,128)(2,1)S(1)} %copy-done), custom_call_target="tpu_custom_call" | custom-call | flops 226492416 | bytes 1572864 | tf_op jit(solution)/shard_map/hidden_grad/pallas_call | solution.py:269
  61.4 8.3 %collective-permute-done.7 = bf16[2,144,768]{2,1,0:T(8,128)(2,1)S(1)} collective-permute-done((bf16[2,144,768]{2,1,0:T(8,128)(2,1)S(1)}, bf16[2,144,768]{2,1,0:T(8,128)(2,1)S(1)}, u32[]{:S(2)}, u32[]{:S(2)}) %collective-permute-start.7) | collective-permute-done | bytes 442400 | tf_op jit(solution)/shard_map/ppermute | solution.py:465
  69.7 1.1 convert_add_fusion
  70.9 3.2 %collective-permute-done.10 = bf16[144,768]{1,0:T(8,128)(2,1)S(1)} collective-permute-done((bf16[144,768]{1,0:T(8,128)(2,1)S(1)}, bf16[144,768]{1,0:T(8,128)(2,1)S(1)}, u32[]{:S(2)}, u32[]{:S(2)}) %collective-permute-start.10) | collective-permute-done | bytes 221216 | tf_op jit(solution)/shard_map/ppermute | solution.py:465
  76.0 1.5 %collective-permute-start.2 = (bf16[512,256]{1,0:T(8,128)(2,1)S(1)}, bf16[512,256]{1,0:T(8,128)(2,1)}, u32[]{:S(2)}, u32[]{:S(2)}) collective-permute-start(bf16[512,256]{1,0:T(8,128)(2,1)S(1)} %pad_maximum_fusion.1.kv_ref), channel_id=1, source_target_pairs={{0,1},{1,0},{2,3},{3,2},{4,5},{5,4},{6,7},{7,6},{8,9},{9,8},{10,11... | collective-permute-start | bytes 786440 | tf_op jit(solution)/shard_map/ppermute | solution.py:465
  77.6 1.7 %route_out.1 = bf16[8,2,16,1152]{3,2,1,0:T(8,128)(2,1)S(1)} custom-call(s32[2]{0:T(128)S(1)} %pad_add_fusion.pick_ref, bf16[144,768]{1,0:T(8,128)(2,1)S(1)} %get-tuple-element.16.mine_ref, bf16[144,768]{1,0:T(8,128)(2,1)S(1)} %collective-permute-done.8.other_ref, bf16[2,768,1024]{2,1,0:T(8,128)(2,1)S(1)} %copy-done), custom_call_target="tpu_custom_call" | custom-call | flops 452984832 | bytes 3145728 | tf_op jit(solution)/shard_map/route_out/pallas_call | solution.py:298
  80.1 3.5 %all-to-all-start.1 = ((bf16[8,32,1152]{2,1,0:T(8,128)(2,1)}), bf16[8,32,1152]{2,1,0:T(8,128)(2,1)S(1)}, u32[]{:S(2)}, u32[]{:S(2)}) async-start(bf16[8,32,1152]{2,1,0:T(8,128)(2,1)} %bitcast.53), calls=%async_computation.1 | async-start | bytes 1179648 | tf_op jit(solution)/shard_map/all_to_all | solution.py:522
  83.6 1.2 collective-permute-done.2.kv_far_ref
  86.9 16.8 %attention.1 = (bf16[128,2048]{1,0:T(8,128)(2,1)}, bf16[128,2048]{1,0:T(8,128)(2,1)}, f32[512,256]{1,0:T(8,128)S(1)}, bf16[512,256]{1,0:T(8,128)(2,1)S(1)}) custom-call(s32[1]{0:T(128)} %bitcast.me_ref, bf16[128,2048]{1,0:T(8,128)(2,1)S(1)} %copy-done.10, bf16[128,2048]{1,0:T(8,128)(2,1)S(1)} %copy-done.11, bf16[512,256]{1,0:T(8,128)(2,1)S(1)} %pad_maximum_fusion.1.kv_ref, ...), custom_call_target="tpu_custom_call" | custom-call | flops 3221225472 | bytes 2097152 | tf_op jit(solution)/shard_map/attention/pallas_call | solution.py:435
  103.8 1.4 collective-permute-start.3
  105.3 6.4 %collective-permute-done.3 = bf16[512,256]{1,0:T(8,128)(2,1)S(1)} collective-permute-done((bf16[512,256]{1,0:T(8,128)(2,1)S(1)}, bf16[512,256]{1,0:T(8,128)(2,1)S(1)}, u32[]{:S(2)}, u32[]{:S(2)}) %collective-permute-start.3) | collective-permute-done | bytes 262176 | tf_op jit(solution)/shard_map/ppermute | solution.py:465
  112.8 5.3 %route_in.1 = bf16[8,2,16,1152]{3,2,1,0:T(8,128)(2,1)} custom-call(s32[2]{0:T(128)S(1)} %pad_add_fusion.pick_ref, bf16[2,144,768]{2,1,0:T(8,128)(2,1)S(1)} %pad_maximum_fusion.mine_ref, bf16[2,144,768]{2,1,0:T(8,128)(2,1)S(1)} %collective-permute-done.11.other_ref, bf16[2,1024,768]{2,1,0:T(8,128)(2,1)S(1)} %copy-done.3, bf16[2,1024,768]{2,1,0:T(8,128)(2,1)} %up_ref.5), custom_call_target="tpu_custom_call" | custom-call | flops 905969664 | bytes 6291456 | tf_op jit(solution)/shard_map/route_in/pallas_call | solution.py:327
  118.1 4.6 %all-to-all-start.3 = ((bf16[8,32,1152]{2,1,0:T(8,128)(2,1)}), bf16[8,32,1152]{2,1,0:T(8,128)(2,1)S(1)}, u32[]{:S(2)}, u32[]{:S(2)}) async-start(bf16[8,32,1152]{2,1,0:T(8,128)(2,1)} %bitcast.21), calls=%async_computation.3 | async-start | bytes 1179648 | tf_op jit(solution)/shard_map/all_to_all | solution.py:522
  122.7 3.0 %collective-permute-start.5 = (bf16[128,256]{1,0:T(8,128)(2,1)S(1)}, bf16[128,256]{1,0:T(8,128)(2,1)S(1)}, u32[]{:S(2)}, u32[]{:S(2)}) collective-permute-start(bf16[128,256]{1,0:T(8,128)(2,1)S(1)} %slice.77), channel_id=1, source_target_pairs={{0,4},{1,5},{2,6},{3,7},{4,0},{5,1},{6,2},{7,3},{8,12},{9,13},{10,... | collective-permute-start | bytes 196616 | tf_op jit(solution)/shard_map/ppermute | solution.py:465
  125.7 14.7 %collective-permute-done.5 = bf16[128,256]{1,0:T(8,128)(2,1)S(1)} collective-permute-done((bf16[128,256]{1,0:T(8,128)(2,1)S(1)}, bf16[128,256]{1,0:T(8,128)(2,1)S(1)}, u32[]{:S(2)}, u32[]{:S(2)}) %collective-permute-start.5) | collective-permute-done | bytes 65568 | tf_op jit(solution)/shard_map/ppermute | solution.py:465
  140.3 5.8 %all-gather = bf16[512,256]{1,0:T(8,128)(2,1)S(1)} all-gather(bf16[128,256]{1,0:T(8,128)(2,1)S(1)} %fusion.5), channel_id=2, replica_groups=mesh['ctx'=4,'exp'=8] {'ctx'}, dimensions={0}, use_global_device_ids=true | all-gather | bytes 327680 | tf_op jit(solution)/shard_map/all_gather | solution.py:576
  147.5 1.7 %combine_out.1 = bf16[128,1024]{1,0:T(8,128)(2,1)} custom-call(s32[128,2]{1,0:T(8,128)S(1)} %copy.19.ids_ref, f32[128,2]{1,0:T(8,128)S(1)} %copy.20.gain_ref, bf16[256,1152]{1,0:T(8,128)(2,1)S(1)} %bitcast.54), custom_call_target="tpu_custom_call" | custom-call | flops 268435456 | bytes 1179648 | tf_op jit(solution)/shard_map/combine_out/pallas_call | solution.py:168
  149.3 1.7 %combine_in.1 = bf16[128,1024]{1,0:T(8,128)(2,1)} custom-call(s32[128,2]{1,0:T(8,128)S(1)} %copy.19.ids_ref, f32[128,2]{1,0:T(8,128)S(1)} %copy.20.gain_ref, bf16[256,1152]{1,0:T(8,128)(2,1)S(1)} %bitcast.55), custom_call_target="tpu_custom_call" | custom-call | flops 268435456 | bytes 1179648 | tf_op jit(solution)/shard_map/combine_in/pallas_call | solution.py:168
  (70 shorter events, 12.8 us)
Async XLA Ops:
  5.0 23.1 %all-to-all-start = ((bf16[8,32,1152]{2,1,0:T(8,128)(2,1)}), bf16[8,32,1152]{2,1,0:T(8,128)(2,1)S(1)}, u32[]{:S(2)}, u32[]{:S(2)}) async-start(bf16[8,32,1152]{2,1,0:T(8,128)(2,1)} %bitcast.11), calls=%async_computation | async-start | bytes 1179648 | tf_op jit(solution)/shard_map/all_to_all | solution.py:522
  28.1 4.2 %copy-start.4 = (bf16[8,32,1152]{2,1,0:T(8,128)(2,1)}, bf16[8,32,1152]{2,1,0:T(8,128)(2,1)S(1)}, u32[]{:S(2)}) copy-start(bf16[8,32,1152]{2,1,0:T(8,128)(2,1)S(1)} %all-to-all-done) | copy-start | bytes 1769476
  28.1 21.9 %all-to-all-start.2 = ((bf16[8,32,1152]{2,1,0:T(8,128)(2,1)}), bf16[8,32,1152]{2,1,0:T(8,128)(2,1)}, u32[]{:S(2)}, u32[]{:S(2)}) async-start(bf16[8,32,1152]{2,1,0:T(8,128)(2,1)} %bitcast.17), calls=%async_computation.2 | async-start | bytes 1179648 | tf_op jit(solution)/shard_map/all_to_all | solution.py:522
  32.3 1.9 %copy-start.1 = (bf16[2,1024,768]{2,1,0:T(8,128)(2,1)S(1)}, bf16[2,1024,768]{2,1,0:T(8,128)(2,1)}, u32[]{:S(2)}) copy-start(bf16[2,1024,768]{2,1,0:T(8,128)(2,1)} %gate_ref.5) | copy-start | bytes 9437188
  34.2 1.1 copy-start.5
  35.3 14.8 %copy-start = (bf16[2,768,1024]{2,1,0:T(8,128)(2,1)S(1)}, bf16[2,768,1024]{2,1,0:T(8,128)(2,1)}, u32[]{:S(2)}) copy-start(bf16[2,768,1024]{2,1,0:T(8,128)(2,1)} %down_ref.5) | copy-start | bytes 9437188
  39.1 16.5 %collective-permute-start.6 = (bf16[2,144,768]{2,1,0:T(8,128)(2,1)}, bf16[2,144,768]{2,1,0:T(8,128)(2,1)}, u32[]{:S(2)}, u32[]{:S(2)}) collective-permute-start(bf16[2,144,768]{2,1,0:T(8,128)(2,1)} %gate_up.3), channel_id=1, source_target_pairs={{0,8},{8,0},{16,24},{24,16},{1,9},{9,1},{17,25},{25,17},{2,10},{10... | collective-permute-start | bytes 1327112 | tf_op jit(solution)/shard_map/ppermute | solution.py:465
  39.9 18.4 %copy-start.14 = (bf16[128,128]{1,0:T(8,128)(2,1)}, bf16[128,128]{1,0:T(8,128)(2,1)S(1)}, u32[]{:S(2)}) copy-start(bf16[128,128]{1,0:T(8,128)(2,1)S(1)} %get-tuple-element.25) | copy-start | bytes 98308
  39.9 18.4 %copy-start.16 = (bf16[128,128]{1,0:T(8,128)(2,1)}, bf16[128,128]{1,0:T(8,128)(2,1)S(1)}, u32[]{:S(2)}) copy-start(bf16[128,128]{1,0:T(8,128)(2,1)S(1)} %get-tuple-element.26) | copy-start | bytes 98308
  39.9 18.4 %collective-permute-start = (bf16[128,256]{1,0:T(8,128)(2,1)S(1)}, bf16[128,256]{1,0:T(8,128)(2,1)S(1)}, u32[]{:S(2)}, u32[]{:S(2)}) collective-permute-start(bf16[128,256]{1,0:T(8,128)(2,1)S(1)} %pad_maximum_fusion.5), channel_id=1, source_target_pairs={{0,4},{1,5},{2,6},{3,7},{4,0},{5,1},{6,2},{7,3},{8,12},{9,13},{10,... | collective-permute-start | bytes 196616 | tf_op jit(solution)/shard_map/ppermute | solution.py:465
  50.0 2.4 %copy-start.2 = (bf16[2,1024,768]{2,1,0:T(8,128)(2,1)S(1)}, bf16[2,1024,768]{2,1,0:T(8,128)(2,1)}, u32[]{:S(2)}) copy-start(bf16[2,1024,768]{2,1,0:T(8,128)(2,1)} %gate_ref.5) | copy-start | bytes 9437188
  50.0 2.4 %copy-start.6 = (bf16[8,32,1152]{2,1,0:T(8,128)(2,1)S(1)}, bf16[8,32,1152]{2,1,0:T(8,128)(2,1)}, u32[]{:S(2)}) copy-start(bf16[8,32,1152]{2,1,0:T(8,128)(2,1)} %copy-done.4) | copy-start | bytes 1769476
  52.4 8.4 %collective-permute-start.9 = (bf16[144,768]{1,0:T(8,128)(2,1)S(1)}, bf16[144,768]{1,0:T(8,128)(2,1)S(1)}, u32[]{:S(2)}, u32[]{:S(2)}) collective-permute-start(bf16[144,768]{1,0:T(8,128)(2,1)S(1)} %hidden_grad.3), channel_id=1, source_target_pairs={{0,8},{8,0},{16,24},{24,16},{1,9},{9,1},{17,25},{25,17},{2,10},{10... | collective-permute-start | bytes 663560 | tf_op jit(solution)/shard_map/ppermute | solution.py:465
  56.7 13.0 %collective-permute-start.7 = (bf16[2,144,768]{2,1,0:T(8,128)(2,1)S(1)}, bf16[2,144,768]{2,1,0:T(8,128)(2,1)S(1)}, u32[]{:S(2)}, u32[]{:S(2)}) collective-permute-start(bf16[2,144,768]{2,1,0:T(8,128)(2,1)S(1)} %fusion), channel_id=1, source_target_pairs={{0,16},{8,24},{16,0},{24,8},{1,17},{9,25},{17,1},{25,9},{2,18},{10... | collective-permute-start | bytes 1327112 | tf_op jit(solution)/shard_map/ppermute | solution.py:465
  58.3 12.6 %copy-start.18 = (bf16[128,256]{1,0:T(8,128)(2,1)}, bf16[128,256]{1,0:T(8,128)(2,1)S(1)}, u32[]{:S(2)}) copy-start(bf16[128,256]{1,0:T(8,128)(2,1)S(1)} %collective-permute-done) | copy-start | bytes 196612
  58.4 16.7 %collective-permute-start.1 = (bf16[256,256]{1,0:T(8,128)(2,1)S(1)}, bf16[256,256]{1,0:T(8,128)(2,1)S(1)}, u32[]{:S(2)}, u32[]{:S(2)}) collective-permute-start(bf16[256,256]{1,0:T(8,128)(2,1)S(1)} %pad_maximum_fusion.2), channel_id=1, source_target_pairs={{0,2},{1,3},{2,0},{3,1},{4,6},{5,7},{6,4},{7,5},{8,10},{9,11},{10,... | collective-permute-start | bytes 393224 | tf_op jit(solution)/shard_map/ppermute | solution.py:465
  60.8 14.3 %copy-start.15 = (bf16[128,128]{1,0:T(8,128)(2,1)S(1)}, bf16[128,128]{1,0:T(8,128)(2,1)}, u32[]{:S(2)}) copy-start(bf16[128,128]{1,0:T(8,128)(2,1)} %copy-done.14) | copy-start | bytes 98308
  60.8 14.3 %copy-start.17 = (bf16[128,128]{1,0:T(8,128)(2,1)S(1)}, bf16[128,128]{1,0:T(8,128)(2,1)}, u32[]{:S(2)}) copy-start(bf16[128,128]{1,0:T(8,128)(2,1)} %copy-done.16) | copy-start | bytes 98308
  60.9 13.2 %collective-permute-start.10 = (bf16[144,768]{1,0:T(8,128)(2,1)S(1)}, bf16[144,768]{1,0:T(8,128)(2,1)S(1)}, u32[]{:S(2)}, u32[]{:S(2)}) collective-permute-start(bf16[144,768]{1,0:T(8,128)(2,1)S(1)} %fusion.2), channel_id=1, source_target_pairs={{0,16},{8,24},{16,0},{24,8},{1,17},{9,25},{17,1},{25,9},{2,18},{10... | collective-permute-start | bytes 663560 | tf_op jit(solution)/shard_map/ppermute | solution.py:465
  75.1 2.5 %collective-permute-start.8 = (bf16[144,768]{1,0:T(8,128)(2,1)S(1)}, bf16[144,768]{1,0:T(8,128)(2,1)S(1)}, u32[]{:S(2)}, u32[]{:S(2)}) collective-permute-start(bf16[144,768]{1,0:T(8,128)(2,1)S(1)} %get-tuple-element.16.mine_ref), channel_id=1, source_target_pairs={{0,8},{8,0},{16,24},{24,16},{1,9},{9,1},{17,25},{25,17},{2,10},{10... | collective-permute-start | bytes 663560 | tf_op jit(solution)/shard_map/ppermute | solution.py:465
  76.0 8.9 %collective-permute-start.2 = (bf16[512,256]{1,0:T(8,128)(2,1)S(1)}, bf16[512,256]{1,0:T(8,128)(2,1)}, u32[]{:S(2)}, u32[]{:S(2)}) collective-permute-start(bf16[512,256]{1,0:T(8,128)(2,1)S(1)} %pad_maximum_fusion.1.kv_ref), channel_id=1, source_target_pairs={{0,1},{1,0},{2,3},{3,2},{4,5},{5,4},{6,7},{7,6},{8,9},{9,8},{10,11... | collective-permute-start | bytes 786440 | tf_op jit(solution)/shard_map/ppermute | solution.py:465
  80.1 38.0 %all-to-all-start.1 = ((bf16[8,32,1152]{2,1,0:T(8,128)(2,1)}), bf16[8,32,1152]{2,1,0:T(8,128)(2,1)S(1)}, u32[]{:S(2)}, u32[]{:S(2)}) async-start(bf16[8,32,1152]{2,1,0:T(8,128)(2,1)} %bitcast.53), calls=%async_computation.1 | async-start | bytes 1179648 | tf_op jit(solution)/shard_map/all_to_all | solution.py:522
  84.9 1.0 copy-start.10
  85.9 1.0 copy-start.11
  86.9 18.3 %copy-start.12 = (bf16[1,144,768]{2,1,0:T(8,128)(2,1)S(1)}, bf16[1,144,768]{2,1,0:T(8,128)(2,1)}, u32[]{:S(2)}) copy-start(bf16[1,144,768]{2,1,0:T(8,128)(2,1)} %get-tuple-element.14) | copy-start | bytes 663556
  86.9 18.3 %copy-start.13 = (bf16[1,144,768]{2,1,0:T(8,128)(2,1)S(1)}, bf16[1,144,768]{2,1,0:T(8,128)(2,1)}, u32[]{:S(2)}) copy-start(bf16[1,144,768]{2,1,0:T(8,128)(2,1)} %get-tuple-element.15) | copy-start | bytes 663556
  86.9 25.8 %copy-start.3 = (bf16[2,1024,768]{2,1,0:T(8,128)(2,1)S(1)}, bf16[2,1024,768]{2,1,0:T(8,128)(2,1)}, u32[]{:S(2)}) copy-start(bf16[2,1024,768]{2,1,0:T(8,128)(2,1)} %gate_ref.5) | copy-start | bytes 9437188
  103.8 7.9 %collective-permute-start.3 = (bf16[512,256]{1,0:T(8,128)(2,1)S(1)}, bf16[512,256]{1,0:T(8,128)(2,1)S(1)}, u32[]{:S(2)}, u32[]{:S(2)}) collective-permute-start(bf16[512,256]{1,0:T(8,128)(2,1)S(1)} %get-tuple-element.13), channel_id=1, source_target_pairs={{0,1},{1,0},{2,3},{3,2},{4,5},{5,4},{6,7},{7,6},{8,9},{9,8},{10,11... | collective-permute-start | bytes 786440 | tf_op jit(solution)/shard_map/ppermute | solution.py:465
  105.3 7.5 %collective-permute-start.11 = (bf16[2,144,768]{2,1,0:T(8,128)(2,1)S(1)}, bf16[2,144,768]{2,1,0:T(8,128)(2,1)S(1)}, u32[]{:S(2)}, u32[]{:S(2)}) collective-permute-start(bf16[2,144,768]{2,1,0:T(8,128)(2,1)S(1)} %pad_maximum_fusion.mine_ref), channel_id=1, source_target_pairs={{0,8},{8,0},{16,24},{24,16},{1,9},{9,1},{17,25},{25,17},{2,10},{10... | collective-permute-start | bytes 1327112 | tf_op jit(solution)/shard_map/ppermute | solution.py:465
  111.8 10.9 %collective-permute-start.4 = (bf16[256,256]{1,0:T(8,128)(2,1)S(1)}, bf16[256,256]{1,0:T(8,128)(2,1)S(1)}, u32[]{:S(2)}, u32[]{:S(2)}) collective-permute-start(bf16[256,256]{1,0:T(8,128)(2,1)S(1)} %slice.76), channel_id=1, source_target_pairs={{0,2},{1,3},{2,0},{3,1},{4,6},{5,7},{6,4},{7,5},{8,10},{9,11},{10,... | collective-permute-start | bytes 393224 | tf_op jit(solution)/shard_map/ppermute | solution.py:465
  118.1 31.2 %all-to-all-start.3 = ((bf16[8,32,1152]{2,1,0:T(8,128)(2,1)}), bf16[8,32,1152]{2,1,0:T(8,128)(2,1)S(1)}, u32[]{:S(2)}, u32[]{:S(2)}) async-start(bf16[8,32,1152]{2,1,0:T(8,128)(2,1)} %bitcast.21), calls=%async_computation.3 | async-start | bytes 1179648 | tf_op jit(solution)/shard_map/all_to_all | solution.py:522
  122.7 17.6 %collective-permute-start.5 = (bf16[128,256]{1,0:T(8,128)(2,1)S(1)}, bf16[128,256]{1,0:T(8,128)(2,1)S(1)}, u32[]{:S(2)}, u32[]{:S(2)}) collective-permute-start(bf16[128,256]{1,0:T(8,128)(2,1)S(1)} %slice.77), channel_id=1, source_target_pairs={{0,4},{1,5},{2,6},{3,7},{4,0},{5,1},{6,2},{7,3},{8,12},{9,13},{10,... | collective-permute-start | bytes 196616 | tf_op jit(solution)/shard_map/ppermute | solution.py:465
  (3 other events, 2.7 us)

commit v2 on v1

v2 whole, which is shorter than its diff:
```python
import functools
import math

import jax
import jax.numpy as jnp
from jax import lax
from jax.experimental import pallas as pl
from jax.experimental.pallas import tpu as pltpu
from jax.sharding import PartitionSpec as P

HEAD_SIZE = 128
LANES = 128
ROW_TILE = 16
PAIRS = 2
SMALL_VMEM = 16 * 1024 * 1024
LARGE_VMEM = 20 * 1024 * 1024
EXPERT_VMEM = 16 * 1024 * 1024
BF16 = jnp.bfloat16
F32 = jnp.float32


def dot(a, b, a_dim=1, b_dim=0):
    return lax.dot_general(a, b, (((a_dim,), (b_dim,)), ((), ())), preferred_element_type=F32)


def iota(shape, dim):
    return lax.broadcasted_iota(jnp.int32, shape, dim)


def params(vmem_bytes):
    return pltpu.CompilerParams(vmem_limit_bytes=vmem_bytes, dimension_semantics=("arbitrary",))


def in_hbm(value):
    return pltpu.with_memory_space_constraint(value, pltpu.HBM)


def cost(flops, bytes_accessed, transcendentals=0):
    return pl.CostEstimate(
        flops=int(flops), bytes_accessed=int(bytes_accessed), transcendentals=int(transcendentals)
    )


def power_of_two(value):
    return value > 0 and value & (value - 1) == 0


class Slots:
    def __init__(self, slot_count, width, exp_count, local_experts):
        whole = slot_count // ROW_TILE * ROW_TILE
        rem = slot_count - whole
        blocks = width // LANES
        self.fold = (
            whole > 0
            and rem > 0
            and power_of_two(rem)
            and power_of_two(exp_count)
            and rem * blocks <= whole
            and (rem * exp_count) % ROW_TILE == 0
        )
        self.rows = whole if self.fold or rem == 0 else whole + ROW_TILE
        self.rem = rem if self.fold else 0
        self.blocks = blocks
        self.width = width
        self.columns = width + (LANES if self.fold else 0)
        self.exp_count = exp_count
        self.local = local_experts
        self.experts = exp_count * local_experts
        self.total = self.experts * self.rows
        self.per_expert = exp_count * (self.rows + self.rem)


def route_places(ids, slots):
    top, tokens = ids.shape
    expert = iota((-(-slots.experts // ROW_TILE) * ROW_TILE, tokens), 0)
    hits = [(ids[r : r + 1, :] == expert).astype(F32) for r in range(top)]
    earlier = (iota((tokens, tokens), 0) < iota((tokens, tokens), 1)).astype(BF16)
    before = dot(sum(hits).astype(BF16), earlier)
    found = []
    for r in range(top):
        rank = jnp.sum(hits[r] * before, axis=0, keepdims=True)
        base = ids[r : r + 1, :].astype(F32) * slots.rows
        inside = rank < slots.rows
        main = jnp.where(inside, base + rank, -1.0)
        folded = jnp.where(inside, -65536.0, base + rank - slots.rows)
        found.append((main, folded))
    return found


def as_column(row):
    tokens = row.shape[1]
    return jnp.transpose(jnp.broadcast_to(row, (LANES, tokens)))[:, 0:1]


def dispatch_kernel(slots, weighted, ids_ref, gain_ref, rows_ref, out_ref):
    top, tokens = ids_ref.shape
    places = route_places(ids_ref[...], slots)
    gains = [gain_ref[r : r + 1, :] for r in range(top)]
    slot = iota((slots.total, tokens), 0).astype(F32)
    rows = rows_ref[...]

    def picks(wanted):
        pick = jnp.zeros((slots.total, tokens), F32)
        gain = pick
        for r in range(top):
            here = slot == wanted[r]
            pick = jnp.where(here, 1.0, pick)
            gain = jnp.where(here, gains[r], gain)
        return pick.astype(BF16), gain

    pick, gain = picks([main for main, _ in places])
    taken = dot(pick, rows)
    if weighted:
        taken = taken * jnp.sum(gain, axis=1, keepdims=True)
    out_ref[:, : slots.width] = taken.astype(BF16)
    if slots.fold:
        taken = jnp.zeros((slots.total, LANES), F32)
        total_gain = jnp.zeros((slots.total, tokens), F32)
        for f in range(slots.blocks):
            pick, gain = picks([start + float(f * slots.rem) for _, start in places])
            taken = taken + dot(pick, rows[:, f * LANES : (f + 1) * LANES])
            total_gain = total_gain + gain
        if weighted:
            taken = taken * jnp.sum(total_gain, axis=1, keepdims=True)
        out_ref[:, slots.width :] = taken.astype(BF16)


def dispatch(slots, weighted, ids, gains, rows):
    return pl.pallas_call(
        functools.partial(dispatch_kernel, slots, weighted),
        out_shape=jax.ShapeDtypeStruct((slots.total, slots.columns), BF16),
        compiler_params=pltpu.CompilerParams(vmem_limit_bytes=LARGE_VMEM),
        cost_estimate=cost(4 * slots.total * LANES * slots.width, 4 * slots.total * slots.columns),
        name="dispatch_scaled" if weighted else "dispatch_rows",
    )(in_hbm(ids), in_hbm(gains), in_hbm(rows))


def combine_kernel(slots, weighted, ids_ref, gain_ref, back_ref, out_ref):
    top, tokens = ids_ref.shape
    places = [
        (as_column(main), as_column(start))
        for main, start in route_places(ids_ref[...], slots)
    ]
    gains = [as_column(gain_ref[r : r + 1, :]) if weighted else 1.0 for r in range(top)]
    slot = iota((tokens, slots.total), 1).astype(F32)

    def table(wanted):
        found = jnp.zeros((tokens, slots.total), F32)
        for r in range(top):
            found = jnp.where(slot == wanted[r], gains[r], found)
        return found

    def apply(found, rows):
        high = found.astype(BF16)
        result = dot(high, rows)
        if weighted:
            result = result + dot((found - high.astype(F32)).astype(BF16), rows)
        return result

    result = apply(table([main for main, _ in places]), back_ref[:, : slots.width])
    if slots.fold:
        folded = back_ref[:, slots.width :]
        extra = [
            apply(table([start + float(f * slots.rem) for _, start in places]), folded)
            for f in range(slots.blocks)
        ]
        result = result + jnp.concatenate(extra, axis=1)
    out_ref[...] = result.astype(BF16)


def combine(slots, weighted, ids, gains, back):
    tokens = ids.shape[1]
    return pl.pallas_call(
        functools.partial(combine_kernel, slots, weighted),
        out_shape=jax.ShapeDtypeStruct((tokens, slots.width), BF16),
        compiler_params=pltpu.CompilerParams(vmem_limit_bytes=SMALL_VMEM),
        cost_estimate=cost(8 * slots.total * LANES * slots.width, 4 * slots.total * slots.columns),
        name="combine_out" if weighted else "combine_in",
    )(ids, gains, back)


def fold_table(slots, shape, folded_dim):
    folded = iota(shape, folded_dim)
    plain = iota(shape, 1 - folded_dim)
    rem_bits = int(math.log2(slots.rem))
    exp_bits = int(math.log2(slots.exp_count))
    j = plain & (slots.rem - 1)
    source = (plain >> rem_bits) & (slots.exp_count - 1)
    f = plain >> (rem_bits + exp_bits)
    return (folded == source * slots.rows + f * slots.rem + j).astype(F32).astype(BF16)


def unpack_rows(slots, block):
    flat = block.reshape(slots.exp_count * slots.rows, slots.columns)
    if not slots.fold:
        return flat
    each = slots.exp_count * slots.rem
    plain = dot(
        fold_table(slots, (slots.blocks * each, slots.exp_count * slots.rows), 1),
        flat[:, slots.width :],
    ).astype(BF16)
    extra = jnp.concatenate(
        [plain[f * each : (f + 1) * each] for f in range(slots.blocks)], axis=1
    )
    return jnp.concatenate([flat[:, : slots.width], extra], axis=0)


def pack_rows(slots, rows, out_ref):
    count = slots.exp_count * slots.rows
    main = rows[:count].reshape(slots.exp_count, slots.rows, slots.width)
    out_ref[:, :, : slots.width] = main
    if slots.fold:
        each = slots.exp_count * slots.rem
        stacked = jnp.concatenate(
            [rows[count:, f * LANES : (f + 1) * LANES] for f in range(slots.blocks)], axis=0
        )
        folded = dot(fold_table(slots, (count, slots.blocks * each), 0), stacked).astype(BF16)
        out_ref[:, :, slots.width :] = folded.reshape(slots.exp_count, slots.rows, LANES)


def hold_kernel(*refs):
    count = len(refs) // 2
    copies = [
        pltpu.make_async_copy(refs[i], refs[count + i], refs[-1].at[i]) for i in range(count)
    ]
    for copy in copies:
        copy.start()
    for copy in copies:
        copy.wait()


def hold(*weights):
    return pl.pallas_call(
        hold_kernel,
        in_specs=[pl.BlockSpec(memory_space=pl.ANY)] * len(weights),
        out_specs=[pl.BlockSpec(memory_space=pltpu.VMEM)] * len(weights),
        out_shape=[pltpu.VMEM(value.shape, value.dtype) for value in weights],
        scratch_shapes=[pltpu.SemaphoreType.DMA((len(weights),))],
        compiler_params=pltpu.CompilerParams(vmem_limit_bytes=SMALL_VMEM),
        cost_estimate=cost(0, sum(value.size * 4 for value in weights)),
        name="hold_weights",
    )(*[in_hbm(value) for value in weights])


def expert_call(kernel, name, out_shape, scalars, *operands):
    in_vmem = pl.BlockSpec(memory_space=pltpu.VMEM)
    return pl.pallas_call(
        kernel,
        in_specs=[pl.BlockSpec(memory_space=pltpu.SMEM)] + [in_vmem] * len(operands),
        out_specs=[in_vmem] * len(out_shape) if isinstance(out_shape, list) else in_vmem,
        out_shape=out_shape,
        compiler_params=pltpu.CompilerParams(vmem_limit_bytes=EXPERT_VMEM),
        name=name,
    )(scalars, *operands)


def expert_part(kernel, name, slots, expert, recv, weights, shape, arrived):
    if arrived is None:
        out = jax.ShapeDtypeStruct(shape, BF16)
        return expert_call(functools.partial(kernel, slots), name, out, expert, recv, *weights)
    out = [jax.ShapeDtypeStruct(shape, F32), jax.ShapeDtypeStruct(shape, BF16)]
    return expert_call(functools.partial(kernel, slots), name, out, expert, recv, *weights, arrived)


def store_part(index, part, refs):
    if len(refs) == 1:
        refs[0][index] = part.astype(BF16)
        return
    arrived_ref, out_ref, low_ref = refs
    total = part + arrived_ref[index].astype(F32)
    out_ref[index] = total
    low_ref[index] = total.astype(BF16)


def gate_up_kernel(slots, expert_ref, recv_ref, gate_ref, up_ref, *refs):
    e = expert_ref[0]
    rows = unpack_rows(slots, recv_ref[:, e])
    store_part(0, dot(rows, gate_ref[e]), refs)
    store_part(1, dot(rows, up_ref[e]), refs)


def gate_up(slots, expert, recv, gate_proj, up_proj, arrived=None):
    shape = (2, slots.per_expert, gate_proj.shape[2])
    weights = (gate_proj, up_proj)
    return expert_part(gate_up_kernel, "gate_up", slots, expert, recv, weights, shape, arrived)


def hidden_grad_kernel(slots, expert_ref, recv_ref, down_ref, *refs):
    e = expert_ref[0]
    rows = unpack_rows(slots, recv_ref[:, e])
    store_part(..., dot(rows, down_ref[e], 1, 1), refs)


def hidden_grad_part(slots, expert, recv, down_proj, arrived=None):
    shape = (slots.per_expert, down_proj.shape[1])
    return expert_part(
        hidden_grad_kernel, "hidden_grad", slots, expert, recv, (down_proj,), shape, arrived
    )


def route_out_kernel(slots, order_ref, mine_ref, other_ref, down_ref, out_ref):
    for at, hidden_ref in enumerate((mine_ref, other_ref)):
        e = order_ref[at]
        pack_rows(slots, dot(hidden_ref[...], down_ref[e]).astype(BF16), out_ref.at[:, e])


def route_out(slots, order, mine, other, down_proj):
    out = jax.ShapeDtypeStruct((slots.exp_count, slots.local, slots.rows, slots.columns), BF16)
    kernel = functools.partial(route_out_kernel, slots)
    return expert_call(kernel, "route_out", out, order, mine, other, down_proj)


def route_in_kernel(slots, order_ref, mine_ref, other_ref, gate_ref, up_ref, out_ref):
    for at, back_ref in enumerate((mine_ref, other_ref)):
        e = order_ref[at]
        total = dot(back_ref[0], gate_ref[e], 1, 1) + dot(back_ref[1], up_ref[e], 1, 1)
        pack_rows(slots, total.astype(BF16), out_ref.at[:, e])


def route_in(slots, order, mine, other, gate_proj, up_proj):
    out = jax.ShapeDtypeStruct((slots.exp_count, slots.local, slots.rows, slots.columns), BF16)
    kernel = functools.partial(route_in_kernel, slots)
    return expert_call(kernel, "route_in", out, order, mine, other, gate_proj, up_proj)


def attention_kernel(offsets, tokens, chunk, first, last, me_ref, q_ref, g_ref, kv_ref, kv_far_ref, *refs):
    if not first:
        carry_ref, refs = refs[0], refs[3:]
    out_ref, qgrad_ref = refs[:2]
    if last:
        keep_ref, send_ref = refs[2:4]
    else:
        carried_ref = refs[2]
    scores_ref, low_ref, key_t, value_t, key_acc, value_acc = refs[-6:]
    d = HEAD_SIZE
    step = pl.program_id(0)
    me = me_ref[0]
    half = kv_ref.shape[0]
    seq = 2 * half
    scale = d ** (-0.5)
    to_base2 = scale * math.log2(math.e)

    @pl.when(step == 0)
    def _():
        for start, ref in ((0, kv_ref), (half, kv_far_ref)):
            for at in range(0, half, tokens):
                both = jnp.transpose(ref[at : at + tokens, :])
                key_t[:, start + at : start + at + tokens] = both[:d]
                value_t[:, start + at : start + at + tokens] = both[d:]
        if first:
            key_acc[...] = jnp.zeros_like(key_acc)
            value_acc[...] = jnp.zeros_like(value_acc)
        else:
            key_acc[...] = carry_ref[:, :d]
            value_acc[...] = carry_ref[:, d:]

    def piece(at, column):
        ref, start = (kv_ref, at) if at < half else (kv_far_ref, at - half)
        return ref[start : start + chunk, column : column + d]

    pairs = scores_ref.shape[0]
    lanes = scores_ref.shape[2]
    heads = lanes // tokens
    chunks = range(0, seq, chunk)
    ahead = iota((tokens, lanes), 0) - (iota((tokens, lanes), 1) & (tokens - 1))
    limits = [(me - (me ^ offset)) * tokens for offset in offsets]

    def columns(pair, h):
        start = (pair * heads + h) * d
        return slice(start, start + d)

    def stacked(ref, pair):
        return jnp.concatenate([ref[:, columns(pair, h)] for h in range(heads)], axis=0)

    every = range(pairs)
    q = [stacked(q_ref, pair) for pair in every]
    g = [stacked(g_ref, pair) for pair in every]
    q_t = [jnp.transpose(value) for value in q]
    g_t = [jnp.transpose(value) for value in g]

    top = []
    for pair in every:
        largest = jnp.full((1, lanes), -jnp.inf, F32)
        for at in chunks:
            scores = dot(piece(at, 0), q_t[pair])
            for part in range(0, chunk, tokens):
                allowed = ahead <= limits[(at + part) // tokens]
                some = jnp.where(allowed, scores[part : part + tokens], -jnp.inf)
                scores_ref[pair, at + part : at + part + tokens, :] = some
                largest = jnp.maximum(largest, jnp.max(some, axis=0, keepdims=True))
        top.append(largest * to_base2)
    inverse = []
    for pair in every:
        total = jnp.zeros((1, lanes), F32)
        for at in chunks:
            raised = jnp.exp2(scores_ref[pair, at : at + chunk, :] * to_base2 - top[pair])
            low_ref[pair, at : at + chunk, :] = raised.astype(BF16)
            total = total + jnp.sum(raised, axis=0, keepdims=True)
        inverse.append(1.0 / total)
    row_dot = []
    for pair in every:
        spread = jnp.zeros((d, lanes), F32)
        for at in chunks:
            spread = spread + dot(value_t[:, at : at + chunk], low_ref[pair, at : at + chunk, :])
        attended = (spread * inverse[pair]).astype(BF16).astype(F32)
        row_dot.append(jnp.sum(g_t[pair].astype(F32) * attended, axis=0, keepdims=True))
        for h in range(heads):
            rows = slice(h * tokens, (h + 1) * tokens)
            out_ref[:, columns(pair, h)] = jnp.transpose(attended[:, rows]).astype(BF16)
    for pair in every:
        q_even = jnp.transpose(q_t[pair].astype(F32) * inverse[pair]).astype(BF16)
        g_even = jnp.transpose(g_t[pair].astype(F32) * inverse[pair]).astype(BF16)
        query_back = jnp.zeros((d, lanes), F32)
        for at in chunks:
            low = low_ref[pair, at : at + chunk, :]
            prob_grad = dot(piece(at, d), g_t[pair])
            score_grad = (low.astype(F32) * (prob_grad - row_dot[pair])).astype(BF16)
            query_back = query_back + dot(key_t[:, at : at + chunk], score_grad)
            key_acc[at : at + chunk, :] += dot(score_grad, q_even)
            value_acc[at : at + chunk, :] += dot(low, g_even)
        query_back = query_back * (inverse[pair] * scale)
        for h in range(heads):
            rows = slice(h * tokens, (h + 1) * tokens)
            qgrad_ref[:, columns(pair, h)] = jnp.transpose(query_back[:, rows]).astype(BF16)

    @pl.when(step == pl.num_programs(0) - 1)
    def _():
        if last:
            keep_ref[:, :d] = key_acc[:half, :] * scale
            keep_ref[:, d:] = value_acc[:half, :]
            send_ref[:, :d] = (key_acc[half:, :] * scale).astype(BF16)
            send_ref[:, d:] = value_acc[half:, :].astype(BF16)
        else:
            carried_ref[:, :d] = key_acc[...]
            carried_ref[:, d:] = value_acc[...]


def attention(me, offsets, queries, attn_grad, kv_near, kv_far, part, parts, carried=None):
    tokens, columns = queries.shape
    half, both = kv_near.shape
    seq = 2 * half
    heads = columns // HEAD_SIZE
    group = 2 if heads % (2 * parts) == 0 else 1
    pairs = PAIRS if heads % (group * PAIRS * parts) == 0 and seq <= 2048 else 1
    lanes = group * tokens
    chunk = min(256, half)
    steps = heads // (group * pairs * parts)
    first, last = part == 0, part == parts - 1
    tile = pl.BlockSpec((tokens, pairs * group * HEAD_SIZE), lambda i, m: (0, i + part * steps))
    whole = pl.BlockSpec((half, both), lambda i, m: (0, 0))
    sums = pl.BlockSpec((seq, both), lambda i, m: (0, 0))
    held = pl.BlockSpec(memory_space=pl.ANY)
    wide = jax.ShapeDtypeStruct(queries.shape, BF16)
    if last:
        final = [jax.ShapeDtypeStruct((half, both), F32), jax.ShapeDtypeStruct((half, both), BF16)]
    else:
        final = [jax.ShapeDtypeStruct((seq, both), F32)]
    return pl.pallas_call(
        functools.partial(attention_kernel, offsets, tokens, chunk, first, last),
        grid_spec=pltpu.PrefetchScalarGridSpec(
            num_scalar_prefetch=1,
            grid=(steps,),
            in_specs=[tile, tile, whole, whole] + ([] if first else [sums, held, held]),
            out_specs=[tile, tile] + ([whole, whole] if last else [sums]),
            scratch_shapes=[
                pltpu.VMEM((pairs, seq, lanes), F32),
                pltpu.VMEM((pairs, seq, lanes), BF16),
                pltpu.VMEM((HEAD_SIZE, seq), BF16),
                pltpu.VMEM((HEAD_SIZE, seq), BF16),
                pltpu.VMEM((seq, HEAD_SIZE), F32),
                pltpu.VMEM((seq, HEAD_SIZE), F32),
            ],
        ),
        out_shape=[wide, wide] + final,
        input_output_aliases={} if first else {6: 0, 7: 1},
        compiler_params=params(LARGE_VMEM),
        cost_estimate=cost(
            12 * tokens * columns * seq // parts,
            8 * tokens * columns // parts,
            tokens * heads * seq // parts,
        ),
        name="attention",
    )(me, in_hbm(queries), in_hbm(attn_grad), kv_near, kv_far, *(() if first else (carried[2], carried[0], carried[1])))


def swap(value, axis, bit):
    count = lax.axis_size(axis)
    return lax.ppermute(value, axis, [(i, i ^ bit) for i in range(count)])


def after(value, *earlier):
    return lax.optimization_barrier((value, *earlier))[0]


def far_bits(count):
    bits = []
    bit = count // 2
    while bit >= 1:
        bits.append(bit)
        bit //= 2
    return bits


def spread_sum(part, low, ctx_count, beside):
    result = None
    bit = 2
    while bit < ctx_count:
        arrived = swap(low, "ctx", bit)
        if result is None:
            result = beside(low)
            arrived = after(arrived, *result)
        part = part + arrived.astype(F32)
        low = part.astype(BF16)
        bit *= 2
    return part, beside(low) if result is None else result


def activate(gate, up):
    return (jax.nn.silu(gate) * up).astype(BF16)


def gate_backward(hidden_grad, gate, up):
    s = jax.nn.sigmoid(gate)
    gate_back = (hidden_grad * up * s * (1.0 + gate * (1.0 - s))).astype(BF16)
    up_back = (hidden_grad * (gate * s)).astype(BF16)
    return jnp.stack([gate_back, up_back])


def body(
    queries, key_proj, value_matrix_rows, attn_grad, moe_input, moe_grad,
    expert_ids, route_weights, gate_proj, up_proj, down_proj,
):
    ctx_count = lax.axis_size("ctx")
    exp_count = lax.axis_size("exp")
    ctx_index = lax.axis_index("ctx")
    exp_index = lax.axis_index("exp")
    tokens = queries.shape[0]
    d = HEAD_SIZE
    kv_heads = key_proj.shape[1] // d
    sharers = ctx_count // kv_heads
    kv_head = ctx_index // sharers
    width = moe_input.shape[1]
    local = gate_proj.shape[0]
    expert_total = local * exp_count
    slot_count = 2 * ((tokens + expert_total - 2) // (expert_total - 1))
    slots = Slots(slot_count, width, exp_count, local)
    core = ctx_index % 2
    mine = core.astype(jnp.int32).reshape(1)
    other = 1 - mine
    order = jnp.concatenate([mine, other])
    shape = (exp_count, local, slots.rows, slots.columns)

    def exchange(rows):
        flat = rows.reshape(exp_count, local * slots.rows, slots.columns)
        return lax.all_to_all(flat, "exp", split_axis=0, concat_axis=0, tiled=True)

    me = exp_index.astype(jnp.int32).reshape(1)
    ids = expert_ids.T
    gains = route_weights.T
    send_rows = dispatch(slots, False, ids, gains, moe_input)
    recv_rows = exchange(send_rows).reshape(shape)
    send_scaled = dispatch(slots, True, ids, gains, after(moe_grad, send_rows))

    key_proj = after(key_proj, send_scaled)
    own = jnp.concatenate(
        [
            lax.dynamic_slice_in_dim(key_proj, kv_head * d, d, 1),
            lax.dynamic_slice_in_dim(value_matrix_rows, kv_head * d, d, 1),
        ],
        axis=1,
    )
    offsets = list(range(0, exp_count, 2)) + list(range(1, exp_count, 2))
    gathered = [swap(own, "exp", offset) for offset in offsets[1 : exp_count // 2]]
    gate_held, up_held, down_proj = hold(after(gate_proj, own), up_proj, down_proj)
    kv = jnp.concatenate([own, *gathered], axis=0)
    kv_far = swap(kv, "exp", 1)

    def heads(part, carried, earlier):
        return attention(
            me, tuple(offsets), after(queries, earlier), attn_grad, kv, kv_far, part, 1, carried
        )

    recv_rows = after(recv_rows, down_proj)
    gu_send = gate_up(slots, other, recv_rows, gate_held, up_held)
    gu_recv = swap(gu_send, "ctx", 1)
    recv_rows = after(recv_rows, gu_send, kv)
    gu_part, gu_low = gate_up(slots, mine, recv_rows, gate_held, up_held, gu_recv)
    recv_scaled = exchange(after(send_scaled, gu_low)).reshape(shape)
    (gate_full, up_full), (attn_out, query_grad, kv_keep, kv_send) = spread_sum(
        gu_part, gu_low, ctx_count, lambda part: heads(0, None, part)
    )
    hidden = activate(gate_full, up_full)
    hidden_other = swap(hidden, "ctx", 1)
    hg_send = hidden_grad_part(slots, other, after(recv_scaled, hidden), down_proj)
    hg_recv = swap(hg_send, "ctx", 1)
    out_rows = route_out(slots, order, after(hidden, hg_send), hidden_other, down_proj)
    back_out = exchange(out_rows).reshape(slots.total, slots.columns)

    hg_part, hg_low = hidden_grad_part(
        slots, mine, after(recv_scaled, out_rows), down_proj, hg_recv
    )
    hg_full, _ = spread_sum(hg_part, hg_low, ctx_count, lambda part: (part,))
    kv_sum = kv_keep + swap(kv_send, "exp", 1).astype(F32)
    kv_low = kv_sum.astype(BF16)
    blocks = exp_count // 2
    kv_parts = [
        swap(kv_low[i * tokens : (i + 1) * tokens], "exp", offsets[i]) for i in range(1, blocks)
    ]
    back = gate_backward(hg_full, gate_full, up_full)
    back_other = swap(back, "ctx", 1)
    kv_total = kv_sum[:tokens]
    for part in kv_parts:
        kv_total = kv_total + part.astype(F32)
    kv_total = kv_total.astype(BF16)
    in_rows = route_in(slots, order, back, back_other, gate_proj, up_proj)
    back_in = exchange(after(in_rows, kv_total)).reshape(slots.total, slots.columns)

    moe_out = combine(slots, True, ids, gains, after(back_out, in_rows))
    input_grad = combine(slots, False, ids, gains, back_in)

    kv_every = lax.all_gather(after(kv_total, in_rows), "ctx", axis=0, tiled=False)
    if sharers > 1:
        kv_every = kv_every.astype(F32).reshape(kv_heads, sharers, tokens, 2 * d).sum(axis=1)
    kv_every = kv_every.astype(BF16)
    key_grad = jnp.concatenate([kv_every[h, :, :d] for h in range(kv_heads)], axis=1)
    value_grad = jnp.concatenate([kv_every[h, :, d:] for h in range(kv_heads)], axis=1)
    return (attn_out, query_grad, key_grad, value_grad, moe_out, input_grad)


def solution(mesh):
    placed = (
        P("exp", "ctx"),
        P("exp", None),
        P("exp", None),
        P("exp", "ctx"),
        P("exp", "ctx"),
        P("exp", "ctx"),
        P("exp", None),
        P("exp", None),
        P("exp", "ctx", None),
        P("exp", "ctx", None),
        P("exp", None, "ctx"),
    )
    return jax.shard_map(
        body,
        mesh=mesh,
        in_specs=placed,
        out_specs=(
            P("exp", "ctx"),
            P("exp", "ctx"),
            P("exp", None),
            P("exp", None),
            P("exp", "ctx"),
            P("exp", "ctx"),
        ),
        check_vma=False,
    )
```

time: 152 us -> 126 us (0.83)
  waiting for transfers between devices: 54 us -> 28.3 us
  Pallas kernels: 42.2 us -> 39 us
  starting transfers between devices: 31.9 us -> 34.2 us
  local copies, waits for them, and re-layouts: 10.2 us -> 12 us
    ppermute x12 -> x14, waiting for transfers between devices: 33.7 us -> 17.2 us  [swap(): return lax.ppermute(value, axis, [(i, i ^ bit) for i in range(count)])]
    all_to_all x4, waiting for transfers between devices: 20.3 us -> 11.2 us  [exchange(): return lax.all_to_all(flat, 'exp', split_axis=0, concat_axis=0, tiled=True)]
    pallas_call x1, Pallas kernels: 16.8 us -> 13.5 us  [attention(): pl.pallas_call(functools.partial(attention_kernel, offsets, tokens, chunk...]
    ppermute x12 -> x14, starting transfers between devices: 12.4 us -> 14.6 us  [swap(): return lax.ppermute(value, axis, [(i, i ^ bit) for i in range(count)])]
    unnamed x40 -> x34, local copies, waits for them, and re-layouts: 9.37 us -> 11.2 us
    pallas_call x6 -> x7, Pallas kernels: 18.3 us -> 17.2 us  [the longest x6 13.4 us: expert_call(): pl.pallas_call(kernel, in_specs=[pl.BlockSpec(memory_space=pltpu.SMEM)] +...]
  transfers between devices with their start and end apart: 16 -> 18, of which waited for: 7 -> 7; matrix products, arithmetic and copies ran while one was open for 4% -> 4% of each run, Pallas kernels for 26% -> 27%
where the time goes in v2:
time: 126 us; the launch traced here: 125 us
  Pallas kernels  39 us (31%)
  starting transfers between devices  34.2 us (27%)
  waiting for transfers between devices  28.3 us (22%)
  local copies, waits for them, and re-layouts  12 us (10%)
  blocking collectives  5.77 us (5%)
  other arithmetic  4.28 us (3%)
    all_to_all x4, starting transfers between devices, exchange(): return lax.all_to_all(flat, 'exp', split_axis=0, concat_axis=0, tiled=True)  19.6 us
    ppermute x14, waiting for transfers between devices, swap(): return lax.ppermute(value, axis, [(i, i ^ bit) for i in range(count)])  17.2 us
    ppermute x14, starting transfers between devices, swap(): return lax.ppermute(value, axis, [(i, i ^ bit) for i in range(count)])  14.6 us
    pallas_call x1, Pallas kernels, attention(): pl.pallas_call(functools.partial(attention_kernel, offsets, tokens, chunk...  13.5 us
    pallas_call x6, Pallas kernels, expert_call(): pl.pallas_call(kernel, in_specs=[pl.BlockSpec(memory_space=pltpu.SMEM)] +...  13.4 us
    unnamed x34, local copies, waits for them, and re-layouts  11.2 us
    all_to_all x4, waiting for transfers between devices, exchange(): return lax.all_to_all(flat, 'exp', split_axis=0, concat_axis=0, tiled=True)  11.2 us
    all_gather x1, blocking collectives, body(): lax.all_gather(after(kv_total, in_rows), 'ctx', axis=0, tiled=False)  5.77 us
  transfers between devices with their start and end apart: 18, of which 7 were waited for; matrix products, arithmetic and copies ran while one was open for 4% of the time, Pallas kernels for 27%

profile of v2, /device:TPU:0, one launch (start us, length us, event | category | flops | bytes accessed | tf_op | source)
XLA Modules:
  0.0 124.6 jit_solution(11424594544267787538)
XLA Ops:
  0.6 2.4 %dispatch_rows.1 = bf16[256,1152]{1,0:T(8,128)(2,1)} custom-call(s32[2,128]{1,0:T(2,128)} %bitcast.56, f32[2,128]{1,0:T(2,128)} %bitcast.60, bf16[128,1024]{1,0:T(8,128)(2,1)} %rows_ref.1), custom_call_target="tpu_custom_call" | custom-call | flops 134217728 | bytes 1179648 | tf_op jit(solution)/shard_map/dispatch_rows/pallas_call | solution.py:129
  3.1 7.2 %all-to-all-start = ((bf16[8,32,1152]{2,1,0:T(8,128)(2,1)}), bf16[8,32,1152]{2,1,0:T(8,128)(2,1)}, u32[]{:S(2)}, u32[]{:S(2)}) async-start(bf16[8,32,1152]{2,1,0:T(8,128)(2,1)} %bitcast.4), calls=%async_computation | async-start | bytes 1179648 | tf_op jit(solution)/shard_map/all_to_all | solution.py:555
  10.3 1.7 %dispatch_scaled.1 = bf16[256,1152]{1,0:T(8,128)(2,1)S(1)} custom-call(s32[2,128]{1,0:T(2,128)} %bitcast.57, f32[2,128]{1,0:T(2,128)} %bitcast.61, bf16[128,1024]{1,0:T(8,128)(2,1)} %rows_ref.2), custom_call_target="tpu_custom_call" | custom-call | flops 134217728 | bytes 1179648 | tf_op jit(solution)/shard_map/dispatch_scaled/pallas_call | solution.py:129
  13.6 3.8 %hold_weights.1 = (bf16[2,1024,768]{2,1,0:T(8,128)(2,1)S(1)}, bf16[2,1024,768]{2,1,0:T(8,128)(2,1)S(1)}, bf16[2,768,1024]{2,1,0:T(8,128)(2,1)S(1)}) custom-call(bf16[2,1024,768]{2,1,0:T(8,128)(2,1)} %gate_ref.1, bf16[2,1024,768]{2,1,0:T(8,128)(2,1)} %up_ref.1, bf16[2,768,1024]{2,1,0:T(8,128)(2,1)} %refs_2_.1), custom_call_target="tpu_custom_call" | custom-call | bytes 18874368 | tf_op jit(solution)/shard_map/hold_weights/pallas_call | solution.py:233
  17.4 1.6 %copy-done.2 = bf16[2,1024,768]{2,1,0:T(8,128)(2,1)} copy-done((bf16[2,1024,768]{2,1,0:T(8,128)(2,1)}, bf16[2,1024,768]{2,1,0:T(8,128)(2,1)S(1)}, u32[]{:S(2)}) %copy-start.2) | copy-done | bytes 3145752
  19.0 1.7 %copy-done.4 = bf16[2,1024,768]{2,1,0:T(8,128)(2,1)} copy-done((bf16[2,1024,768]{2,1,0:T(8,128)(2,1)}, bf16[2,1024,768]{2,1,0:T(8,128)(2,1)S(1)}, u32[]{:S(2)}) %copy-start.4) | copy-done | bytes 3145752
  20.7 5.6 %all-to-all-done = bf16[8,32,1152]{2,1,0:T(8,128)(2,1)} async-done(((bf16[8,32,1152]{2,1,0:T(8,128)(2,1)}), bf16[8,32,1152]{2,1,0:T(8,128)(2,1)}, u32[]{:S(2)}, u32[]{:S(2)}) %all-to-all-start) | async-done | bytes 589856 | tf_op jit(solution)/shard_map/all_to_all | solution.py:555
  26.3 1.9 %copy-done.3 = bf16[2,1024,768]{2,1,0:T(8,128)(2,1)S(1)} copy-done((bf16[2,1024,768]{2,1,0:T(8,128)(2,1)S(1)}, bf16[2,1024,768]{2,1,0:T(8,128)(2,1)}, u32[]{:S(2)}) %copy-start.3) | copy-done | bytes 3145752
  28.2 1.9 %copy-done.5 = bf16[2,1024,768]{2,1,0:T(8,128)(2,1)S(1)} copy-done((bf16[2,1024,768]{2,1,0:T(8,128)(2,1)S(1)}, bf16[2,1024,768]{2,1,0:T(8,128)(2,1)}, u32[]{:S(2)}) %copy-start.5) | copy-done | bytes 3145752
  30.1 1.8 %gate_up.2 = bf16[2,144,768]{2,1,0:T(8,128)(2,1)S(1)} custom-call(s32[1]{0:T(128)S(6)} %sub.8.expert_ref, bf16[8,2,16,1152]{3,2,1,0:T(8,128)(2,1)} %bitcast.5.recv_ref, bf16[2,1024,768]{2,1,0:T(8,128)(2,1)S(1)} %copy-done.3, bf16[2,1024,768]{2,1,0:T(8,128)(2,1)S(1)} %copy-done.5), custom_call_target="tpu_custom_call" | custom-call | tf_op jit(solution)/shard_map/gate_up/pallas_call | solution.py:247
  33.8 2.6 %collective-permute-start.2 = (bf16[128,256]{1,0:T(8,128)(2,1)S(1)}, bf16[128,256]{1,0:T(8,128)(2,1)S(1)}, u32[]{:S(2)}, u32[]{:S(2)}) collective-permute-start(bf16[128,256]{1,0:T(8,128)(2,1)S(1)} %pad_maximum_fusion.4), channel_id=1, source_target_pairs={{0,6},{1,7},{2,4},{3,5},{4,2},{5,3},{6,0},{7,1},{8,14},{9,15},{10,... | collective-permute-start | bytes 196616 | tf_op jit(solution)/shard_map/ppermute | solution.py:488
  37.2 4.1 %collective-permute-done.1 = bf16[128,256]{1,0:T(8,128)(2,1)S(1)} collective-permute-done((bf16[128,256]{1,0:T(8,128)(2,1)S(1)}, bf16[128,256]{1,0:T(8,128)(2,1)S(1)}, u32[]{:S(2)}, u32[]{:S(2)}) %collective-permute-start.1) | collective-permute-done | bytes 65568 | tf_op jit(solution)/shard_map/ppermute | solution.py:488
  42.3 1.8 %gate_up.3 = (f32[2,144,768]{2,1,0:T(8,128)S(1)}, bf16[2,144,768]{2,1,0:T(8,128)(2,1)S(1)}) custom-call(s32[1]{0:T(128)} %bitcast.1.expert_ref, bf16[8,2,16,1152]{3,2,1,0:T(8,128)(2,1)} %bitcast.5.recv_ref, bf16[2,1024,768]{2,1,0:T(8,128)(2,1)S(1)} %copy-done.3, bf16[2,1024,768]{2,1,0:T(8,128)(2,1)S(1)} %copy-done.5, ...), custom_call_target="tpu_custom_call" | custom-call | tf_op jit(solution)/shard_map/gate_up/pallas_call | solution.py:247
  45.7 4.2 %all-to-all-start.1 = ((bf16[8,32,1152]{2,1,0:T(8,128)(2,1)}), bf16[8,32,1152]{2,1,0:T(8,128)(2,1)}, u32[]{:S(2)}, u32[]{:S(2)}) async-start(bf16[8,32,1152]{2,1,0:T(8,128)(2,1)} %bitcast.54), calls=%async_computation.1 | async-start | bytes 1179648 | tf_op jit(solution)/shard_map/all_to_all | solution.py:555
  49.9 1.6 %collective-permute-start.9 = (bf16[2,144,768]{2,1,0:T(8,128)(2,1)}, bf16[2,144,768]{2,1,0:T(8,128)(2,1)}, u32[]{:S(2)}, u32[]{:S(2)}) collective-permute-start(bf16[2,144,768]{2,1,0:T(8,128)(2,1)} %copy-done.14), channel_id=1, source_target_pairs={{0,16},{8,24},{16,0},{24,8},{1,17},{9,25},{17,1},{25,9},{2,18},{10... | collective-permute-start | bytes 1327112 | tf_op jit(solution)/shard_map/ppermute | solution.py:488
  51.5 13.5 %attention.1 = (bf16[128,2048]{1,0:T(8,128)(2,1)}, bf16[128,2048]{1,0:T(8,128)(2,1)}, f32[512,256]{1,0:T(8,128)S(1)}, bf16[512,256]{1,0:T(8,128)(2,1)}) custom-call(s32[1]{0:T(128)} %bitcast.me_ref, bf16[128,2048]{1,0:T(8,128)(2,1)} %q_ref, bf16[128,2048]{1,0:T(8,128)(2,1)} %g_ref.1, bf16[512,256]{1,0:T(8,128)(2,1)S(1)} %pad_maximum_fusion.1.kv_ref, ...), custom_call_target="tpu_custom_call" | custom-call | flops 3221225472 | bytes 2097152 | tf_op jit(solution)/shard_map/attention/pallas_call | solution.py:458
  65.1 1.9 %collective-permute-start.5 = (bf16[512,256]{1,0:T(8,128)(2,1)}, bf16[512,256]{1,0:T(8,128)(2,1)}, u32[]{:S(2)}, u32[]{:S(2)}) collective-permute-start(bf16[512,256]{1,0:T(8,128)(2,1)} %get-tuple-element.45), channel_id=1, source_target_pairs={{0,1},{1,0},{2,3},{3,2},{4,5},{5,4},{6,7},{7,6},{8,9},{9,8},{10,11... | collective-permute-start | bytes 786440 | tf_op jit(solution)/shard_map/ppermute | solution.py:488
  69.0 2.4 %hidden_grad.2 = bf16[144,768]{1,0:T(8,128)(2,1)} custom-call(s32[1]{0:T(128)S(6)} %sub.8.expert_ref, bf16[8,2,16,1152]{3,2,1,0:T(8,128)(2,1)} %bitcast.7.recv_ref, bf16[2,768,1024]{2,1,0:T(8,128)(2,1)S(1)} %get-tuple-element.35.down_ref), custom_call_target="tpu_custom_call" | custom-call | tf_op jit(solution)/shard_map/hidden_grad/pallas_call | solution.py:247
  72.0 1.9 %route_out.1 = bf16[8,2,16,1152]{3,2,1,0:T(8,128)(2,1)S(1)} custom-call(s32[2]{0:T(128)S(1)} %pad_add_fusion.order_ref, bf16[144,768]{1,0:T(8,128)(2,1)S(1)} %multiply_convert_fusion.2.mine_ref, bf16[144,768]{1,0:T(8,128)(2,1)} %collective-permute-done.10.other_ref, bf16[2,768,1024]{2,1,0:T(8,128)(2,1)S(1)} %get-tuple-element.35.down_ref), custom_call_target="tpu_custom_call" | custom-call | tf_op jit(solution)/shard_map/route_out/pallas_call | solution.py:247
  74.7 4.6 %all-to-all-start.2 = ((bf16[8,32,1152]{2,1,0:T(8,128)(2,1)}), bf16[8,32,1152]{2,1,0:T(8,128)(2,1)}, u32[]{:S(2)}, u32[]{:S(2)}) async-start(bf16[8,32,1152]{2,1,0:T(8,128)(2,1)} %bitcast.53), calls=%async_computation.2 | async-start | bytes 1179648 | tf_op jit(solution)/shard_map/all_to_all | solution.py:555
  79.3 1.9 %hidden_grad.3 = (f32[144,768]{1,0:T(8,128)S(1)}, bf16[144,768]{1,0:T(8,128)(2,1)S(1)}) custom-call(s32[1]{0:T(128)} %bitcast.1.expert_ref, bf16[8,2,16,1152]{3,2,1,0:T(8,128)(2,1)} %bitcast.7.recv_ref, bf16[2,768,1024]{2,1,0:T(8,128)(2,1)S(1)} %get-tuple-element.35.down_ref, bf16[144,768]{1,0:T(8,128)(2,1)} %collective-permute-done.11.refs_0_), custom_call_target="tpu_custom_call" | custom-call | tf_op jit(solution)/shard_map/hidden_grad/pallas_call | solution.py:247
  81.8 1.3 %fusion.6 = (bf16[512,256]{1,0:T(8,128)(2,1)S(1)}, f32[512,256]{1,0:T(8,128)S(1)}) fusion(f32[512,256]{1,0:T(8,128)S(1)} %copy-done.11, bf16[512,256]{1,0:T(8,128)(2,1)} %collective-permute-done.5), kind=kLoop, calls=%fused_computation.32 | loop fusion | flops 393216 | bytes 1572864 | tf_op jit(solution)/shard_map/convert_element_type | solution.py:604
  83.1 5.3 %collective-permute-done.12 = bf16[144,768]{1,0:T(8,128)(2,1)S(1)} collective-permute-done((bf16[144,768]{1,0:T(8,128)(2,1)S(1)}, bf16[144,768]{1,0:T(8,128)(2,1)S(1)}, u32[]{:S(2)}, u32[]{:S(2)}) %collective-permute-start.12) | collective-permute-done | bytes 221216 | tf_op jit(solution)/shard_map/ppermute | solution.py:488
  88.8 1.8 %collective-permute-start.6 = (bf16[128,256]{1,0:T(8,128)(2,1)S(1)}, bf16[128,256]{1,0:T(8,128)(2,1)S(1)}, u32[]{:S(2)}, u32[]{:S(2)}) collective-permute-start(bf16[128,256]{1,0:T(8,128)(2,1)S(1)} %get-tuple-element.70), channel_id=1, source_target_pairs={{0,2},{1,3},{2,0},{3,1},{4,6},{5,7},{6,4},{7,5},{8,10},{9,11},{10,... | collective-permute-start | bytes 196616 | tf_op jit(solution)/shard_map/ppermute | solution.py:488
  90.6 2.4 %collective-permute-start.7 = (bf16[128,256]{1,0:T(8,128)(2,1)S(1)}, bf16[128,256]{1,0:T(8,128)(2,1)S(1)}, u32[]{:S(2)}, u32[]{:S(2)}) collective-permute-start(bf16[128,256]{1,0:T(8,128)(2,1)S(1)} %get-tuple-element.72), channel_id=1, source_target_pairs={{0,4},{1,5},{2,6},{3,7},{4,0},{5,1},{6,2},{7,3},{8,12},{9,13},{10,... | collective-permute-start | bytes 196616 | tf_op jit(solution)/shard_map/ppermute | solution.py:488
  93.5 6.7 %collective-permute-done.7 = bf16[128,256]{1,0:T(8,128)(2,1)S(1)} collective-permute-done((bf16[128,256]{1,0:T(8,128)(2,1)S(1)}, bf16[128,256]{1,0:T(8,128)(2,1)S(1)}, u32[]{:S(2)}, u32[]{:S(2)}) %collective-permute-start.7) | collective-permute-done | bytes 65568 | tf_op jit(solution)/shard_map/ppermute | solution.py:488
  100.3 3.7 %route_in.1 = bf16[8,2,16,1152]{3,2,1,0:T(8,128)(2,1)} custom-call(s32[2]{0:T(128)S(1)} %pad_add_fusion.order_ref, bf16[2,144,768]{2,1,0:T(8,128)(2,1)S(1)} %pad_maximum_fusion.mine_ref, bf16[2,144,768]{2,1,0:T(8,128)(2,1)S(1)} %collective-permute-done.13.other_ref, bf16[2,1024,768]{2,1,0:T(8,128)(2,1)S(1)} %copy-done, bf16[2,1024,768]{2,1,0:T(8,128)(2,1)S(1)} %copy-done.1), custom_call_target="tpu_custom_call" | custom-call | tf_op jit(solution)/shard_map/route_in/pallas_call | solution.py:247
  104.0 3.6 %all-to-all-start.3 = ((bf16[8,32,1152]{2,1,0:T(8,128)(2,1)}), bf16[8,32,1152]{2,1,0:T(8,128)(2,1)S(1)}, u32[]{:S(2)}, u32[]{:S(2)}) async-start(bf16[8,32,1152]{2,1,0:T(8,128)(2,1)} %bitcast.23), calls=%async_computation.3 | async-start | bytes 1179648 | tf_op jit(solution)/shard_map/all_to_all | solution.py:555
  107.6 5.8 %all-gather = bf16[512,256]{1,0:T(8,128)(2,1)S(1)} all-gather(bf16[128,256]{1,0:T(8,128)(2,1)S(1)} %fusion.5), channel_id=2, replica_groups=mesh['ctx'=4,'exp'=8] {'ctx'}, dimensions={0}, use_global_device_ids=true | all-gather | bytes 327680 | tf_op jit(solution)/shard_map/all_gather | solution.py:621
  114.8 2.7 %combine_out.1 = bf16[128,1024]{1,0:T(8,128)(2,1)} custom-call(s32[2,128]{1,0:T(2,128)S(1)} %bitcast.58, f32[2,128]{1,0:T(2,128)S(1)} %bitcast.62, bf16[256,1152]{1,0:T(8,128)(2,1)} %bitcast.22.back_ref), custom_call_target="tpu_custom_call" | custom-call | flops 268435456 | bytes 1179648 | tf_op jit(solution)/shard_map/combine_out/pallas_call | solution.py:173
  117.5 5.6 %all-to-all-done.3 = bf16[8,32,1152]{2,1,0:T(8,128)(2,1)S(1)} async-done(((bf16[8,32,1152]{2,1,0:T(8,128)(2,1)}), bf16[8,32,1152]{2,1,0:T(8,128)(2,1)S(1)}, u32[]{:S(2)}, u32[]{:S(2)}) %all-to-all-start.3) | async-done | bytes 589856 | tf_op jit(solution)/shard_map/all_to_all | solution.py:555
  123.1 1.5 %combine_in.1 = bf16[128,1024]{1,0:T(8,128)(2,1)} custom-call(s32[2,128]{1,0:T(2,128)S(1)} %bitcast.59, f32[2,128]{1,0:T(2,128)S(1)} %bitcast.63, bf16[256,1152]{1,0:T(8,128)(2,1)S(1)} %bitcast.55), custom_call_target="tpu_custom_call" | custom-call | flops 268435456 | bytes 1179648 | tf_op jit(solution)/shard_map/combine_in/pallas_call | solution.py:173
  (65 shorter events, 13.4 us)
Async XLA Ops:
  3.1 23.2 %all-to-all-start = ((bf16[8,32,1152]{2,1,0:T(8,128)(2,1)}), bf16[8,32,1152]{2,1,0:T(8,128)(2,1)}, u32[]{:S(2)}, u32[]{:S(2)}) async-start(bf16[8,32,1152]{2,1,0:T(8,128)(2,1)} %bitcast.4), calls=%async_computation | async-start | bytes 1179648 | tf_op jit(solution)/shard_map/all_to_all | solution.py:555
  17.4 1.6 %copy-start.2 = (bf16[2,1024,768]{2,1,0:T(8,128)(2,1)}, bf16[2,1024,768]{2,1,0:T(8,128)(2,1)S(1)}, u32[]{:S(2)}) copy-start(bf16[2,1024,768]{2,1,0:T(8,128)(2,1)S(1)} %get-tuple-element.37.gate_ref) | copy-start | bytes 9437188
  19.0 1.7 %copy-start.4 = (bf16[2,1024,768]{2,1,0:T(8,128)(2,1)}, bf16[2,1024,768]{2,1,0:T(8,128)(2,1)S(1)}, u32[]{:S(2)}) copy-start(bf16[2,1024,768]{2,1,0:T(8,128)(2,1)S(1)} %get-tuple-element.38.up_ref) | copy-start | bytes 9437188
  26.3 1.9 %copy-start.3 = (bf16[2,1024,768]{2,1,0:T(8,128)(2,1)S(1)}, bf16[2,1024,768]{2,1,0:T(8,128)(2,1)}, u32[]{:S(2)}) copy-start(bf16[2,1024,768]{2,1,0:T(8,128)(2,1)} %copy-done.2) | copy-start | bytes 9437188
  28.2 1.9 %copy-start.5 = (bf16[2,1024,768]{2,1,0:T(8,128)(2,1)S(1)}, bf16[2,1024,768]{2,1,0:T(8,128)(2,1)}, u32[]{:S(2)}) copy-start(bf16[2,1024,768]{2,1,0:T(8,128)(2,1)} %copy-done.4) | copy-start | bytes 9437188
  31.9 10.4 %collective-permute-start.3 = (bf16[2,144,768]{2,1,0:T(8,128)(2,1)S(1)}, bf16[2,144,768]{2,1,0:T(8,128)(2,1)S(1)}, u32[]{:S(2)}, u32[]{:S(2)}) collective-permute-start(bf16[2,144,768]{2,1,0:T(8,128)(2,1)S(1)} %gate_up.2), channel_id=1, source_target_pairs={{0,8},{8,0},{16,24},{24,16},{1,9},{9,1},{17,25},{25,17},{2,10},{10... | collective-permute-start | bytes 1327112 | tf_op jit(solution)/shard_map/ppermute | solution.py:488
  32.0 5.2 %collective-permute-start = (bf16[128,256]{1,0:T(8,128)(2,1)S(1)}, bf16[128,256]{1,0:T(8,128)(2,1)S(1)}, u32[]{:S(2)}, u32[]{:S(2)}) collective-permute-start(bf16[128,256]{1,0:T(8,128)(2,1)S(1)} %pad_maximum_fusion.4), channel_id=1, source_target_pairs={{0,2},{1,3},{2,0},{3,1},{4,6},{5,7},{6,4},{7,5},{8,10},{9,11},{10,... | collective-permute-start | bytes 196616 | tf_op jit(solution)/shard_map/ppermute | solution.py:488
  32.7 8.6 %collective-permute-start.1 = (bf16[128,256]{1,0:T(8,128)(2,1)S(1)}, bf16[128,256]{1,0:T(8,128)(2,1)S(1)}, u32[]{:S(2)}, u32[]{:S(2)}) collective-permute-start(bf16[128,256]{1,0:T(8,128)(2,1)S(1)} %pad_maximum_fusion.4), channel_id=1, source_target_pairs={{0,4},{1,5},{2,6},{3,7},{4,0},{5,1},{6,2},{7,3},{8,12},{9,13},{10,... | collective-permute-start | bytes 196616 | tf_op jit(solution)/shard_map/ppermute | solution.py:488
  33.8 7.5 %collective-permute-start.2 = (bf16[128,256]{1,0:T(8,128)(2,1)S(1)}, bf16[128,256]{1,0:T(8,128)(2,1)S(1)}, u32[]{:S(2)}, u32[]{:S(2)}) collective-permute-start(bf16[128,256]{1,0:T(8,128)(2,1)S(1)} %pad_maximum_fusion.4), channel_id=1, source_target_pairs={{0,6},{1,7},{2,4},{3,5},{4,2},{5,3},{6,0},{7,1},{8,14},{9,15},{10,... | collective-permute-start | bytes 196616 | tf_op jit(solution)/shard_map/ppermute | solution.py:488
  41.3 10.2 %collective-permute-start.4 = (bf16[512,256]{1,0:T(8,128)(2,1)S(1)}, bf16[512,256]{1,0:T(8,128)(2,1)}, u32[]{:S(2)}, u32[]{:S(2)}) collective-permute-start(bf16[512,256]{1,0:T(8,128)(2,1)S(1)} %pad_maximum_fusion.1.kv_ref), channel_id=1, source_target_pairs={{0,1},{1,0},{2,3},{3,2},{4,5},{5,4},{6,7},{7,6},{8,9},{9,8},{10,11... | collective-permute-start | bytes 786440 | tf_op jit(solution)/shard_map/ppermute | solution.py:488
  44.1 0.9 copy-start.8
  45.7 23.2 %all-to-all-start.1 = ((bf16[8,32,1152]{2,1,0:T(8,128)(2,1)}), bf16[8,32,1152]{2,1,0:T(8,128)(2,1)}, u32[]{:S(2)}, u32[]{:S(2)}) async-start(bf16[8,32,1152]{2,1,0:T(8,128)(2,1)} %bitcast.54), calls=%async_computation.1 | async-start | bytes 1179648 | tf_op jit(solution)/shard_map/all_to_all | solution.py:555
  49.9 17.0 %collective-permute-start.9 = (bf16[2,144,768]{2,1,0:T(8,128)(2,1)}, bf16[2,144,768]{2,1,0:T(8,128)(2,1)}, u32[]{:S(2)}, u32[]{:S(2)}) collective-permute-start(bf16[2,144,768]{2,1,0:T(8,128)(2,1)} %copy-done.14), channel_id=1, source_target_pairs={{0,16},{8,24},{16,0},{24,8},{1,17},{9,25},{17,1},{25,9},{2,18},{10... | collective-permute-start | bytes 1327112 | tf_op jit(solution)/shard_map/ppermute | solution.py:488
  51.5 15.4 %copy-start.9 = (f32[2,144,768]{2,1,0:T(8,128)S(1)}, f32[2,144,768]{2,1,0:T(8,128)}, u32[]{:S(2)}) copy-start(f32[2,144,768]{2,1,0:T(8,128)} %copy-done.8) | copy-start | bytes 2654212
  65.0 3.0 %copy-start.10 = (f32[512,256]{1,0:T(8,128)}, f32[512,256]{1,0:T(8,128)S(1)}, u32[]{:S(2)}) copy-start(f32[512,256]{1,0:T(8,128)S(1)} %get-tuple-element.44) | copy-start | bytes 1572868
  65.1 16.7 %collective-permute-start.5 = (bf16[512,256]{1,0:T(8,128)(2,1)}, bf16[512,256]{1,0:T(8,128)(2,1)}, u32[]{:S(2)}, u32[]{:S(2)}) collective-permute-start(bf16[512,256]{1,0:T(8,128)(2,1)} %get-tuple-element.45), channel_id=1, source_target_pairs={{0,1},{1,0},{2,3},{3,2},{4,5},{5,4},{6,7},{7,6},{8,9},{9,8},{10,11... | collective-permute-start | bytes 786440 | tf_op jit(solution)/shard_map/ppermute | solution.py:488
  68.1 0.9 copy-start.15
  69.0 3.0 %collective-permute-start.10 = (bf16[144,768]{1,0:T(8,128)(2,1)S(1)}, bf16[144,768]{1,0:T(8,128)(2,1)}, u32[]{:S(2)}, u32[]{:S(2)}) collective-permute-start(bf16[144,768]{1,0:T(8,128)(2,1)S(1)} %multiply_convert_fusion.2.mine_ref), channel_id=1, source_target_pairs={{0,8},{8,0},{16,24},{24,16},{1,9},{9,1},{17,25},{25,17},{2,10},{10... | collective-permute-start | bytes 663560 | tf_op jit(solution)/shard_map/ppermute | solution.py:488
  71.4 7.9 %collective-permute-start.11 = (bf16[144,768]{1,0:T(8,128)(2,1)}, bf16[144,768]{1,0:T(8,128)(2,1)}, u32[]{:S(2)}, u32[]{:S(2)}) collective-permute-start(bf16[144,768]{1,0:T(8,128)(2,1)} %hidden_grad.2), channel_id=1, source_target_pairs={{0,8},{8,0},{16,24},{24,16},{1,9},{9,1},{17,25},{25,17},{2,10},{10... | collective-permute-start | bytes 663560 | tf_op jit(solution)/shard_map/ppermute | solution.py:488
  74.7 29.3 %all-to-all-start.2 = ((bf16[8,32,1152]{2,1,0:T(8,128)(2,1)}), bf16[8,32,1152]{2,1,0:T(8,128)(2,1)}, u32[]{:S(2)}, u32[]{:S(2)}) async-start(bf16[8,32,1152]{2,1,0:T(8,128)(2,1)} %bitcast.53), calls=%async_computation.2 | async-start | bytes 1179648 | tf_op jit(solution)/shard_map/all_to_all | solution.py:555
  79.3 2.5 %copy-start.11 = (f32[512,256]{1,0:T(8,128)S(1)}, f32[512,256]{1,0:T(8,128)}, u32[]{:S(2)}) copy-start(f32[512,256]{1,0:T(8,128)} %copy-done.10) | copy-start | bytes 1572868
  79.3 9.1 %copy-start.16 = (f32[2,144,768]{2,1,0:T(8,128)S(1)}, f32[2,144,768]{2,1,0:T(8,128)}, u32[]{:S(2)}) copy-start(f32[2,144,768]{2,1,0:T(8,128)} %copy-done.15) | copy-start | bytes 2654212
  79.3 21.0 %copy-start.1 = (bf16[2,1024,768]{2,1,0:T(8,128)(2,1)S(1)}, bf16[2,1024,768]{2,1,0:T(8,128)(2,1)}, u32[]{:S(2)}) copy-start(bf16[2,1024,768]{2,1,0:T(8,128)(2,1)} %up_ref.1) | copy-start | bytes 9437188
  81.2 19.1 %copy-start = (bf16[2,1024,768]{2,1,0:T(8,128)(2,1)S(1)}, bf16[2,1024,768]{2,1,0:T(8,128)(2,1)}, u32[]{:S(2)}) copy-start(bf16[2,1024,768]{2,1,0:T(8,128)(2,1)} %gate_ref.1) | copy-start | bytes 9437188
  81.2 7.1 %collective-permute-start.12 = (bf16[144,768]{1,0:T(8,128)(2,1)S(1)}, bf16[144,768]{1,0:T(8,128)(2,1)S(1)}, u32[]{:S(2)}, u32[]{:S(2)}) collective-permute-start(bf16[144,768]{1,0:T(8,128)(2,1)S(1)} %get-tuple-element.53), channel_id=1, source_target_pairs={{0,16},{8,24},{16,0},{24,8},{1,17},{9,25},{17,1},{25,9},{2,18},{10... | collective-permute-start | bytes 663560 | tf_op jit(solution)/shard_map/ppermute | solution.py:488
  88.7 11.6 %collective-permute-start.13 = (bf16[2,144,768]{2,1,0:T(8,128)(2,1)S(1)}, bf16[2,144,768]{2,1,0:T(8,128)(2,1)S(1)}, u32[]{:S(2)}, u32[]{:S(2)}) collective-permute-start(bf16[2,144,768]{2,1,0:T(8,128)(2,1)S(1)} %pad_maximum_fusion.mine_ref), channel_id=1, source_target_pairs={{0,8},{8,0},{16,24},{24,16},{1,9},{9,1},{17,25},{25,17},{2,10},{10... | collective-permute-start | bytes 1327112 | tf_op jit(solution)/shard_map/ppermute | solution.py:488
  88.8 4.7 %collective-permute-start.6 = (bf16[128,256]{1,0:T(8,128)(2,1)S(1)}, bf16[128,256]{1,0:T(8,128)(2,1)S(1)}, u32[]{:S(2)}, u32[]{:S(2)}) collective-permute-start(bf16[128,256]{1,0:T(8,128)(2,1)S(1)} %get-tuple-element.70), channel_id=1, source_target_pairs={{0,2},{1,3},{2,0},{3,1},{4,6},{5,7},{6,4},{7,5},{8,10},{9,11},{10,... | collective-permute-start | bytes 196616 | tf_op jit(solution)/shard_map/ppermute | solution.py:488
  90.6 9.7 %collective-permute-start.7 = (bf16[128,256]{1,0:T(8,128)(2,1)S(1)}, bf16[128,256]{1,0:T(8,128)(2,1)S(1)}, u32[]{:S(2)}, u32[]{:S(2)}) collective-permute-start(bf16[128,256]{1,0:T(8,128)(2,1)S(1)} %get-tuple-element.72), channel_id=1, source_target_pairs={{0,4},{1,5},{2,6},{3,7},{4,0},{5,1},{6,2},{7,3},{8,12},{9,13},{10,... | collective-permute-start | bytes 196616 | tf_op jit(solution)/shard_map/ppermute | solution.py:488
  92.9 7.3 %collective-permute-start.8 = (bf16[128,256]{1,0:T(8,128)(2,1)S(1)}, bf16[128,256]{1,0:T(8,128)(2,1)S(1)}, u32[]{:S(2)}, u32[]{:S(2)}) collective-permute-start(bf16[128,256]{1,0:T(8,128)(2,1)S(1)} %get-tuple-element.71), channel_id=1, source_target_pairs={{0,6},{1,7},{2,4},{3,5},{4,2},{5,3},{6,0},{7,1},{8,14},{9,15},{10,... | collective-permute-start | bytes 196616 | tf_op jit(solution)/shard_map/ppermute | solution.py:488
  100.3 14.5 %copy-start.12 = (s32[128,2]{0,1:T(2,128)S(1)}, s32[128,2]{0,1:T(2,128)}, u32[]{:S(2)}) copy-start(s32[128,2]{0,1:T(2,128)} %param.17) | copy-start | bytes 3076
  100.3 14.5 %copy-start.13 = (f32[128,2]{0,1:T(2,128)S(1)}, f32[128,2]{0,1:T(2,128)}, u32[]{:S(2)}) copy-start(f32[128,2]{0,1:T(2,128)} %param.18) | copy-start | bytes 3076
  104.0 19.1 %all-to-all-start.3 = ((bf16[8,32,1152]{2,1,0:T(8,128)(2,1)}), bf16[8,32,1152]{2,1,0:T(8,128)(2,1)S(1)}, u32[]{:S(2)}, u32[]{:S(2)}) async-start(bf16[8,32,1152]{2,1,0:T(8,128)(2,1)} %bitcast.23), calls=%async_computation.3 | async-start | bytes 1179648 | tf_op jit(solution)/shard_map/all_to_all | solution.py:555
  (3 other events, 2.4 us)

commit v3 on v2

--- a/solution.py
+++ b/solution.py
@@ -11,7 +11,8 @@
 HEAD_SIZE = 128
 LANES = 128
 ROW_TILE = 16
-PAIRS = 2
+PAIRS = 4
+CHUNK = 512
 SMALL_VMEM = 16 * 1024 * 1024
 LARGE_VMEM = 20 * 1024 * 1024
 EXPERT_VMEM = 16 * 1024 * 1024
@@ -218,109 +219,203 @@
         out_ref[:, :, slots.width :] = folded.reshape(slots.exp_count, slots.rows, LANES)
 
 
-def hold_kernel(*refs):
-    count = len(refs) // 2
+def fetch(sources, targets, sems):
     copies = [
-        pltpu.make_async_copy(refs[i], refs[count + i], refs[-1].at[i]) for i in range(count)
+        pltpu.make_async_copy(source, target, sems.at[i])
+        for i, (source, target) in enumerate(zip(sources, targets))
     ]
     for copy in copies:
         copy.start()
-    for copy in copies:
+    return copies
+
+
+def hold_kernel(expert_ref, gate_ref, up_ref, out_ref, sems):
+    e = expert_ref[0]
+    for copy in fetch([gate_ref.at[e], up_ref.at[e]], [out_ref.at[0], out_ref.at[1]], sems):
         copy.wait()
 
 
-def hold(*weights):
+def hold(expert, gate_proj, up_proj):
+    return expert_call(
+        hold_kernel, "hold_weights", pltpu.VMEM((2, *gate_proj.shape[1:]), BF16), expert,
+        in_hbm(gate_proj), in_hbm(up_proj), anywhere=(0, 1), copies=2,
+    )
+
+
+def expert_call(kernel, name, out_shape, scalars, *operands, anywhere=(), copies=0, held=None):
+    in_vmem = pl.BlockSpec(memory_space=pltpu.VMEM)
+    specs = [
+        pl.BlockSpec(memory_space=pl.ANY) if i in anywhere else in_vmem
+        for i in range(len(operands))
+    ]
+    if scalars is not None:
+        specs = [pl.BlockSpec(memory_space=pltpu.SMEM)] + specs
+        operands = (scalars, *operands)
+    scratch = [] if held is None else [pltpu.VMEM(held, BF16)]
+    if copies:
+        scratch.append(pltpu.SemaphoreType.DMA((copies,)))
     return pl.pallas_call(
-        hold_kernel,
-        in_specs=[pl.BlockSpec(memory_space=pl.ANY)] * len(weights),
-        out_specs=[pl.BlockSpec(memory_space=pltpu.VMEM)] * len(weights),
-        out_shape=[pltpu.VMEM(value.shape, value.dtype) for value in weights],
-        scratch_shapes=[pltpu.SemaphoreType.DMA((len(weights),))],
-        compiler_params=pltpu.CompilerParams(vmem_limit_bytes=SMALL_VMEM),
-        cost_estimate=cost(0, sum(value.size * 4 for value in weights)),
-        name="hold_weights",
-    )(*[in_hbm(value) for value in weights])
-
-
-def expert_call(kernel, name, out_shape, scalars, *operands):
+        kernel,
+        in_specs=specs,
+        out_specs=[in_vmem] * len(out_shape) if isinstance(out_shape, list) else in_vmem,
+        out_shape=out_shape,
+        scratch_shapes=scratch,
+        compiler_params=pltpu.CompilerParams(vmem_limit_bytes=EXPERT_VMEM),
+        name=name,
+    )(*operands)
+
+
+def gate_up_send_kernel(
+    slots, order_ref, recv_ref, held_ref, gate_ref, up_ref, out_ref, next_ref, rows_ref, all_ref, sems
+):
+    e, following = order_ref[0], order_ref[1]
+    copies = fetch(
+        [recv_ref, gate_ref.at[following], up_ref.at[following]],
+        [all_ref, next_ref.at[0], next_ref.at[1]],
+        sems,
+    )
+    copies[0].wait()
+    rows = unpack_rows(slots, all_ref[:, e])
+    out_ref[0] = dot(rows, held_ref[0]).astype(BF16)
+    out_ref[1] = dot(rows, held_ref[1]).astype(BF16)
+    rows_ref[...] = unpack_rows(slots, all_ref[:, following])
+    for copy in copies[1:]:
+        copy.wait()
+
+
+def gate_up_send(slots, order, recv, held, gate_proj, up_proj):
+    out = [
+        jax.ShapeDtypeStruct((2, slots.per_expert, gate_proj.shape[2]), BF16),
+        pltpu.VMEM(held.shape, BF16),
+        jax.ShapeDtypeStruct((slots.per_expert, slots.width), BF16),
+    ]
+    return expert_call(
+        functools.partial(gate_up_send_kernel, slots), "gate_up_send", out, order,
+        in_hbm(recv), held, in_hbm(gate_proj), in_hbm(up_proj),
+        anywhere=(0, 2, 3), copies=3, held=recv.shape,
+    )
+
+
+def gate_up_keep_kernel(rows_ref, held_ref, arrived_ref, out_ref):
+    for i in range(2):
+        part = dot(rows_ref[...], held_ref[i]) + arrived_ref[i].astype(F32)
+        out_ref[i] = part.astype(BF16)
+
+
+def gate_up_keep(rows, held, arrived):
+    out = jax.ShapeDtypeStruct(arrived.shape, BF16)
+    return expert_call(gate_up_keep_kernel, "gate_up_keep", out, None, rows, held, arrived)
+
+
+def hidden_grad_send_kernel(slots, order_ref, recv_ref, down_ref, out_ref, rows_ref):
+    rows = unpack_rows(slots, recv_ref[:, order_ref[0]])
+    out_ref[...] = dot(rows, down_ref[order_ref[0]], 1, 1).astype(BF16)
+    rows_ref[...] = unpack_rows(slots, recv_ref[:, order_ref[1]])
+
+
+def hidden_grad_send(slots, order, recv, down_proj):
+    out = [
+        jax.ShapeDtypeStruct((slots.per_expert, down_proj.shape[1]), BF16),
+        jax.ShapeDtypeStruct((slots.per_expert, slots.width), BF16),
+    ]
+    kernel = functools.partial(hidden_grad_send_kernel, slots)
+    return expert_call(kernel, "hidden_grad_send", out, order, recv, down_proj)
+
+
+def hidden_grad_keep_kernel(expert_ref, rows_ref, down_ref, arrived_ref, out_ref):
+    part = dot(rows_ref[...], down_ref[expert_ref[0]], 1, 1) + arrived_ref[...].astype(F32)
+    out_ref[...] = part.astype(BF16)
+
+
+def hidden_grad_keep(expert, rows, down_proj, arrived):
+    out = jax.ShapeDtypeStruct(arrived.shape, BF16)
+    return expert_call(
+        hidden_grad_keep_kernel, "hidden_grad_keep", out, expert, rows, down_proj, arrived
+    )
+
+
+def store_rows(slots, rows, expert, packed_ref, out_ref, sem):
+    pack_rows(slots, rows, packed_ref)
+    copy = pltpu.make_async_copy(packed_ref, out_ref.at[:, expert], sem)
+    copy.start()
+    return copy
+
+
+def packed_shape(slots):
+    return (slots.exp_count, slots.local, slots.rows, slots.columns)
+
+
+def packed_scratch(slots):
+    return pltpu.VMEM((slots.local, slots.exp_count, slots.rows, slots.columns), BF16)
+
+
+def route_out_kernel(slots, order_ref, mine_ref, other_ref, down_ref, out_ref, packed_ref, sems):
+    stores = []
+    for at, hidden_ref in enumerate((mine_ref, other_ref)):
+        e = order_ref[at]
+        rows = dot(hidden_ref[...], down_ref[e]).astype(BF16)
+        stores.append(store_rows(slots, rows, e, packed_ref.at[at], out_ref, sems.at[at]))
+    for store in stores:
+        store.wait()
+
+
+def route_out(slots, order, mine, other, down_proj):
     in_vmem = pl.BlockSpec(memory_space=pltpu.VMEM)
     return pl.pallas_call(
-        kernel,
-        in_specs=[pl.BlockSpec(memory_space=pltpu.SMEM)] + [in_vmem] * len(operands),
-        out_specs=[in_vmem] * len(out_shape) if isinstance(out_shape, list) else in_vmem,
-        out_shape=out_shape,
+        functools.partial(route_out_kernel, slots),
+        in_specs=[pl.BlockSpec(memory_space=pltpu.SMEM), in_vmem, in_vmem, in_vmem],
+        out_specs=pl.BlockSpec(memory_space=pltpu.HBM),
+        out_shape=pltpu.HBM(packed_shape(slots), BF16),
+        scratch_shapes=[packed_scratch(slots), pltpu.SemaphoreType.DMA((slots.local,))],
         compiler_params=pltpu.CompilerParams(vmem_limit_bytes=EXPERT_VMEM),
-        name=name,
-    )(scalars, *operands)
-
-
-def expert_part(kernel, name, slots, expert, recv, weights, shape, arrived):
-    if arrived is None:
-        out = jax.ShapeDtypeStruct(shape, BF16)
-        return expert_call(functools.partial(kernel, slots), name, out, expert, recv, *weights)
-    out = [jax.ShapeDtypeStruct(shape, F32), jax.ShapeDtypeStruct(shape, BF16)]
-    return expert_call(functools.partial(kernel, slots), name, out, expert, recv, *weights, arrived)
-
-
-def store_part(index, part, refs):
-    if len(refs) == 1:
-        refs[0][index] = part.astype(BF16)
-        return
-    arrived_ref, out_ref, low_ref = refs
-    total = part + arrived_ref[index].astype(F32)
-    out_ref[index] = total
-    low_ref[index] = total.astype(BF16)
-
-
-def gate_up_kernel(slots, expert_ref, recv_ref, gate_ref, up_ref, *refs):
-    e = expert_ref[0]
-    rows = unpack_rows(slots, recv_ref[:, e])
-    store_part(0, dot(rows, gate_ref[e]), refs)
-    store_part(1, dot(rows, up_ref[e]), refs)
-
-
-def gate_up(slots, expert, recv, gate_proj, up_proj, arrived=None):
-    shape = (2, slots.per_expert, gate_proj.shape[2])
-    weights = (gate_proj, up_proj)
-    return expert_part(gate_up_kernel, "gate_up", slots, expert, recv, weights, shape, arrived)
-
-
-def hidden_grad_kernel(slots, expert_ref, recv_ref, down_ref, *refs):
-    e = expert_ref[0]
-    rows = unpack_rows(slots, recv_ref[:, e])
-    store_part(..., dot(rows, down_ref[e], 1, 1), refs)
-
-
-def hidden_grad_part(slots, expert, recv, down_proj, arrived=None):
-    shape = (slots.per_expert, down_proj.shape[1])
-    return expert_part(
-        hidden_grad_kernel, "hidden_grad", slots, expert, recv, (down_proj,), shape, arrived
-    )
-
-
-def route_out_kernel(slots, order_ref, mine_ref, other_ref, down_ref, out_ref):
-    for at, hidden_ref in enumerate((mine_ref, other_ref)):
-        e = order_ref[at]
-        pack_rows(slots, dot(hidden_ref[...], down_ref[e]).astype(BF16), out_ref.at[:, e])
-
-
-def route_out(slots, order, mine, other, down_proj):
-    out = jax.ShapeDtypeStruct((slots.exp_count, slots.local, slots.rows, slots.columns), BF16)
-    kernel = functools.partial(route_out_kernel, slots)
-    return expert_call(kernel, "route_out", out, order, mine, other, down_proj)
-
-
-def route_in_kernel(slots, order_ref, mine_ref, other_ref, gate_ref, up_ref, out_ref):
-    for at, back_ref in enumerate((mine_ref, other_ref)):
-        e = order_ref[at]
-        total = dot(back_ref[0], gate_ref[e], 1, 1) + dot(back_ref[1], up_ref[e], 1, 1)
-        pack_rows(slots, total.astype(BF16), out_ref.at[:, e])
-
-
-def route_in(slots, order, mine, other, gate_proj, up_proj):
-    out = jax.ShapeDtypeStruct((slots.exp_count, slots.local, slots.rows, slots.columns), BF16)
-    kernel = functools.partial(route_in_kernel, slots)
-    return expert_call(kernel, "route_in", out, order, mine, other, gate_proj, up_proj)
+        name="route_out",
+    )(order, mine, other, down_proj)
+
+
+def route_in_kernel(
+    slots, order_ref, mine_ref, other_ref, held_ref, gate_ref, up_ref, out_ref,
+    mine_held, other_held, next_ref, packed_ref, sems, out_sems,
+):
+    first, second = order_ref[0], order_ref[1]
+    copies = fetch(
+        [mine_ref, gate_ref.at[second], up_ref.at[second], other_ref],
+        [mine_held, next_ref.at[0], next_ref.at[1], other_held],
+        sems,
+    )
+    copies[0].wait()
+    total = dot(mine_held[0], held_ref[0], 1, 1) + dot(mine_held[1], held_ref[1], 1, 1)
+    rows = total.astype(BF16)
+    stores = [store_rows(slots, rows, first, packed_ref.at[0], out_ref, out_sems.at[0])]
+    for copy in copies[1:]:
+        copy.wait()
+    total = dot(other_held[0], next_ref[0], 1, 1) + dot(other_held[1], next_ref[1], 1, 1)
+    rows = total.astype(BF16)
+    stores.append(store_rows(slots, rows, second, packed_ref.at[1], out_ref, out_sems.at[1]))
+    for store in stores:
+        store.wait()
+
+
+def route_in(slots, order, mine, other, held, gate_proj, up_proj):
+    anywhere = pl.BlockSpec(memory_space=pl.ANY)
+    return pl.pallas_call(
+        functools.partial(route_in_kernel, slots),
+        in_specs=[
+            pl.BlockSpec(memory_space=pltpu.SMEM), anywhere, anywhere,
+            pl.BlockSpec(memory_space=pltpu.VMEM), anywhere, anywhere,
+        ],
+        out_specs=pl.BlockSpec(memory_space=pltpu.HBM),
+        out_shape=pltpu.HBM(packed_shape(slots), BF16),
+        scratch_shapes=[
+            pltpu.VMEM(mine.shape, BF16),
+            pltpu.VMEM(other.shape, BF16),
+            pltpu.VMEM(held.shape, BF16),
+            packed_scratch(slots),
+            pltpu.SemaphoreType.DMA((4,)),
+            pltpu.SemaphoreType.DMA((slots.local,)),
+        ],
+        compiler_params=pltpu.CompilerParams(vmem_limit_bytes=EXPERT_VMEM),
+        name="route_in",
+    )(order, mine, other, held, in_hbm(gate_proj), in_hbm(up_proj))
 
 
 def attention_kernel(offsets, tokens, chunk, first, last, me_ref, q_ref, g_ref, kv_ref, kv_far_ref, *refs):
@@ -377,9 +472,14 @@
     g = [stacked(g_ref, pair) for pair in every]
     q_t = [jnp.transpose(value) for value in q]
     g_t = [jnp.transpose(value) for value in g]
-
-    top = []
-    for pair in every:
+    top, inverse, row_dot = {}, {}, {}
+
+    def keep_rows(ref, pair, value):
+        low = value.astype(BF16)
+        for h in range(heads):
+            ref[:, columns(pair, h)] = jnp.transpose(low[:, h * tokens : (h + 1) * tokens])
+
+    def score_stage(pair):
         largest = jnp.full((1, lanes), -jnp.inf, F32)
         for at in chunks:
             scores = dot(piece(at, 0), q_t[pair])
@@ -388,40 +488,46 @@
                 some = jnp.where(allowed, scores[part : part + tokens], -jnp.inf)
                 scores_ref[pair, at + part : at + part + tokens, :] = some
                 largest = jnp.maximum(largest, jnp.max(some, axis=0, keepdims=True))
-        top.append(largest * to_base2)
-    inverse = []
-    for pair in every:
+            yield
+        top[pair] = largest * to_base2
+
+    def raise_stage(pair):
         total = jnp.zeros((1, lanes), F32)
         for at in chunks:
             raised = jnp.exp2(scores_ref[pair, at : at + chunk, :] * to_base2 - top[pair])
-            low_ref[pair, at : at + chunk, :] = raised.astype(BF16)
+            scores_ref[pair, at : at + chunk, :] = raised
             total = total + jnp.sum(raised, axis=0, keepdims=True)
-        inverse.append(1.0 / total)
-    row_dot = []
-    for pair in every:
-        spread = jnp.zeros((d, lanes), F32)
+            yield
+        inverse[pair] = 1.0 / total
+
+    def attend_stage(pair):
+        attended = jnp.zeros((d, lanes), F32)
         for at in chunks:
-            spread = spread + dot(value_t[:, at : at + chunk], low_ref[pair, at : at + chunk, :])
-        attended = (spread * inverse[pair]).astype(BF16).astype(F32)
-        row_dot.append(jnp.sum(g_t[pair].astype(F32) * attended, axis=0, keepdims=True))
-        for h in range(heads):
-            rows = slice(h * tokens, (h + 1) * tokens)
-            out_ref[:, columns(pair, h)] = jnp.transpose(attended[:, rows]).astype(BF16)
-    for pair in every:
-        q_even = jnp.transpose(q_t[pair].astype(F32) * inverse[pair]).astype(BF16)
-        g_even = jnp.transpose(g_t[pair].astype(F32) * inverse[pair]).astype(BF16)
+            low = (scores_ref[pair, at : at + chunk, :] * inverse[pair]).astype(BF16)
+            low_ref[pair, at : at + chunk, :] = low
+            attended = attended + dot(value_t[:, at : at + chunk], low)
+            value_acc[at : at + chunk, :] += dot(low, g[pair])
+            yield
+        keep_rows(out_ref, pair, attended)
+        attended = attended.astype(BF16).astype(F32)
+        row_dot[pair] = jnp.sum(g_t[pair].astype(F32) * attended, axis=0, keepdims=True)
+
+    def back_stage(pair):
         query_back = jnp.zeros((d, lanes), F32)
         for at in chunks:
             low = low_ref[pair, at : at + chunk, :]
             prob_grad = dot(piece(at, d), g_t[pair])
             score_grad = (low.astype(F32) * (prob_grad - row_dot[pair])).astype(BF16)
             query_back = query_back + dot(key_t[:, at : at + chunk], score_grad)
-            key_acc[at : at + chunk, :] += dot(score_grad, q_even)
-            value_acc[at : at + chunk, :] += dot(low, g_even)
-        query_back = query_back * (inverse[pair] * scale)
-        for h in range(heads):
-            rows = slice(h * tokens, (h + 1) * tokens)
-            qgrad_ref[:, columns(pair, h)] = jnp.transpose(query_back[:, rows]).astype(BF16)
+            key_acc[at : at + chunk, :] += dot(score_grad, q[pair])
+            yield
+        keep_rows(qgrad_ref, pair, query_back * scale)
+
+    stages = (score_stage, raise_stage, attend_stage, back_stage)
+    for slot in range(pairs + len(stages) - 1):
+        running = [stages[slot - pair](pair) for pair in every if 0 <= slot - pair < len(stages)]
+        while running:
+            running = [stage for stage in running if next(stage, True) is None]
 
     @pl.when(step == pl.num_programs(0) - 1)
     def _():
@@ -440,10 +546,10 @@
     half, both = kv_near.shape
     seq = 2 * half
     heads = columns // HEAD_SIZE
-    group = 2 if heads % (2 * parts) == 0 else 1
+    group = 4 if heads % (4 * parts) == 0 and seq <= 2048 else 2 if heads % (2 * parts) == 0 else 1
     pairs = PAIRS if heads % (group * PAIRS * parts) == 0 and seq <= 2048 else 1
     lanes = group * tokens
-    chunk = min(256, half)
+    chunk = min(CHUNK, half)
     steps = heads // (group * pairs * parts)
     first, last = part == 0, part == parts - 1
     tile = pl.BlockSpec((tokens, pairs * group * HEAD_SIZE), lambda i, m: (0, i + part * steps))
@@ -480,7 +586,7 @@
             tokens * heads * seq // parts,
         ),
         name="attention",
-    )(me, in_hbm(queries), in_hbm(attn_grad), kv_near, kv_far, *(() if first else (carried[2], carried[0], carried[1])))
+    )(me, in_hbm(queries), in_hbm(attn_grad), in_hbm(kv_near), in_hbm(kv_far), *(() if first else (carried[2], carried[0], carried[1])))
 
 
 def swap(value, axis, bit):
@@ -501,18 +607,22 @@
     return bits
 
 
-def spread_sum(part, low, ctx_count, beside):
+def spread_sum(part, ctx_count, beside):
     result = None
     bit = 2
-    while bit < ctx_count:
-        arrived = swap(low, "ctx", bit)
+    while True:
+        arrived = swap(part.astype(BF16), "ctx", bit)
         if result is None:
-            result = beside(low)
+            result = beside(part)
             arrived = after(arrived, *result)
-        part = part + arrived.astype(F32)
-        low = part.astype(BF16)
         bit *= 2
-    return part, beside(low) if result is None else result
+        if bit >= ctx_count:
+            return (part, arrived), result
+        part = part.astype(F32) + arrived.astype(F32)
+
+
+def total_of(addends):
+    return addends[0].astype(F32) + addends[1].astype(F32)
 
 
 def activate(gate, up):
@@ -557,62 +667,66 @@
     me = exp_index.astype(jnp.int32).reshape(1)
     ids = expert_ids.T
     gains = route_weights.T
-    send_rows = dispatch(slots, False, ids, gains, moe_input)
-    recv_rows = exchange(send_rows).reshape(shape)
-    send_scaled = dispatch(slots, True, ids, gains, after(moe_grad, send_rows))
-
-    key_proj = after(key_proj, send_scaled)
-    own = jnp.concatenate(
+
+    kv = jnp.concatenate(
         [
             lax.dynamic_slice_in_dim(key_proj, kv_head * d, d, 1),
             lax.dynamic_slice_in_dim(value_matrix_rows, kv_head * d, d, 1),
         ],
         axis=1,
     )
-    offsets = list(range(0, exp_count, 2)) + list(range(1, exp_count, 2))
-    gathered = [swap(own, "exp", offset) for offset in offsets[1 : exp_count // 2]]
-    gate_held, up_held, down_proj = hold(after(gate_proj, own), up_proj, down_proj)
-    kv = jnp.concatenate([own, *gathered], axis=0)
-    kv_far = swap(kv, "exp", 1)
+    send_rows = dispatch(slots, False, ids, gains, moe_input)
+    offsets = [0]
+    kv_far = None
+    for bit in far_bits(exp_count):
+        if kv_far is not None:
+            kv = jnp.concatenate([kv, after(kv_far, send_rows)], axis=0)
+        if bit == 2:
+            recv_rows = exchange(after(send_rows, kv)).reshape(shape)
+        kv_far = swap(kv, "exp", bit)
+        offsets = offsets + [o ^ bit for o in offsets]
+    send_scaled = dispatch(slots, True, ids, gains, after(moe_grad, send_rows))
+    held = hold(other, after(gate_proj, send_scaled), up_proj)
 
     def heads(part, carried, earlier):
         return attention(
             me, tuple(offsets), after(queries, earlier), attn_grad, kv, kv_far, part, 1, carried
         )
 
-    recv_rows = after(recv_rows, down_proj)
-    gu_send = gate_up(slots, other, recv_rows, gate_held, up_held)
+    recv_rows = after(recv_rows, kv)
+    gu_send, held, rows = gate_up_send(slots, order[::-1], recv_rows, held, gate_proj, up_proj)
     gu_recv = swap(gu_send, "ctx", 1)
-    recv_rows = after(recv_rows, gu_send, kv)
-    gu_part, gu_low = gate_up(slots, mine, recv_rows, gate_held, up_held, gu_recv)
-    recv_scaled = exchange(after(send_scaled, gu_low)).reshape(shape)
-    (gate_full, up_full), (attn_out, query_grad, kv_keep, kv_send) = spread_sum(
-        gu_part, gu_low, ctx_count, lambda part: heads(0, None, part)
-    )
-    hidden = activate(gate_full, up_full)
+    gu_part = gate_up_keep(rows, held, gu_recv)
+    recv_scaled = exchange(after(send_scaled, gu_part)).reshape(shape)
+    gate_up_sum, (attn_out, query_grad, kv_keep, kv_send) = spread_sum(
+        gu_part, ctx_count, lambda part: heads(0, None, part)
+    )
+    kv_recv = swap(kv_send, "exp", 1)
+    hidden = activate(*total_of(gate_up_sum))
     hidden_other = swap(hidden, "ctx", 1)
-    hg_send = hidden_grad_part(slots, other, after(recv_scaled, hidden), down_proj)
+    hg_send, rows = hidden_grad_send(slots, order[::-1], after(recv_scaled, hidden), down_proj)
     hg_recv = swap(hg_send, "ctx", 1)
     out_rows = route_out(slots, order, after(hidden, hg_send), hidden_other, down_proj)
-    back_out = exchange(out_rows).reshape(slots.total, slots.columns)
-
-    hg_part, hg_low = hidden_grad_part(
-        slots, mine, after(recv_scaled, out_rows), down_proj, hg_recv
-    )
-    hg_full, _ = spread_sum(hg_part, hg_low, ctx_count, lambda part: (part,))
-    kv_sum = kv_keep + swap(kv_send, "exp", 1).astype(F32)
+    back_out = exchange(after(out_rows, kv_recv)).reshape(slots.total, slots.columns)
+
+    hg_part = hidden_grad_keep(mine, after(rows, out_rows), down_proj, hg_recv)
+    kv_sum = kv_keep + after(kv_recv, hg_part).astype(F32)
     kv_low = kv_sum.astype(BF16)
     blocks = exp_count // 2
     kv_parts = [
         swap(kv_low[i * tokens : (i + 1) * tokens], "exp", offsets[i]) for i in range(1, blocks)
     ]
-    back = gate_backward(hg_full, gate_full, up_full)
+    gate_up_sum = [after(value, hg_part) for value in gate_up_sum]
+    gate_up_total = total_of(gate_up_sum)
+    held = hold(mine, after(gate_proj, hg_part), up_proj)
+    hg_sum, _ = spread_sum(hg_part, ctx_count, lambda part: (kv_low, gate_up_total, held))
+    back = gate_backward(total_of(hg_sum), *gate_up_total)
     back_other = swap(back, "ctx", 1)
+    in_rows = route_in(slots, order, back, back_other, held, gate_proj, up_proj)
     kv_total = kv_sum[:tokens]
     for part in kv_parts:
-        kv_total = kv_total + part.astype(F32)
+        kv_total = kv_total + after(part, in_rows).astype(F32)
     kv_total = kv_total.astype(BF16)
-    in_rows = route_in(slots, order, back, back_other, gate_proj, up_proj)
     back_in = exchange(after(in_rows, kv_total)).reshape(slots.total, slots.columns)
 
     moe_out = combine(slots, True, ids, gains, after(back_out, in_rows))

time: 126 us -> 111 us (0.88)
  local copies, waits for them, and re-layouts: 12 us -> 3.33 us
  waiting for transfers between devices: 28.3 us -> 20 us
  other arithmetic: 4.28 us -> 6.33 us
  starting transfers between devices: 34.2 us -> 35.9 us
    unnamed x34 -> x18, local copies, waits for them, and re-layouts: 11.2 us -> 2.39 us
    ppermute x14 -> x13, waiting for transfers between devices: 17.2 us -> 11.5 us  [swap(): return lax.ppermute(value, axis, [(i, i ^ bit) for i in range(count)])]
    pallas_call x1, Pallas kernels: 13.5 us -> 9.92 us  [attention(): pl.pallas_call(functools.partial(attention_kernel, offsets, tokens, chunk...]
    all_to_all x4, waiting for transfers between devices: 11.2 us -> 8.43 us  [exchange(): return lax.all_to_all(flat, 'exp', split_axis=0, concat_axis=0, tiled=True)]
    ppermute x14 -> x13, starting transfers between devices: 14.6 us -> 17.3 us  [swap(): return lax.ppermute(value, axis, [(i, i ^ bit) for i in range(count)])]
    pallas_call x7 -> x8, Pallas kernels: 17.2 us -> 19.2 us  [the longest x6 11.8 us: expert_call(): pl.pallas_call(kernel, in_specs=specs, out_specs=[in_vmem] * len(out_shap...]
    add x1 -> x2, other arithmetic: 1.09 us -> 2.47 us  [total_of(): return addends[0].astype(F32) + addends[1].astype(F32)]
  transfers between devices with their start and end apart: 18 -> 17, of which waited for: 7 -> 8; matrix products, arithmetic and copies ran while one was open for 4% -> 6% of each run, Pallas kernels for 27% -> 31%
where the time goes in v3:
time: 111 us; the launch traced here: 110 us
  Pallas kernels  38.3 us (35%)
  starting transfers between devices  35.9 us (32%)
  waiting for transfers between devices  20 us (18%)
  other arithmetic  6.33 us (6%)
  blocking collectives  5.77 us (5%)
  local copies, waits for them, and re-layouts  3.33 us (3%)
    all_to_all x4, starting transfers between devices, exchange(): return lax.all_to_all(flat, 'exp', split_axis=0, concat_axis=0, tiled=True)  18.6 us
    ppermute x13, starting transfers between devices, swap(): return lax.ppermute(value, axis, [(i, i ^ bit) for i in range(count)])  17.3 us
    pallas_call x6, Pallas kernels, expert_call(): pl.pallas_call(kernel, in_specs=specs, out_specs=[in_vmem] * len(out_shap...  11.8 us
    ppermute x13, waiting for transfers between devices, swap(): return lax.ppermute(value, axis, [(i, i ^ bit) for i in range(count)])  11.5 us
    pallas_call x1, Pallas kernels, attention(): pl.pallas_call(functools.partial(attention_kernel, offsets, tokens, chunk...  9.92 us
    all_to_all x4, waiting for transfers between devices, exchange(): return lax.all_to_all(flat, 'exp', split_axis=0, concat_axis=0, tiled=True)  8.43 us
    all_gather x1, blocking collectives, body(): lax.all_gather(after(kv_total, in_rows), 'ctx', axis=0, tiled=False)  5.77 us
    pallas_call x2, Pallas kernels, dispatch(): pl.pallas_call(functools.partial(dispatch_kernel, slots, weighted), out_s...  4.91 us
  transfers between devices with their start and end apart: 17, of which 8 were waited for; matrix products, arithmetic and copies ran while one was open for 6% of the time, Pallas kernels for 31%

profile of v3, /device:TPU:0, one launch (start us, length us, event | category | flops | bytes accessed | tf_op | source)
XLA Modules:
  0.0 110.4 jit_solution(14412984737958945639)
XLA Ops:
  1.4 4.1 %collective-permute-start = (bf16[128,256]{1,0:T(8,128)(2,1)S(1)}, bf16[128,256]{1,0:T(8,128)(2,1)S(1)}, u32[]{:S(2)}, u32[]{:S(2)}) collective-permute-start(bf16[128,256]{1,0:T(8,128)(2,1)S(1)} %pad_maximum_fusion.5), channel_id=1, source_target_pairs={{0,4},{1,5},{2,6},{3,7},{4,0},{5,1},{6,2},{7,3},{8,12},{9,13},{10,... | collective-permute-start | bytes 196616 | tf_op jit(solution)/shard_map/ppermute | solution.py:594
  5.5 2.4 %dispatch_rows.1 = bf16[256,1152]{1,0:T(8,128)(2,1)} custom-call(s32[2,128]{1,0:T(2,128)} %bitcast.66, f32[2,128]{1,0:T(2,128)} %bitcast.70, bf16[128,1024]{1,0:T(8,128)(2,1)} %rows_ref.1), custom_call_target="tpu_custom_call" | custom-call | flops 134217728 | bytes 1179648 | tf_op jit(solution)/shard_map/dispatch_rows/pallas_call | solution.py:130
  7.9 1.2 %collective-permute-done = bf16[128,256]{1,0:T(8,128)(2,1)S(1)} collective-permute-done((bf16[128,256]{1,0:T(8,128)(2,1)S(1)}, bf16[128,256]{1,0:T(8,128)(2,1)S(1)}, u32[]{:S(2)}, u32[]{:S(2)}) %collective-permute-start) | collective-permute-done | bytes 65568 | tf_op jit(solution)/shard_map/ppermute | solution.py:594
  9.2 5.6 %all-to-all-start = ((bf16[8,32,1152]{2,1,0:T(8,128)(2,1)}), bf16[8,32,1152]{2,1,0:T(8,128)(2,1)}, u32[]{:S(2)}, u32[]{:S(2)}) async-start(bf16[8,32,1152]{2,1,0:T(8,128)(2,1)} %bitcast.4), calls=%async_computation | async-start | bytes 1179648 | tf_op jit(solution)/shard_map/all_to_all | solution.py:665
  14.8 2.0 %collective-permute-start.1 = (bf16[256,256]{1,0:T(8,128)(2,1)S(1)}, bf16[256,256]{1,0:T(8,128)(2,1)}, u32[]{:S(2)}, u32[]{:S(2)}) collective-permute-start(bf16[256,256]{1,0:T(8,128)(2,1)S(1)} %pad_maximum_fusion.2), channel_id=1, source_target_pairs={{0,2},{1,3},{2,0},{3,1},{4,6},{5,7},{6,4},{7,5},{8,10},{9,11},{10,... | collective-permute-start | bytes 393224 | tf_op jit(solution)/shard_map/ppermute | solution.py:594
  17.0 2.5 %dispatch_scaled.1 = bf16[256,1152]{1,0:T(8,128)(2,1)} custom-call(s32[2,128]{1,0:T(2,128)} %bitcast.67, f32[2,128]{1,0:T(2,128)} %bitcast.71, bf16[128,1024]{1,0:T(8,128)(2,1)} %rows_ref.2), custom_call_target="tpu_custom_call" | custom-call | flops 134217728 | bytes 1179648 | tf_op jit(solution)/shard_map/dispatch_scaled/pallas_call | solution.py:130
  19.5 1.9 %hold_weights.2.held_ref = bf16[2,1024,768]{2,1,0:T(8,128)(2,1)S(1)} custom-call(s32[1]{0:T(128)S(6)} %sub.8.expert_ref, bf16[2,1024,768]{2,1,0:T(8,128)(2,1)} %gate_ref.5, bf16[2,1024,768]{2,1,0:T(8,128)(2,1)} %up_ref.7), custom_call_target="tpu_custom_call" | custom-call | tf_op jit(solution)/shard_map/hold_weights/pallas_call | solution.py:257
  21.4 6.3 %collective-permute-done.1 = bf16[256,256]{1,0:T(8,128)(2,1)} collective-permute-done((bf16[256,256]{1,0:T(8,128)(2,1)S(1)}, bf16[256,256]{1,0:T(8,128)(2,1)}, u32[]{:S(2)}, u32[]{:S(2)}) %collective-permute-start.1) | collective-permute-done | bytes 131104 | tf_op jit(solution)/shard_map/ppermute | solution.py:594
  28.7 1.9 %all-to-all-done = bf16[8,32,1152]{2,1,0:T(8,128)(2,1)} async-done(((bf16[8,32,1152]{2,1,0:T(8,128)(2,1)}), bf16[8,32,1152]{2,1,0:T(8,128)(2,1)}, u32[]{:S(2)}, u32[]{:S(2)}) %all-to-all-start) | async-done | bytes 589856 | tf_op jit(solution)/shard_map/all_to_all | solution.py:665
  30.6 2.6 %gate_up_send.1 = (bf16[2,144,768]{2,1,0:T(8,128)(2,1)S(1)}, bf16[2,1024,768]{2,1,0:T(8,128)(2,1)S(1)}, bf16[144,1024]{1,0:T(8,128)(2,1)S(1)}) custom-call(s32[2]{0:T(128)S(1)} %rev.4.order_ref, bf16[8,2,16,1152]{3,2,1,0:T(8,128)(2,1)} %bitcast.5.recv_ref, bf16[2,1024,768]{2,1,0:T(8,128)(2,1)S(1)} %hold_weights.2.held_ref, bf16[2,1024,768]{2,1,0:T(8,128)(2,1)} %gate_ref.5, ...), custom_call_target="tpu_custom_call" | custom-call | tf_op jit(solution)/shard_map/gate_up_send/pallas_call | solution.py:257
  33.4 1.5 %collective-permute-start.3 = (bf16[512,256]{1,0:T(8,128)(2,1)S(1)}, bf16[512,256]{1,0:T(8,128)(2,1)S(1)}, u32[]{:S(2)}, u32[]{:S(2)}) collective-permute-start(bf16[512,256]{1,0:T(8,128)(2,1)S(1)} %pad_maximum_fusion.1.kv_ref), channel_id=1, source_target_pairs={{0,1},{1,0},{2,3},{3,2},{4,5},{5,4},{6,7},{7,6},{8,9},{9,8},{10,11... | collective-permute-start | bytes 786440 | tf_op jit(solution)/shard_map/ppermute | solution.py:594
  35.1 1.4 %gate_up_keep.1 = bf16[2,144,768]{2,1,0:T(8,128)(2,1)} custom-call(bf16[144,1024]{1,0:T(8,128)(2,1)S(1)} %get-tuple-element.45.rows_ref, bf16[2,1024,768]{2,1,0:T(8,128)(2,1)S(1)} %get-tuple-element.46.held_ref, bf16[2,144,768]{2,1,0:T(8,128)(2,1)S(1)} %collective-permute-done.2.arrived_ref), custom_call_target="tpu_custom_call" | custom-call | tf_op jit(solution)/shard_map/gate_up_keep/pallas_call | solution.py:257
  36.5 4.3 %all-to-all-start.1 = ((bf16[8,32,1152]{2,1,0:T(8,128)(2,1)}), bf16[8,32,1152]{2,1,0:T(8,128)(2,1)}, u32[]{:S(2)}, u32[]{:S(2)}) async-start(bf16[8,32,1152]{2,1,0:T(8,128)(2,1)} %bitcast.6), calls=%async_computation.1 | async-start | bytes 1179648 | tf_op jit(solution)/shard_map/all_to_all | solution.py:665
  40.9 1.5 %collective-permute-start.5 = (bf16[2,144,768]{2,1,0:T(8,128)(2,1)}, bf16[2,144,768]{2,1,0:T(8,128)(2,1)}, u32[]{:S(2)}, u32[]{:S(2)}) collective-permute-start(bf16[2,144,768]{2,1,0:T(8,128)(2,1)} %gate_up_keep.1), channel_id=1, source_target_pairs={{0,16},{8,24},{16,0},{24,8},{1,17},{9,25},{17,1},{25,9},{2,18},{10... | collective-permute-start | bytes 1327112 | tf_op jit(solution)/shard_map/ppermute | solution.py:594
  43.1 9.9 %attention.1 = (bf16[128,2048]{1,0:T(8,128)(2,1)}, bf16[128,2048]{1,0:T(8,128)(2,1)}, f32[512,256]{1,0:T(8,128)S(1)}, bf16[512,256]{1,0:T(8,128)(2,1)}) custom-call(s32[1]{0:T(128)} %bitcast.me_ref, bf16[128,2048]{1,0:T(8,128)(2,1)} %q_ref, bf16[128,2048]{1,0:T(8,128)(2,1)} %g_ref.1, bf16[512,256]{1,0:T(8,128)(2,1)} %copy-done.7, bf16[512,256]{1,0:T(8,128)(2,1)} %copy-done.8), custom_call_target="tpu_custom_call" | custom-call | flops 3221225472 | bytes 2097152 | tf_op jit(solution)/shard_map/attention/pallas_call | solution.py:564
  53.0 2.0 %collective-permute-start.4 = (bf16[512,256]{1,0:T(8,128)(2,1)}, bf16[512,256]{1,0:T(8,128)(2,1)}, u32[]{:S(2)}, u32[]{:S(2)}) collective-permute-start(bf16[512,256]{1,0:T(8,128)(2,1)} %get-tuple-element.52), channel_id=1, source_target_pairs={{0,1},{1,0},{2,3},{3,2},{4,5},{5,4},{6,7},{7,6},{8,9},{9,8},{10,11... | collective-permute-start | bytes 786440 | tf_op jit(solution)/shard_map/ppermute | solution.py:594
  57.2 2.4 %hidden_grad_send.1 = (bf16[144,768]{1,0:T(8,128)(2,1)}, bf16[144,1024]{1,0:T(8,128)(2,1)S(1)}) custom-call(s32[2]{0:T(128)S(1)} %rev.4.order_ref, bf16[8,2,16,1152]{3,2,1,0:T(8,128)(2,1)} %bitcast.7.recv_ref, bf16[2,768,1024]{2,1,0:T(8,128)(2,1)S(1)} %copy-done), custom_call_target="tpu_custom_call" | custom-call | tf_op jit(solution)/shard_map/hidden_grad_send/pallas_call | solution.py:257
  60.3 2.6 %route_out.1 = bf16[8,2,16,1152]{3,2,1,0:T(8,128)(2,1)} custom-call(s32[2]{0:T(128)S(1)} %pad_add_fusion.order_ref, bf16[144,768]{1,0:T(8,128)(2,1)S(1)} %fusion.5.mine_ref, bf16[144,768]{1,0:T(8,128)(2,1)} %collective-permute-done.6.other_ref, bf16[2,768,1024]{2,1,0:T(8,128)(2,1)S(1)} %copy-done), custom_call_target="tpu_custom_call" | custom-call | tf_op jit(solution)/shard_map/route_out/pallas_call | solution.py:364
  63.0 4.5 %all-to-all-start.2 = ((bf16[8,32,1152]{2,1,0:T(8,128)(2,1)}), bf16[8,32,1152]{2,1,0:T(8,128)(2,1)}, u32[]{:S(2)}, u32[]{:S(2)}) async-start(bf16[8,32,1152]{2,1,0:T(8,128)(2,1)} %bitcast.74), calls=%async_computation.2 | async-start | bytes 1179648 | tf_op jit(solution)/shard_map/all_to_all | solution.py:665
  68.5 1.6 %hidden_grad_keep.1 = bf16[144,768]{1,0:T(8,128)(2,1)S(1)} custom-call(s32[1]{0:T(128)} %bitcast.1.expert_ref, bf16[144,1024]{1,0:T(8,128)(2,1)S(1)} %copy-done.4, bf16[2,768,1024]{2,1,0:T(8,128)(2,1)S(1)} %copy-done, bf16[144,768]{1,0:T(8,128)(2,1)} %collective-permute-done.7.arrived_ref), custom_call_target="tpu_custom_call" | custom-call | tf_op jit(solution)/shard_map/hidden_grad_keep/pallas_call | solution.py:257
  70.1 1.4 %collective-permute-start.9 = (bf16[144,768]{1,0:T(8,128)(2,1)S(1)}, bf16[144,768]{1,0:T(8,128)(2,1)S(1)}, u32[]{:S(2)}, u32[]{:S(2)}) collective-permute-start(bf16[144,768]{1,0:T(8,128)(2,1)S(1)} %hidden_grad_keep.1), channel_id=1, source_target_pairs={{0,16},{8,24},{16,0},{24,8},{1,17},{9,25},{17,1},{25,9},{2,18},{10... | collective-permute-start | bytes 663560 | tf_op jit(solution)/shard_map/ppermute | solution.py:594
  71.5 1.9 %hold_weights.3.held_ref = bf16[2,1024,768]{2,1,0:T(8,128)(2,1)S(1)} custom-call(s32[1]{0:T(128)} %bitcast.1.expert_ref, bf16[2,1024,768]{2,1,0:T(8,128)(2,1)} %gate_ref.5, bf16[2,1024,768]{2,1,0:T(8,128)(2,1)} %up_ref.7), custom_call_target="tpu_custom_call" | custom-call | tf_op jit(solution)/shard_map/hold_weights/pallas_call | solution.py:257
  75.7 2.1 %collective-permute-done.9 = bf16[144,768]{1,0:T(8,128)(2,1)S(1)} collective-permute-done((bf16[144,768]{1,0:T(8,128)(2,1)S(1)}, bf16[144,768]{1,0:T(8,128)(2,1)S(1)}, u32[]{:S(2)}, u32[]{:S(2)}) %collective-permute-start.9) | collective-permute-done | bytes 221216 | tf_op jit(solution)/shard_map/ppermute | solution.py:594
  78.2 2.6 %collective-permute-start.8 = (bf16[128,256]{1,0:T(8,128)(2,1)S(1)}, bf16[128,256]{1,0:T(8,128)(2,1)S(1)}, u32[]{:S(2)}, u32[]{:S(2)}) collective-permute-start(bf16[128,256]{1,0:T(8,128)(2,1)S(1)} %get-tuple-element.84), channel_id=1, source_target_pairs={{0,4},{1,5},{2,6},{3,7},{4,0},{5,1},{6,2},{7,3},{8,12},{9,13},{10,... | collective-permute-start | bytes 196616 | tf_op jit(solution)/shard_map/ppermute | solution.py:594
  80.8 1.5 %collective-permute-start.11 = (bf16[128,256]{1,0:T(8,128)(2,1)S(1)}, bf16[128,256]{1,0:T(8,128)(2,1)S(1)}, u32[]{:S(2)}, u32[]{:S(2)}) collective-permute-start(bf16[128,256]{1,0:T(8,128)(2,1)S(1)} %get-tuple-element.86), channel_id=1, source_target_pairs={{0,2},{1,3},{2,0},{3,1},{4,6},{5,7},{6,4},{7,5},{8,10},{9,11},{10,... | collective-permute-start | bytes 196616 | tf_op jit(solution)/shard_map/ppermute | solution.py:594
  82.7 4.8 %route_in.1 = bf16[8,2,16,1152]{3,2,1,0:T(8,128)(2,1)} custom-call(s32[2]{0:T(128)S(1)} %pad_add_fusion.order_ref, bf16[2,144,768]{2,1,0:T(8,128)(2,1)S(1)} %pad_maximum_fusion.mine_ref, bf16[2,144,768]{2,1,0:T(8,128)(2,1)S(1)} %collective-permute-done.10.other_ref, bf16[2,1024,768]{2,1,0:T(8,128)(2,1)S(1)} %hold_weights.3.held_ref, ...), custom_call_target="tpu_custom_call" | custom-call | tf_op jit(solution)/shard_map/route_in/pallas_call | solution.py:400
  87.5 1.5 %collective-permute-done.8 = bf16[128,256]{1,0:T(8,128)(2,1)S(1)} collective-permute-done((bf16[128,256]{1,0:T(8,128)(2,1)S(1)}, bf16[128,256]{1,0:T(8,128)(2,1)S(1)}, u32[]{:S(2)}, u32[]{:S(2)}) %collective-permute-start.8) | collective-permute-done | bytes 65568 | tf_op jit(solution)/shard_map/ppermute | solution.py:594
  89.1 4.1 %all-to-all-start.3 = ((bf16[8,32,1152]{2,1,0:T(8,128)(2,1)}), bf16[8,32,1152]{2,1,0:T(8,128)(2,1)S(1)}, u32[]{:S(2)}, u32[]{:S(2)}) async-start(bf16[8,32,1152]{2,1,0:T(8,128)(2,1)} %bitcast.75), calls=%async_computation.3 | async-start | bytes 1179648 | tf_op jit(solution)/shard_map/all_to_all | solution.py:665
  93.2 5.8 %all-gather = bf16[512,256]{1,0:T(8,128)(2,1)S(1)} all-gather(bf16[128,256]{1,0:T(8,128)(2,1)S(1)} %fusion.10), channel_id=2, replica_groups=mesh['ctx'=4,'exp'=8] {'ctx'}, dimensions={0}, use_global_device_ids=true | all-gather | bytes 327680 | tf_op jit(solution)/shard_map/all_gather | solution.py:735
  100.4 2.7 %combine_out.1 = bf16[128,1024]{1,0:T(8,128)(2,1)} custom-call(s32[2,128]{1,0:T(2,128)S(1)} %bitcast.68, f32[2,128]{1,0:T(2,128)S(1)} %bitcast.72, bf16[256,1152]{1,0:T(8,128)(2,1)} %bitcast.24.back_ref), custom_call_target="tpu_custom_call" | custom-call | flops 268435456 | bytes 1179648 | tf_op jit(solution)/shard_map/combine_out/pallas_call | solution.py:174
  103.1 5.8 %all-to-all-done.3 = bf16[8,32,1152]{2,1,0:T(8,128)(2,1)S(1)} async-done(((bf16[8,32,1152]{2,1,0:T(8,128)(2,1)}), bf16[8,32,1152]{2,1,0:T(8,128)(2,1)S(1)}, u32[]{:S(2)}, u32[]{:S(2)}) %all-to-all-start.3) | async-done | bytes 589856 | tf_op jit(solution)/shard_map/all_to_all | solution.py:665
  108.9 1.5 %combine_in.1 = bf16[128,1024]{1,0:T(8,128)(2,1)} custom-call(s32[2,128]{1,0:T(2,128)S(1)} %bitcast.69, f32[2,128]{1,0:T(2,128)S(1)} %bitcast.73, bf16[256,1152]{1,0:T(8,128)(2,1)S(1)} %bitcast.65), custom_call_target="tpu_custom_call" | custom-call | flops 268435456 | bytes 1179648 | tf_op jit(solution)/shard_map/combine_in/pallas_call | solution.py:174
  (51 shorter events, 11.2 us)
Async XLA Ops:
  1.4 7.8 %collective-permute-start = (bf16[128,256]{1,0:T(8,128)(2,1)S(1)}, bf16[128,256]{1,0:T(8,128)(2,1)S(1)}, u32[]{:S(2)}, u32[]{:S(2)}) collective-permute-start(bf16[128,256]{1,0:T(8,128)(2,1)S(1)} %pad_maximum_fusion.5), channel_id=1, source_target_pairs={{0,4},{1,5},{2,6},{3,7},{4,0},{5,1},{6,2},{7,3},{8,12},{9,13},{10,... | collective-permute-start | bytes 196616 | tf_op jit(solution)/shard_map/ppermute | solution.py:594
  9.2 21.4 %all-to-all-start = ((bf16[8,32,1152]{2,1,0:T(8,128)(2,1)}), bf16[8,32,1152]{2,1,0:T(8,128)(2,1)}, u32[]{:S(2)}, u32[]{:S(2)}) async-start(bf16[8,32,1152]{2,1,0:T(8,128)(2,1)} %bitcast.4), calls=%async_computation | async-start | bytes 1179648 | tf_op jit(solution)/shard_map/all_to_all | solution.py:665
  14.8 13.0 %collective-permute-start.1 = (bf16[256,256]{1,0:T(8,128)(2,1)S(1)}, bf16[256,256]{1,0:T(8,128)(2,1)}, u32[]{:S(2)}, u32[]{:S(2)}) collective-permute-start(bf16[256,256]{1,0:T(8,128)(2,1)S(1)} %pad_maximum_fusion.2), channel_id=1, source_target_pairs={{0,2},{1,3},{2,0},{3,1},{4,6},{5,7},{6,4},{7,5},{8,10},{9,11},{10,... | collective-permute-start | bytes 393224 | tf_op jit(solution)/shard_map/ppermute | solution.py:594
  28.7 4.7 %copy-start.7 = (bf16[512,256]{1,0:T(8,128)(2,1)}, bf16[512,256]{1,0:T(8,128)(2,1)S(1)}, u32[]{:S(2)}) copy-start(bf16[512,256]{1,0:T(8,128)(2,1)S(1)} %pad_maximum_fusion.1.kv_ref) | copy-start | bytes 786436
  33.3 1.9 %collective-permute-start.2 = (bf16[2,144,768]{2,1,0:T(8,128)(2,1)S(1)}, bf16[2,144,768]{2,1,0:T(8,128)(2,1)S(1)}, u32[]{:S(2)}, u32[]{:S(2)}) collective-permute-start(bf16[2,144,768]{2,1,0:T(8,128)(2,1)S(1)} %get-tuple-element.47), channel_id=1, source_target_pairs={{0,8},{8,0},{16,24},{24,16},{1,9},{9,1},{17,25},{25,17},{2,10},{10... | collective-permute-start | bytes 1327112 | tf_op jit(solution)/shard_map/ppermute | solution.py:594
  33.4 9.0 %collective-permute-start.3 = (bf16[512,256]{1,0:T(8,128)(2,1)S(1)}, bf16[512,256]{1,0:T(8,128)(2,1)S(1)}, u32[]{:S(2)}, u32[]{:S(2)}) collective-permute-start(bf16[512,256]{1,0:T(8,128)(2,1)S(1)} %pad_maximum_fusion.1.kv_ref), channel_id=1, source_target_pairs={{0,1},{1,0},{2,3},{3,2},{4,5},{5,4},{6,7},{7,6},{8,9},{9,8},{10,11... | collective-permute-start | bytes 786440 | tf_op jit(solution)/shard_map/ppermute | solution.py:594
  36.5 20.7 %all-to-all-start.1 = ((bf16[8,32,1152]{2,1,0:T(8,128)(2,1)}), bf16[8,32,1152]{2,1,0:T(8,128)(2,1)}, u32[]{:S(2)}, u32[]{:S(2)}) async-start(bf16[8,32,1152]{2,1,0:T(8,128)(2,1)} %bitcast.6), calls=%async_computation.1 | async-start | bytes 1179648 | tf_op jit(solution)/shard_map/all_to_all | solution.py:665
  40.9 14.2 %collective-permute-start.5 = (bf16[2,144,768]{2,1,0:T(8,128)(2,1)}, bf16[2,144,768]{2,1,0:T(8,128)(2,1)}, u32[]{:S(2)}, u32[]{:S(2)}) collective-permute-start(bf16[2,144,768]{2,1,0:T(8,128)(2,1)} %gate_up_keep.1), channel_id=1, source_target_pairs={{0,16},{8,24},{16,0},{24,8},{1,17},{9,25},{17,1},{25,9},{2,18},{10... | collective-permute-start | bytes 1327112 | tf_op jit(solution)/shard_map/ppermute | solution.py:594
  42.4 0.7 copy-start.8
  43.1 14.1 %copy-start = (bf16[2,768,1024]{2,1,0:T(8,128)(2,1)S(1)}, bf16[2,768,1024]{2,1,0:T(8,128)(2,1)}, u32[]{:S(2)}) copy-start(bf16[2,768,1024]{2,1,0:T(8,128)(2,1)} %down_ref.5) | copy-start | bytes 9437188
  53.0 3.3 %copy-start.1 = (f32[512,256]{1,0:T(8,128)}, f32[512,256]{1,0:T(8,128)S(1)}, u32[]{:S(2)}) copy-start(f32[512,256]{1,0:T(8,128)S(1)} %get-tuple-element.51) | copy-start | bytes 1572868
  53.0 9.9 %collective-permute-start.4 = (bf16[512,256]{1,0:T(8,128)(2,1)}, bf16[512,256]{1,0:T(8,128)(2,1)}, u32[]{:S(2)}, u32[]{:S(2)}) collective-permute-start(bf16[512,256]{1,0:T(8,128)(2,1)} %get-tuple-element.52), channel_id=1, source_target_pairs={{0,1},{1,0},{2,3},{3,2},{4,5},{5,4},{6,7},{7,6},{8,9},{9,8},{10,11... | collective-permute-start | bytes 786440 | tf_op jit(solution)/shard_map/ppermute | solution.py:594
  56.4 3.9 %collective-permute-start.6 = (bf16[144,768]{1,0:T(8,128)(2,1)S(1)}, bf16[144,768]{1,0:T(8,128)(2,1)}, u32[]{:S(2)}, u32[]{:S(2)}) collective-permute-start(bf16[144,768]{1,0:T(8,128)(2,1)S(1)} %fusion.5.mine_ref), channel_id=1, source_target_pairs={{0,8},{8,0},{16,24},{24,16},{1,9},{9,1},{17,25},{25,17},{2,10},{10... | collective-permute-start | bytes 663560 | tf_op jit(solution)/shard_map/ppermute | solution.py:594
  59.6 0.7 copy-start.3
  60.3 7.2 %collective-permute-start.7 = (bf16[144,768]{1,0:T(8,128)(2,1)}, bf16[144,768]{1,0:T(8,128)(2,1)}, u32[]{:S(2)}, u32[]{:S(2)}) collective-permute-start(bf16[144,768]{1,0:T(8,128)(2,1)} %get-tuple-element.57), channel_id=1, source_target_pairs={{0,8},{8,0},{16,24},{24,16},{1,9},{9,1},{17,25},{25,17},{2,10},{10... | collective-permute-start | bytes 663560 | tf_op jit(solution)/shard_map/ppermute | solution.py:594
  63.0 26.1 %all-to-all-start.2 = ((bf16[8,32,1152]{2,1,0:T(8,128)(2,1)}), bf16[8,32,1152]{2,1,0:T(8,128)(2,1)}, u32[]{:S(2)}, u32[]{:S(2)}) async-start(bf16[8,32,1152]{2,1,0:T(8,128)(2,1)} %bitcast.74), calls=%async_computation.2 | async-start | bytes 1179648 | tf_op jit(solution)/shard_map/all_to_all | solution.py:665
  67.5 1.0 copy-start.4
  70.1 4.6 %copy-start.2 = (f32[512,256]{1,0:T(8,128)S(1)}, f32[512,256]{1,0:T(8,128)}, u32[]{:S(2)}) copy-start(f32[512,256]{1,0:T(8,128)} %copy-done.1) | copy-start | bytes 1572868
  70.1 7.8 %collective-permute-start.9 = (bf16[144,768]{1,0:T(8,128)(2,1)S(1)}, bf16[144,768]{1,0:T(8,128)(2,1)S(1)}, u32[]{:S(2)}, u32[]{:S(2)}) collective-permute-start(bf16[144,768]{1,0:T(8,128)(2,1)S(1)} %hidden_grad_keep.1), channel_id=1, source_target_pairs={{0,16},{8,24},{16,0},{24,8},{1,17},{9,25},{17,1},{25,9},{2,18},{10... | collective-permute-start | bytes 663560 | tf_op jit(solution)/shard_map/ppermute | solution.py:594
  78.1 4.6 %collective-permute-start.10 = (bf16[2,144,768]{2,1,0:T(8,128)(2,1)S(1)}, bf16[2,144,768]{2,1,0:T(8,128)(2,1)S(1)}, u32[]{:S(2)}, u32[]{:S(2)}) collective-permute-start(bf16[2,144,768]{2,1,0:T(8,128)(2,1)S(1)} %pad_maximum_fusion.mine_ref), channel_id=1, source_target_pairs={{0,8},{8,0},{16,24},{24,16},{1,9},{9,1},{17,25},{25,17},{2,10},{10... | collective-permute-start | bytes 1327112 | tf_op jit(solution)/shard_map/ppermute | solution.py:594
  78.2 10.8 %collective-permute-start.8 = (bf16[128,256]{1,0:T(8,128)(2,1)S(1)}, bf16[128,256]{1,0:T(8,128)(2,1)S(1)}, u32[]{:S(2)}, u32[]{:S(2)}) collective-permute-start(bf16[128,256]{1,0:T(8,128)(2,1)S(1)} %get-tuple-element.84), channel_id=1, source_target_pairs={{0,4},{1,5},{2,6},{3,7},{4,0},{5,1},{6,2},{7,3},{8,12},{9,13},{10,... | collective-permute-start | bytes 196616 | tf_op jit(solution)/shard_map/ppermute | solution.py:594
  80.8 8.2 %collective-permute-start.11 = (bf16[128,256]{1,0:T(8,128)(2,1)S(1)}, bf16[128,256]{1,0:T(8,128)(2,1)S(1)}, u32[]{:S(2)}, u32[]{:S(2)}) collective-permute-start(bf16[128,256]{1,0:T(8,128)(2,1)S(1)} %get-tuple-element.86), channel_id=1, source_target_pairs={{0,2},{1,3},{2,0},{3,1},{4,6},{5,7},{6,4},{7,5},{8,10},{9,11},{10,... | collective-permute-start | bytes 196616 | tf_op jit(solution)/shard_map/ppermute | solution.py:594
  82.3 18.1 %copy-start.5 = (s32[128,2]{0,1:T(2,128)S(1)}, s32[128,2]{0,1:T(2,128)}, u32[]{:S(2)}) copy-start(s32[128,2]{0,1:T(2,128)} %param.17) | copy-start | bytes 3076
  82.3 18.1 %copy-start.6 = (f32[128,2]{0,1:T(2,128)S(1)}, f32[128,2]{0,1:T(2,128)}, u32[]{:S(2)}) copy-start(f32[128,2]{0,1:T(2,128)} %param.18) | copy-start | bytes 3076
  82.3 6.7 %collective-permute-start.12 = (bf16[128,256]{1,0:T(8,128)(2,1)S(1)}, bf16[128,256]{1,0:T(8,128)(2,1)S(1)}, u32[]{:S(2)}, u32[]{:S(2)}) collective-permute-start(bf16[128,256]{1,0:T(8,128)(2,1)S(1)} %get-tuple-element.85), channel_id=1, source_target_pairs={{0,6},{1,7},{2,4},{3,5},{4,2},{5,3},{6,0},{7,1},{8,14},{9,15},{10,... | collective-permute-start | bytes 196616 | tf_op jit(solution)/shard_map/ppermute | solution.py:594
  89.1 19.8 %all-to-all-start.3 = ((bf16[8,32,1152]{2,1,0:T(8,128)(2,1)}), bf16[8,32,1152]{2,1,0:T(8,128)(2,1)S(1)}, u32[]{:S(2)}, u32[]{:S(2)}) async-start(bf16[8,32,1152]{2,1,0:T(8,128)(2,1)} %bitcast.75), calls=%async_computation.3 | async-start | bytes 1179648 | tf_op jit(solution)/shard_map/all_to_all | solution.py:665

commit v4 on v3

--- a/solution.py
+++ b/solution.py
@@ -586,7 +586,7 @@
             tokens * heads * seq // parts,
         ),
         name="attention",
-    )(me, in_hbm(queries), in_hbm(attn_grad), in_hbm(kv_near), in_hbm(kv_far), *(() if first else (carried[2], carried[0], carried[1])))
+    )(me, in_hbm(queries), in_hbm(attn_grad), in_hbm(kv_near), kv_far, *(() if first else (carried[2], carried[0], carried[1])))
 
 
 def swap(value, axis, bit):
@@ -704,12 +704,14 @@
     kv_recv = swap(kv_send, "exp", 1)
     hidden = activate(*total_of(gate_up_sum))
     hidden_other = swap(hidden, "ctx", 1)
-    hg_send, rows = hidden_grad_send(slots, order[::-1], after(recv_scaled, hidden), down_proj)
+    out_rows = route_out(slots, order, hidden, hidden_other, down_proj)
+    back_out = exchange(out_rows).reshape(slots.total, slots.columns)
+
+    hg_send, rows = hidden_grad_send(slots, order[::-1], after(recv_scaled, out_rows), down_proj)
     hg_recv = swap(hg_send, "ctx", 1)
-    out_rows = route_out(slots, order, after(hidden, hg_send), hidden_other, down_proj)
-    back_out = exchange(after(out_rows, kv_recv)).reshape(slots.total, slots.columns)
-
-    hg_part = hidden_grad_keep(mine, after(rows, out_rows), down_proj, hg_recv)
+    hg_part = hidden_grad_keep(mine, rows, down_proj, hg_recv)
+    held = hold(mine, after(gate_proj, hg_part), up_proj)
+
     kv_sum = kv_keep + after(kv_recv, hg_part).astype(F32)
     kv_low = kv_sum.astype(BF16)
     blocks = exp_count // 2
@@ -718,7 +720,6 @@
     ]
     gate_up_sum = [after(value, hg_part) for value in gate_up_sum]
     gate_up_total = total_of(gate_up_sum)
-    held = hold(mine, after(gate_proj, hg_part), up_proj)
     hg_sum, _ = spread_sum(hg_part, ctx_count, lambda part: (kv_low, gate_up_total, held))
     back = gate_backward(total_of(hg_sum), *gate_up_total)
     back_other = swap(back, "ctx", 1)

time: 111 us -> 110 us (level)
  local copies, waits for them, and re-layouts: 3.33 us -> 0.96 us
    unnamed x18 -> x10, local copies, waits for them, and re-layouts: 2.39 us -> 0.02 us
    ppermute x13, waiting for transfers between devices: 11.5 us -> 13.3 us  [swap(): return lax.ppermute(value, axis, [(i, i ^ bit) for i in range(count)])]
  transfers between devices with their start and end apart: 17 -> 17, of which waited for: 8 -> 8; matrix products, arithmetic and copies ran while one was open for 6% -> 7% of each run, Pallas kernels for 31% -> 31%
where the time goes in v4:
time: 110 us; the launch traced here: 109 us
  Pallas kernels  37.7 us (34%)
  starting transfers between devices  36 us (33%)
  waiting for transfers between devices  20.7 us (19%)
  other arithmetic  7.23 us (7%)
  blocking collectives  5.77 us (5%)
    all_to_all x4, starting transfers between devices, exchange(): return lax.all_to_all(flat, 'exp', split_axis=0, concat_axis=0, tiled=True)  19.5 us
    ppermute x13, starting transfers between devices, swap(): return lax.ppermute(value, axis, [(i, i ^ bit) for i in range(count)])  16.5 us
    ppermute x13, waiting for transfers between devices, swap(): return lax.ppermute(value, axis, [(i, i ^ bit) for i in range(count)])  13.3 us
    pallas_call x6, Pallas kernels, expert_call(): pl.pallas_call(kernel, in_specs=specs, out_specs=[in_vmem] * len(out_shap...  11.8 us
    pallas_call x1, Pallas kernels, attention(): pl.pallas_call(functools.partial(attention_kernel, offsets, tokens, chunk...  9.83 us
    all_to_all x4, waiting for transfers between devices, exchange(): return lax.all_to_all(flat, 'exp', split_axis=0, concat_axis=0, tiled=True)  7.46 us
    all_gather x1, blocking collectives, body(): lax.all_gather(after(kv_total, in_rows), 'ctx', axis=0, tiled=False)  5.77 us
    pallas_call x2, Pallas kernels, dispatch(): pl.pallas_call(functools.partial(dispatch_kernel, slots, weighted), out_s...  4.89 us
  transfers between devices with their start and end apart: 17, of which 8 were waited for; matrix products, arithmetic and copies ran while one was open for 7% of the time, Pallas kernels for 31%

profile of v4, /device:TPU:0, one launch (start us, length us, event | category | flops | bytes accessed | tf_op | source)
XLA Modules:
  0.0 109.3 jit_solution(18264842098223950144)
XLA Ops:
  1.4 4.1 %collective-permute-start = (bf16[128,256]{1,0:T(8,128)(2,1)S(1)}, bf16[128,256]{1,0:T(8,128)(2,1)S(1)}, u32[]{:S(2)}, u32[]{:S(2)}) collective-permute-start(bf16[128,256]{1,0:T(8,128)(2,1)S(1)} %pad_maximum_fusion.5), channel_id=1, source_target_pairs={{0,4},{1,5},{2,6},{3,7},{4,0},{5,1},{6,2},{7,3},{8,12},{9,13},{10,... | collective-permute-start | bytes 196616 | tf_op jit(solution)/shard_map/ppermute | solution.py:594
  5.5 2.4 %dispatch_rows.1 = bf16[256,1152]{1,0:T(8,128)(2,1)} custom-call(s32[2,128]{1,0:T(2,128)} %bitcast.66, f32[2,128]{1,0:T(2,128)} %bitcast.70, bf16[128,1024]{1,0:T(8,128)(2,1)} %rows_ref.1), custom_call_target="tpu_custom_call" | custom-call | flops 134217728 | bytes 1179648 | tf_op jit(solution)/shard_map/dispatch_rows/pallas_call | solution.py:130
  7.9 1.3 %collective-permute-done = bf16[128,256]{1,0:T(8,128)(2,1)S(1)} collective-permute-done((bf16[128,256]{1,0:T(8,128)(2,1)S(1)}, bf16[128,256]{1,0:T(8,128)(2,1)S(1)}, u32[]{:S(2)}, u32[]{:S(2)}) %collective-permute-start) | collective-permute-done | bytes 65568 | tf_op jit(solution)/shard_map/ppermute | solution.py:594
  9.2 5.6 %all-to-all-start = ((bf16[8,32,1152]{2,1,0:T(8,128)(2,1)}), bf16[8,32,1152]{2,1,0:T(8,128)(2,1)}, u32[]{:S(2)}, u32[]{:S(2)}) async-start(bf16[8,32,1152]{2,1,0:T(8,128)(2,1)} %bitcast.4), calls=%async_computation | async-start | bytes 1179648 | tf_op jit(solution)/shard_map/all_to_all | solution.py:665
  14.8 2.0 %collective-permute-start.1 = (bf16[256,256]{1,0:T(8,128)(2,1)S(1)}, bf16[256,256]{1,0:T(8,128)(2,1)}, u32[]{:S(2)}, u32[]{:S(2)}) collective-permute-start(bf16[256,256]{1,0:T(8,128)(2,1)S(1)} %pad_maximum_fusion.2), channel_id=1, source_target_pairs={{0,2},{1,3},{2,0},{3,1},{4,6},{5,7},{6,4},{7,5},{8,10},{9,11},{10,... | collective-permute-start | bytes 393224 | tf_op jit(solution)/shard_map/ppermute | solution.py:594
  17.0 2.5 %dispatch_scaled.1 = bf16[256,1152]{1,0:T(8,128)(2,1)} custom-call(s32[2,128]{1,0:T(2,128)} %bitcast.67, f32[2,128]{1,0:T(2,128)} %bitcast.71, bf16[128,1024]{1,0:T(8,128)(2,1)} %rows_ref.2), custom_call_target="tpu_custom_call" | custom-call | flops 134217728 | bytes 1179648 | tf_op jit(solution)/shard_map/dispatch_scaled/pallas_call | solution.py:130
  19.5 1.9 %hold_weights.2.held_ref = bf16[2,1024,768]{2,1,0:T(8,128)(2,1)S(1)} custom-call(s32[1]{0:T(128)S(6)} %sub.8.expert_ref, bf16[2,1024,768]{2,1,0:T(8,128)(2,1)} %gate_ref.5, bf16[2,1024,768]{2,1,0:T(8,128)(2,1)} %up_ref.7), custom_call_target="tpu_custom_call" | custom-call | tf_op jit(solution)/shard_map/hold_weights/pallas_call | solution.py:257
  21.4 6.3 %collective-permute-done.1 = bf16[256,256]{1,0:T(8,128)(2,1)} collective-permute-done((bf16[256,256]{1,0:T(8,128)(2,1)S(1)}, bf16[256,256]{1,0:T(8,128)(2,1)}, u32[]{:S(2)}, u32[]{:S(2)}) %collective-permute-start.1) | collective-permute-done | bytes 131104 | tf_op jit(solution)/shard_map/ppermute | solution.py:594
  27.8 1.6 %pad_maximum_fusion.1.kv_ref = bf16[512,256]{1,0:T(8,128)(2,1)} fusion(bf16[256,256]{1,0:T(8,128)(2,1)} %collective-permute-done.1, bf16[128,256]{1,0:T(8,128)(2,1)S(1)} %collective-permute-done, bf16[128,128]{1,0:T(8,128)(2,1)S(1)} %get-tuple-element.81, bf16[128,128]{1,0:T(8,128)(2,1)S(1)} %get-tuple-element.82), kind=kLoop, calls=%fused_computation.17 | loop fusion | flops 1048576 | bytes 524288 | tf_op jit(solution)/shard_map/concatenate | solution.py:683
  30.6 2.6 %gate_up_send.1 = (bf16[2,144,768]{2,1,0:T(8,128)(2,1)S(1)}, bf16[2,1024,768]{2,1,0:T(8,128)(2,1)S(1)}, bf16[144,1024]{1,0:T(8,128)(2,1)S(1)}) custom-call(s32[2]{0:T(128)S(1)} %rev.4.order_ref, bf16[8,2,16,1152]{3,2,1,0:T(8,128)(2,1)} %bitcast.5.recv_ref, bf16[2,1024,768]{2,1,0:T(8,128)(2,1)S(1)} %hold_weights.2.held_ref, bf16[2,1024,768]{2,1,0:T(8,128)(2,1)} %gate_ref.5, ...), custom_call_target="tpu_custom_call" | custom-call | tf_op jit(solution)/shard_map/gate_up_send/pallas_call | solution.py:257
  33.4 1.5 %collective-permute-start.3 = (bf16[512,256]{1,0:T(8,128)(2,1)}, bf16[512,256]{1,0:T(8,128)(2,1)S(1)}, u32[]{:S(2)}, u32[]{:S(2)}) collective-permute-start(bf16[512,256]{1,0:T(8,128)(2,1)} %pad_maximum_fusion.1.kv_ref), channel_id=1, source_target_pairs={{0,1},{1,0},{2,3},{3,2},{4,5},{5,4},{6,7},{7,6},{8,9},{9,8},{10,11... | collective-permute-start | bytes 786440 | tf_op jit(solution)/shard_map/ppermute | solution.py:594
  35.1 1.4 %gate_up_keep.1 = bf16[2,144,768]{2,1,0:T(8,128)(2,1)} custom-call(bf16[144,1024]{1,0:T(8,128)(2,1)S(1)} %get-tuple-element.42.rows_ref, bf16[2,1024,768]{2,1,0:T(8,128)(2,1)S(1)} %get-tuple-element.43.held_ref, bf16[2,144,768]{2,1,0:T(8,128)(2,1)S(1)} %collective-permute-done.2.arrived_ref), custom_call_target="tpu_custom_call" | custom-call | tf_op jit(solution)/shard_map/gate_up_keep/pallas_call | solution.py:257
  36.5 1.5 %collective-permute-start.5 = (bf16[2,144,768]{2,1,0:T(8,128)(2,1)}, bf16[2,144,768]{2,1,0:T(8,128)(2,1)}, u32[]{:S(2)}, u32[]{:S(2)}) collective-permute-start(bf16[2,144,768]{2,1,0:T(8,128)(2,1)} %gate_up_keep.1), channel_id=1, source_target_pairs={{0,16},{8,24},{16,0},{24,8},{1,17},{9,25},{17,1},{25,9},{2,18},{10... | collective-permute-start | bytes 1327112 | tf_op jit(solution)/shard_map/ppermute | solution.py:594
  38.1 5.0 %all-to-all-start.1 = ((bf16[8,32,1152]{2,1,0:T(8,128)(2,1)}), bf16[8,32,1152]{2,1,0:T(8,128)(2,1)}, u32[]{:S(2)}, u32[]{:S(2)}) async-start(bf16[8,32,1152]{2,1,0:T(8,128)(2,1)} %bitcast.6), calls=%async_computation.1 | async-start | bytes 1179648 | tf_op jit(solution)/shard_map/all_to_all | solution.py:665
  43.1 9.8 %attention.1 = (bf16[128,2048]{1,0:T(8,128)(2,1)}, bf16[128,2048]{1,0:T(8,128)(2,1)}, f32[512,256]{1,0:T(8,128)S(1)}, bf16[512,256]{1,0:T(8,128)(2,1)}) custom-call(s32[1]{0:T(128)} %bitcast.me_ref, bf16[128,2048]{1,0:T(8,128)(2,1)} %q_ref, bf16[128,2048]{1,0:T(8,128)(2,1)} %g_ref.1, bf16[512,256]{1,0:T(8,128)(2,1)} %pad_maximum_fusion.1.kv_ref, ...), custom_call_target="tpu_custom_call" | custom-call | flops 3221225472 | bytes 2097152 | tf_op jit(solution)/shard_map/attention/pallas_call | solution.py:564
  52.9 1.4 %convert_add_fusion.1 = f32[2,144,768]{2,1,0:T(8,128)S(1)} fusion(bf16[2,144,768]{2,1,0:T(8,128)(2,1)} %collective-permute-done.5, bf16[2,144,768]{2,1,0:T(8,128)(2,1)} %gate_up_keep.1), kind=kLoop, calls=%fused_computation.1 | loop fusion | flops 663552 | bytes 1769472 | tf_op jit(solution)/shard_map/add | solution.py:625
  54.6 2.1 %collective-permute-start.4 = (bf16[512,256]{1,0:T(8,128)(2,1)}, bf16[512,256]{1,0:T(8,128)(2,1)}, u32[]{:S(2)}, u32[]{:S(2)}) collective-permute-start(bf16[512,256]{1,0:T(8,128)(2,1)} %get-tuple-element.49), channel_id=1, source_target_pairs={{0,1},{1,0},{2,3},{3,2},{4,5},{5,4},{6,7},{7,6},{8,9},{9,8},{10,11... | collective-permute-start | bytes 786440 | tf_op jit(solution)/shard_map/ppermute | solution.py:594
  56.7 2.2 %route_out.1 = bf16[8,2,16,1152]{3,2,1,0:T(8,128)(2,1)} custom-call(s32[2]{0:T(128)S(1)} %pad_add_fusion.order_ref, bf16[144,768]{1,0:T(8,128)(2,1)S(1)} %fusion.5.mine_ref, bf16[144,768]{1,0:T(8,128)(2,1)S(1)} %collective-permute-done.6.other_ref, bf16[2,768,1024]{2,1,0:T(8,128)(2,1)S(1)} %copy-done), custom_call_target="tpu_custom_call" | custom-call | tf_op jit(solution)/shard_map/route_out/pallas_call | solution.py:364
  59.1 2.4 %hidden_grad_send.1 = (bf16[144,768]{1,0:T(8,128)(2,1)}, bf16[144,1024]{1,0:T(8,128)(2,1)S(1)}) custom-call(s32[2]{0:T(128)S(1)} %rev.4.order_ref, bf16[8,2,16,1152]{3,2,1,0:T(8,128)(2,1)} %bitcast.7.recv_ref, bf16[2,768,1024]{2,1,0:T(8,128)(2,1)S(1)} %copy-done), custom_call_target="tpu_custom_call" | custom-call | tf_op jit(solution)/shard_map/hidden_grad_send/pallas_call | solution.py:257
  61.5 5.4 %all-to-all-start.2 = ((bf16[8,32,1152]{2,1,0:T(8,128)(2,1)}), bf16[8,32,1152]{2,1,0:T(8,128)(2,1)}, u32[]{:S(2)}, u32[]{:S(2)}) async-start(bf16[8,32,1152]{2,1,0:T(8,128)(2,1)} %bitcast.74), calls=%async_computation.2 | async-start | bytes 1179648 | tf_op jit(solution)/shard_map/all_to_all | solution.py:665
  66.8 1.6 %hidden_grad_keep.1 = bf16[144,768]{1,0:T(8,128)(2,1)S(1)} custom-call(s32[1]{0:T(128)} %bitcast.1.expert_ref, bf16[144,1024]{1,0:T(8,128)(2,1)S(1)} %get-tuple-element.53.rows_ref, bf16[2,768,1024]{2,1,0:T(8,128)(2,1)S(1)} %copy-done, bf16[144,768]{1,0:T(8,128)(2,1)} %collective-permute-done.7.arrived_ref), custom_call_target="tpu_custom_call" | custom-call | tf_op jit(solution)/shard_map/hidden_grad_keep/pallas_call | solution.py:257
  69.0 1.9 %hold_weights.3.held_ref = bf16[2,1024,768]{2,1,0:T(8,128)(2,1)S(1)} custom-call(s32[1]{0:T(128)} %bitcast.1.expert_ref, bf16[2,1024,768]{2,1,0:T(8,128)(2,1)} %gate_ref.5, bf16[2,1024,768]{2,1,0:T(8,128)(2,1)} %up_ref.7), custom_call_target="tpu_custom_call" | custom-call | tf_op jit(solution)/shard_map/hold_weights/pallas_call | solution.py:257
  73.2 2.7 %collective-permute-done.9 = bf16[144,768]{1,0:T(8,128)(2,1)S(1)} collective-permute-done((bf16[144,768]{1,0:T(8,128)(2,1)S(1)}, bf16[144,768]{1,0:T(8,128)(2,1)S(1)}, u32[]{:S(2)}, u32[]{:S(2)}) %collective-permute-start.9) | collective-permute-done | bytes 221216 | tf_op jit(solution)/shard_map/ppermute | solution.py:594
  76.3 2.7 %collective-permute-start.8 = (bf16[128,256]{1,0:T(8,128)(2,1)S(1)}, bf16[128,256]{1,0:T(8,128)(2,1)S(1)}, u32[]{:S(2)}, u32[]{:S(2)}) collective-permute-start(bf16[128,256]{1,0:T(8,128)(2,1)S(1)} %get-tuple-element.78), channel_id=1, source_target_pairs={{0,4},{1,5},{2,6},{3,7},{4,0},{5,1},{6,2},{7,3},{8,12},{9,13},{10,... | collective-permute-start | bytes 196616 | tf_op jit(solution)/shard_map/ppermute | solution.py:594
  79.0 1.5 %collective-permute-start.11 = (bf16[128,256]{1,0:T(8,128)(2,1)S(1)}, bf16[128,256]{1,0:T(8,128)(2,1)S(1)}, u32[]{:S(2)}, u32[]{:S(2)}) collective-permute-start(bf16[128,256]{1,0:T(8,128)(2,1)S(1)} %get-tuple-element.80), channel_id=1, source_target_pairs={{0,2},{1,3},{2,0},{3,1},{4,6},{5,7},{6,4},{7,5},{8,10},{9,11},{10,... | collective-permute-start | bytes 196616 | tf_op jit(solution)/shard_map/ppermute | solution.py:594
  80.8 4.7 %route_in.1 = bf16[8,2,16,1152]{3,2,1,0:T(8,128)(2,1)} custom-call(s32[2]{0:T(128)S(1)} %pad_add_fusion.order_ref, bf16[2,144,768]{2,1,0:T(8,128)(2,1)S(1)} %pad_maximum_fusion.mine_ref, bf16[2,144,768]{2,1,0:T(8,128)(2,1)S(1)} %collective-permute-done.10.other_ref, bf16[2,1024,768]{2,1,0:T(8,128)(2,1)S(1)} %hold_weights.3.held_ref, ...), custom_call_target="tpu_custom_call" | custom-call | tf_op jit(solution)/shard_map/route_in/pallas_call | solution.py:400
  85.5 2.7 %collective-permute-done.8 = bf16[128,256]{1,0:T(8,128)(2,1)S(1)} collective-permute-done((bf16[128,256]{1,0:T(8,128)(2,1)S(1)}, bf16[128,256]{1,0:T(8,128)(2,1)S(1)}, u32[]{:S(2)}, u32[]{:S(2)}) %collective-permute-start.8) | collective-permute-done | bytes 65568 | tf_op jit(solution)/shard_map/ppermute | solution.py:594
  88.3 3.5 %all-to-all-start.3 = ((bf16[8,32,1152]{2,1,0:T(8,128)(2,1)}), bf16[8,32,1152]{2,1,0:T(8,128)(2,1)S(1)}, u32[]{:S(2)}, u32[]{:S(2)}) async-start(bf16[8,32,1152]{2,1,0:T(8,128)(2,1)} %bitcast.75), calls=%async_computation.3 | async-start | bytes 1179648 | tf_op jit(solution)/shard_map/all_to_all | solution.py:665
  91.8 2.7 %combine_out.1 = bf16[128,1024]{1,0:T(8,128)(2,1)} custom-call(s32[2,128]{1,0:T(2,128)S(1)} %bitcast.68, f32[2,128]{1,0:T(2,128)S(1)} %bitcast.72, bf16[256,1152]{1,0:T(8,128)(2,1)} %bitcast.24.back_ref), custom_call_target="tpu_custom_call" | custom-call | flops 268435456 | bytes 1179648 | tf_op jit(solution)/shard_map/combine_out/pallas_call | solution.py:174
  94.5 5.8 %all-gather = bf16[512,256]{1,0:T(8,128)(2,1)S(1)} all-gather(bf16[128,256]{1,0:T(8,128)(2,1)S(1)} %fusion.10), channel_id=2, replica_groups=mesh['ctx'=4,'exp'=8] {'ctx'}, dimensions={0}, use_global_device_ids=true | all-gather | bytes 327680 | tf_op jit(solution)/shard_map/all_gather | solution.py:736
  101.7 6.0 %all-to-all-done.3 = bf16[8,32,1152]{2,1,0:T(8,128)(2,1)S(1)} async-done(((bf16[8,32,1152]{2,1,0:T(8,128)(2,1)}), bf16[8,32,1152]{2,1,0:T(8,128)(2,1)S(1)}, u32[]{:S(2)}, u32[]{:S(2)}) %all-to-all-start.3) | async-done | bytes 589856 | tf_op jit(solution)/shard_map/all_to_all | solution.py:665
  107.7 1.5 %combine_in.1 = bf16[128,1024]{1,0:T(8,128)(2,1)} custom-call(s32[2,128]{1,0:T(2,128)S(1)} %bitcast.69, f32[2,128]{1,0:T(2,128)S(1)} %bitcast.73, bf16[256,1152]{1,0:T(8,128)(2,1)S(1)} %bitcast.65), custom_call_target="tpu_custom_call" | custom-call | flops 268435456 | bytes 1179648 | tf_op jit(solution)/shard_map/combine_in/pallas_call | solution.py:174
  (43 shorter events, 7.9 us)
Async XLA Ops:
  1.4 7.8 %collective-permute-start = (bf16[128,256]{1,0:T(8,128)(2,1)S(1)}, bf16[128,256]{1,0:T(8,128)(2,1)S(1)}, u32[]{:S(2)}, u32[]{:S(2)}) collective-permute-start(bf16[128,256]{1,0:T(8,128)(2,1)S(1)} %pad_maximum_fusion.5), channel_id=1, source_target_pairs={{0,4},{1,5},{2,6},{3,7},{4,0},{5,1},{6,2},{7,3},{8,12},{9,13},{10,... | collective-permute-start | bytes 196616 | tf_op jit(solution)/shard_map/ppermute | solution.py:594
  9.2 21.4 %all-to-all-start = ((bf16[8,32,1152]{2,1,0:T(8,128)(2,1)}), bf16[8,32,1152]{2,1,0:T(8,128)(2,1)}, u32[]{:S(2)}, u32[]{:S(2)}) async-start(bf16[8,32,1152]{2,1,0:T(8,128)(2,1)} %bitcast.4), calls=%async_computation | async-start | bytes 1179648 | tf_op jit(solution)/shard_map/all_to_all | solution.py:665
  14.8 13.0 %collective-permute-start.1 = (bf16[256,256]{1,0:T(8,128)(2,1)S(1)}, bf16[256,256]{1,0:T(8,128)(2,1)}, u32[]{:S(2)}, u32[]{:S(2)}) collective-permute-start(bf16[256,256]{1,0:T(8,128)(2,1)S(1)} %pad_maximum_fusion.2), channel_id=1, source_target_pairs={{0,2},{1,3},{2,0},{3,1},{4,6},{5,7},{6,4},{7,5},{8,10},{9,11},{10,... | collective-permute-start | bytes 393224 | tf_op jit(solution)/shard_map/ppermute | solution.py:594
  33.3 1.9 %collective-permute-start.2 = (bf16[2,144,768]{2,1,0:T(8,128)(2,1)S(1)}, bf16[2,144,768]{2,1,0:T(8,128)(2,1)S(1)}, u32[]{:S(2)}, u32[]{:S(2)}) collective-permute-start(bf16[2,144,768]{2,1,0:T(8,128)(2,1)S(1)} %get-tuple-element.44), channel_id=1, source_target_pairs={{0,8},{8,0},{16,24},{24,16},{1,9},{9,1},{17,25},{25,17},{2,10},{10... | collective-permute-start | bytes 1327112 | tf_op jit(solution)/shard_map/ppermute | solution.py:594
  33.4 9.7 %collective-permute-start.3 = (bf16[512,256]{1,0:T(8,128)(2,1)}, bf16[512,256]{1,0:T(8,128)(2,1)S(1)}, u32[]{:S(2)}, u32[]{:S(2)}) collective-permute-start(bf16[512,256]{1,0:T(8,128)(2,1)} %pad_maximum_fusion.1.kv_ref), channel_id=1, source_target_pairs={{0,1},{1,0},{2,3},{3,2},{4,5},{5,4},{6,7},{7,6},{8,9},{9,8},{10,11... | collective-permute-start | bytes 786440 | tf_op jit(solution)/shard_map/ppermute | solution.py:594
  36.5 16.4 %collective-permute-start.5 = (bf16[2,144,768]{2,1,0:T(8,128)(2,1)}, bf16[2,144,768]{2,1,0:T(8,128)(2,1)}, u32[]{:S(2)}, u32[]{:S(2)}) collective-permute-start(bf16[2,144,768]{2,1,0:T(8,128)(2,1)} %gate_up_keep.1), channel_id=1, source_target_pairs={{0,16},{8,24},{16,0},{24,8},{1,17},{9,25},{17,1},{25,9},{2,18},{10... | collective-permute-start | bytes 1327112 | tf_op jit(solution)/shard_map/ppermute | solution.py:594
  38.1 21.0 %all-to-all-start.1 = ((bf16[8,32,1152]{2,1,0:T(8,128)(2,1)}), bf16[8,32,1152]{2,1,0:T(8,128)(2,1)}, u32[]{:S(2)}, u32[]{:S(2)}) async-start(bf16[8,32,1152]{2,1,0:T(8,128)(2,1)} %bitcast.6), calls=%async_computation.1 | async-start | bytes 1179648 | tf_op jit(solution)/shard_map/all_to_all | solution.py:665
  43.1 13.6 %copy-start = (bf16[2,768,1024]{2,1,0:T(8,128)(2,1)S(1)}, bf16[2,768,1024]{2,1,0:T(8,128)(2,1)}, u32[]{:S(2)}) copy-start(bf16[2,768,1024]{2,1,0:T(8,128)(2,1)} %down_ref.5) | copy-start | bytes 9437188
  52.9 3.7 %copy-start.1 = (f32[512,256]{1,0:T(8,128)}, f32[512,256]{1,0:T(8,128)S(1)}, u32[]{:S(2)}) copy-start(f32[512,256]{1,0:T(8,128)S(1)} %get-tuple-element.48) | copy-start | bytes 1572868
  54.5 2.2 %collective-permute-start.6 = (bf16[144,768]{1,0:T(8,128)(2,1)S(1)}, bf16[144,768]{1,0:T(8,128)(2,1)S(1)}, u32[]{:S(2)}, u32[]{:S(2)}) collective-permute-start(bf16[144,768]{1,0:T(8,128)(2,1)S(1)} %fusion.5.mine_ref), channel_id=1, source_target_pairs={{0,8},{8,0},{16,24},{24,16},{1,9},{9,1},{17,25},{25,17},{2,10},{10... | collective-permute-start | bytes 663560 | tf_op jit(solution)/shard_map/ppermute | solution.py:594
  54.6 16.3 %collective-permute-start.4 = (bf16[512,256]{1,0:T(8,128)(2,1)}, bf16[512,256]{1,0:T(8,128)(2,1)}, u32[]{:S(2)}, u32[]{:S(2)}) collective-permute-start(bf16[512,256]{1,0:T(8,128)(2,1)} %get-tuple-element.49), channel_id=1, source_target_pairs={{0,1},{1,0},{2,3},{3,2},{4,5},{5,4},{6,7},{7,6},{8,9},{9,8},{10,11... | collective-permute-start | bytes 786440 | tf_op jit(solution)/shard_map/ppermute | solution.py:594
  61.5 5.4 %collective-permute-start.7 = (bf16[144,768]{1,0:T(8,128)(2,1)}, bf16[144,768]{1,0:T(8,128)(2,1)}, u32[]{:S(2)}, u32[]{:S(2)}) collective-permute-start(bf16[144,768]{1,0:T(8,128)(2,1)} %get-tuple-element.54), channel_id=1, source_target_pairs={{0,8},{8,0},{16,24},{24,16},{1,9},{9,1},{17,25},{25,17},{2,10},{10... | collective-permute-start | bytes 663560 | tf_op jit(solution)/shard_map/ppermute | solution.py:594
  61.5 26.8 %all-to-all-start.2 = ((bf16[8,32,1152]{2,1,0:T(8,128)(2,1)}), bf16[8,32,1152]{2,1,0:T(8,128)(2,1)}, u32[]{:S(2)}, u32[]{:S(2)}) async-start(bf16[8,32,1152]{2,1,0:T(8,128)(2,1)} %bitcast.74), calls=%async_computation.2 | async-start | bytes 1179648 | tf_op jit(solution)/shard_map/all_to_all | solution.py:665
  68.4 3.7 %copy-start.2 = (f32[512,256]{1,0:T(8,128)S(1)}, f32[512,256]{1,0:T(8,128)}, u32[]{:S(2)}) copy-start(f32[512,256]{1,0:T(8,128)} %copy-done.1) | copy-start | bytes 1572868
  68.4 7.5 %collective-permute-start.9 = (bf16[144,768]{1,0:T(8,128)(2,1)S(1)}, bf16[144,768]{1,0:T(8,128)(2,1)S(1)}, u32[]{:S(2)}, u32[]{:S(2)}) collective-permute-start(bf16[144,768]{1,0:T(8,128)(2,1)S(1)} %hidden_grad_keep.1), channel_id=1, source_target_pairs={{0,16},{8,24},{16,0},{24,8},{1,17},{9,25},{17,1},{25,9},{2,18},{10... | collective-permute-start | bytes 663560 | tf_op jit(solution)/shard_map/ppermute | solution.py:594
  76.2 4.6 %collective-permute-start.10 = (bf16[2,144,768]{2,1,0:T(8,128)(2,1)S(1)}, bf16[2,144,768]{2,1,0:T(8,128)(2,1)S(1)}, u32[]{:S(2)}, u32[]{:S(2)}) collective-permute-start(bf16[2,144,768]{2,1,0:T(8,128)(2,1)S(1)} %pad_maximum_fusion.mine_ref), channel_id=1, source_target_pairs={{0,8},{8,0},{16,24},{24,16},{1,9},{9,1},{17,25},{25,17},{2,10},{10... | collective-permute-start | bytes 1327112 | tf_op jit(solution)/shard_map/ppermute | solution.py:594
  76.3 11.9 %collective-permute-start.8 = (bf16[128,256]{1,0:T(8,128)(2,1)S(1)}, bf16[128,256]{1,0:T(8,128)(2,1)S(1)}, u32[]{:S(2)}, u32[]{:S(2)}) collective-permute-start(bf16[128,256]{1,0:T(8,128)(2,1)S(1)} %get-tuple-element.78), channel_id=1, source_target_pairs={{0,4},{1,5},{2,6},{3,7},{4,0},{5,1},{6,2},{7,3},{8,12},{9,13},{10,... | collective-permute-start | bytes 196616 | tf_op jit(solution)/shard_map/ppermute | solution.py:594
  79.0 9.2 %collective-permute-start.11 = (bf16[128,256]{1,0:T(8,128)(2,1)S(1)}, bf16[128,256]{1,0:T(8,128)(2,1)S(1)}, u32[]{:S(2)}, u32[]{:S(2)}) collective-permute-start(bf16[128,256]{1,0:T(8,128)(2,1)S(1)} %get-tuple-element.80), channel_id=1, source_target_pairs={{0,2},{1,3},{2,0},{3,1},{4,6},{5,7},{6,4},{7,5},{8,10},{9,11},{10,... | collective-permute-start | bytes 196616 | tf_op jit(solution)/shard_map/ppermute | solution.py:594
  80.5 11.3 %copy-start.3 = (s32[128,2]{0,1:T(2,128)S(1)}, s32[128,2]{0,1:T(2,128)}, u32[]{:S(2)}) copy-start(s32[128,2]{0,1:T(2,128)} %param.17) | copy-start | bytes 3076
  80.5 11.3 %copy-start.4 = (f32[128,2]{0,1:T(2,128)S(1)}, f32[128,2]{0,1:T(2,128)}, u32[]{:S(2)}) copy-start(f32[128,2]{0,1:T(2,128)} %param.18) | copy-start | bytes 3076
  80.5 7.7 %collective-permute-start.12 = (bf16[128,256]{1,0:T(8,128)(2,1)S(1)}, bf16[128,256]{1,0:T(8,128)(2,1)S(1)}, u32[]{:S(2)}, u32[]{:S(2)}) collective-permute-start(bf16[128,256]{1,0:T(8,128)(2,1)S(1)} %get-tuple-element.79), channel_id=1, source_target_pairs={{0,6},{1,7},{2,4},{3,5},{4,2},{5,3},{6,0},{7,1},{8,14},{9,15},{10,... | collective-permute-start | bytes 196616 | tf_op jit(solution)/shard_map/ppermute | solution.py:594
  88.3 19.5 %all-to-all-start.3 = ((bf16[8,32,1152]{2,1,0:T(8,128)(2,1)}), bf16[8,32,1152]{2,1,0:T(8,128)(2,1)S(1)}, u32[]{:S(2)}, u32[]{:S(2)}) async-start(bf16[8,32,1152]{2,1,0:T(8,128)(2,1)} %bitcast.75), calls=%async_computation.3 | async-start | bytes 1179648 | tf_op jit(solution)/shard_map/all_to_all | solution.py:665

commit v5 on v4

--- a/solution.py
+++ b/solution.py
@@ -13,6 +13,7 @@
 ROW_TILE = 16
 PAIRS = 4
 CHUNK = 512
+OVERLAP_FLOPS = 2.25e9
 SMALL_VMEM = 16 * 1024 * 1024
 LARGE_VMEM = 20 * 1024 * 1024
 EXPERT_VMEM = 16 * 1024 * 1024
@@ -175,7 +176,7 @@
         functools.partial(combine_kernel, slots, weighted),
         out_shape=jax.ShapeDtypeStruct((tokens, slots.width), BF16),
         compiler_params=pltpu.CompilerParams(vmem_limit_bytes=SMALL_VMEM),
-        cost_estimate=cost(8 * slots.total * LANES * slots.width, 4 * slots.total * slots.columns),
+        cost_estimate=cost(OVERLAP_FLOPS if weighted else 1e7, 4 * slots.total * slots.columns),
         name="combine_out" if weighted else "combine_in",
     )(ids, gains, back)
 
@@ -728,9 +729,9 @@
     for part in kv_parts:
         kv_total = kv_total + after(part, in_rows).astype(F32)
     kv_total = kv_total.astype(BF16)
-    back_in = exchange(after(in_rows, kv_total)).reshape(slots.total, slots.columns)
-
-    moe_out = combine(slots, True, ids, gains, after(back_out, in_rows))
+    back_in = exchange(in_rows).reshape(slots.total, slots.columns)
+
+    moe_out = combine(slots, True, ids, gains, after(back_out, kv_total))
     input_grad = combine(slots, False, ids, gains, back_in)
 
     kv_every = lax.all_gather(after(kv_total, in_rows), "ctx", axis=0, tiled=False)

time: 110 us -> 109 us (level)
  waiting for transfers between devices: 20.7 us -> 19.3 us
    ppermute x13, waiting for transfers between devices: 13.3 us -> 10.6 us  [swap(): return lax.ppermute(value, axis, [(i, i ^ bit) for i in range(count)])]
    all_to_all x4, waiting for transfers between devices: 7.46 us -> 8.72 us  [exchange(): return lax.all_to_all(flat, 'exp', split_axis=0, concat_axis=0, tiled=True)]
where the time goes in v5:
time: 109 us
  Pallas kernels  37.7 us (35%)
  starting transfers between devices  36.7 us (34%)
  waiting for transfers between devices  19.3 us (18%)
  other arithmetic  7.23 us (7%)
  blocking collectives  5.79 us (5%)
    all_to_all x4, starting transfers between devices, exchange(): return lax.all_to_all(flat, 'exp', split_axis=0, concat_axis=0, tiled=True)  20.2 us
    ppermute x13, starting transfers between devices, swap(): return lax.ppermute(value, axis, [(i, i ^ bit) for i in range(count)])  16.5 us
    pallas_call x6, Pallas kernels, expert_call(): pl.pallas_call(kernel, in_specs=specs, out_specs=[in_vmem] * len(out_shap...  11.8 us
    ppermute x13, waiting for transfers between devices, swap(): return lax.ppermute(value, axis, [(i, i ^ bit) for i in range(count)])  10.6 us
    pallas_call x1, Pallas kernels, attention(): pl.pallas_call(functools.partial(attention_kernel, offsets, tokens, chunk...  9.83 us
    all_to_all x4, waiting for transfers between devices, exchange(): return lax.all_to_all(flat, 'exp', split_axis=0, concat_axis=0, tiled=True)  8.72 us
    all_gather x1, blocking collectives, body(): lax.all_gather(after(kv_total, in_rows), 'ctx', axis=0, tiled=False)  5.79 us
    pallas_call x2, Pallas kernels, dispatch(): pl.pallas_call(functools.partial(dispatch_kernel, slots, weighted), out_s...  4.89 us
  transfers between devices with their start and end apart: 17, of which 8 were waited for; matrix products, arithmetic and copies ran while one was open for 7% of the time, Pallas kernels for 31%

profile of v5, /device:TPU:0, one launch (start us, length us, event | category | flops | bytes accessed | tf_op | source)
XLA Modules:
  0.0 108.5 jit_solution(7676368123670470226)
XLA Ops:
  1.4 4.1 %collective-permute-start = (bf16[128,256]{1,0:T(8,128)(2,1)S(1)}, bf16[128,256]{1,0:T(8,128)(2,1)S(1)}, u32[]{:S(2)}, u32[]{:S(2)}) collective-permute-start(bf16[128,256]{1,0:T(8,128)(2,1)S(1)} %pad_maximum_fusion.5), channel_id=1, source_target_pairs={{0,4},{1,5},{2,6},{3,7},{4,0},{5,1},{6,2},{7,3},{8,12},{9,13},{10,... | collective-permute-start | bytes 196616 | tf_op jit(solution)/shard_map/ppermute | solution.py:595
  5.5 2.4 %dispatch_rows.1 = bf16[256,1152]{1,0:T(8,128)(2,1)} custom-call(s32[2,128]{1,0:T(2,128)} %bitcast.66, f32[2,128]{1,0:T(2,128)} %bitcast.70, bf16[128,1024]{1,0:T(8,128)(2,1)} %rows_ref.1), custom_call_target="tpu_custom_call" | custom-call | flops 134217728 | bytes 1179648 | tf_op jit(solution)/shard_map/dispatch_rows/pallas_call | solution.py:131
  7.9 1.3 %collective-permute-done = bf16[128,256]{1,0:T(8,128)(2,1)S(1)} collective-permute-done((bf16[128,256]{1,0:T(8,128)(2,1)S(1)}, bf16[128,256]{1,0:T(8,128)(2,1)S(1)}, u32[]{:S(2)}, u32[]{:S(2)}) %collective-permute-start) | collective-permute-done | bytes 65568 | tf_op jit(solution)/shard_map/ppermute | solution.py:595
  9.2 5.6 %all-to-all-start = ((bf16[8,32,1152]{2,1,0:T(8,128)(2,1)}), bf16[8,32,1152]{2,1,0:T(8,128)(2,1)}, u32[]{:S(2)}, u32[]{:S(2)}) async-start(bf16[8,32,1152]{2,1,0:T(8,128)(2,1)} %bitcast.4), calls=%async_computation | async-start | bytes 1179648 | tf_op jit(solution)/shard_map/all_to_all | solution.py:666
  14.8 2.0 %collective-permute-start.1 = (bf16[256,256]{1,0:T(8,128)(2,1)S(1)}, bf16[256,256]{1,0:T(8,128)(2,1)}, u32[]{:S(2)}, u32[]{:S(2)}) collective-permute-start(bf16[256,256]{1,0:T(8,128)(2,1)S(1)} %pad_maximum_fusion.2), channel_id=1, source_target_pairs={{0,2},{1,3},{2,0},{3,1},{4,6},{5,7},{6,4},{7,5},{8,10},{9,11},{10,... | collective-permute-start | bytes 393224 | tf_op jit(solution)/shard_map/ppermute | solution.py:595
  17.0 2.5 %dispatch_scaled.1 = bf16[256,1152]{1,0:T(8,128)(2,1)} custom-call(s32[2,128]{1,0:T(2,128)} %bitcast.67, f32[2,128]{1,0:T(2,128)} %bitcast.71, bf16[128,1024]{1,0:T(8,128)(2,1)} %rows_ref.2), custom_call_target="tpu_custom_call" | custom-call | flops 134217728 | bytes 1179648 | tf_op jit(solution)/shard_map/dispatch_scaled/pallas_call | solution.py:131
  19.5 1.9 %hold_weights.2.held_ref = bf16[2,1024,768]{2,1,0:T(8,128)(2,1)S(1)} custom-call(s32[1]{0:T(128)S(6)} %sub.8.expert_ref, bf16[2,1024,768]{2,1,0:T(8,128)(2,1)} %gate_ref.5, bf16[2,1024,768]{2,1,0:T(8,128)(2,1)} %up_ref.7), custom_call_target="tpu_custom_call" | custom-call | tf_op jit(solution)/shard_map/hold_weights/pallas_call | solution.py:258
  21.4 6.3 %collective-permute-done.1 = bf16[256,256]{1,0:T(8,128)(2,1)} collective-permute-done((bf16[256,256]{1,0:T(8,128)(2,1)S(1)}, bf16[256,256]{1,0:T(8,128)(2,1)}, u32[]{:S(2)}, u32[]{:S(2)}) %collective-permute-start.1) | collective-permute-done | bytes 131104 | tf_op jit(solution)/shard_map/ppermute | solution.py:595
  27.8 1.6 %pad_maximum_fusion.1.kv_ref = bf16[512,256]{1,0:T(8,128)(2,1)} fusion(bf16[256,256]{1,0:T(8,128)(2,1)} %collective-permute-done.1, bf16[128,256]{1,0:T(8,128)(2,1)S(1)} %collective-permute-done, bf16[128,128]{1,0:T(8,128)(2,1)S(1)} %get-tuple-element.79, bf16[128,128]{1,0:T(8,128)(2,1)S(1)} %get-tuple-element.80), kind=kLoop, calls=%fused_computation.17 | loop fusion | flops 1048576 | bytes 524288 | tf_op jit(solution)/shard_map/concatenate | solution.py:684
  30.6 2.6 %gate_up_send.1 = (bf16[2,144,768]{2,1,0:T(8,128)(2,1)S(1)}, bf16[2,1024,768]{2,1,0:T(8,128)(2,1)S(1)}, bf16[144,1024]{1,0:T(8,128)(2,1)S(1)}) custom-call(s32[2]{0:T(128)S(1)} %rev.4.order_ref, bf16[8,2,16,1152]{3,2,1,0:T(8,128)(2,1)} %bitcast.5.recv_ref, bf16[2,1024,768]{2,1,0:T(8,128)(2,1)S(1)} %hold_weights.2.held_ref, bf16[2,1024,768]{2,1,0:T(8,128)(2,1)} %gate_ref.5, ...), custom_call_target="tpu_custom_call" | custom-call | tf_op jit(solution)/shard_map/gate_up_send/pallas_call | solution.py:258
  33.4 1.5 %collective-permute-start.3 = (bf16[512,256]{1,0:T(8,128)(2,1)}, bf16[512,256]{1,0:T(8,128)(2,1)S(1)}, u32[]{:S(2)}, u32[]{:S(2)}) collective-permute-start(bf16[512,256]{1,0:T(8,128)(2,1)} %pad_maximum_fusion.1.kv_ref), channel_id=1, source_target_pairs={{0,1},{1,0},{2,3},{3,2},{4,5},{5,4},{6,7},{7,6},{8,9},{9,8},{10,11... | collective-permute-start | bytes 786440 | tf_op jit(solution)/shard_map/ppermute | solution.py:595
  35.1 1.4 %gate_up_keep.1 = bf16[2,144,768]{2,1,0:T(8,128)(2,1)} custom-call(bf16[144,1024]{1,0:T(8,128)(2,1)S(1)} %get-tuple-element.41.rows_ref, bf16[2,1024,768]{2,1,0:T(8,128)(2,1)S(1)} %get-tuple-element.42.held_ref, bf16[2,144,768]{2,1,0:T(8,128)(2,1)S(1)} %collective-permute-done.2.arrived_ref), custom_call_target="tpu_custom_call" | custom-call | tf_op jit(solution)/shard_map/gate_up_keep/pallas_call | solution.py:258
  36.5 1.5 %collective-permute-start.5 = (bf16[2,144,768]{2,1,0:T(8,128)(2,1)}, bf16[2,144,768]{2,1,0:T(8,128)(2,1)}, u32[]{:S(2)}, u32[]{:S(2)}) collective-permute-start(bf16[2,144,768]{2,1,0:T(8,128)(2,1)} %gate_up_keep.1), channel_id=1, source_target_pairs={{0,16},{8,24},{16,0},{24,8},{1,17},{9,25},{17,1},{25,9},{2,18},{10... | collective-permute-start | bytes 1327112 | tf_op jit(solution)/shard_map/ppermute | solution.py:595
  38.1 5.0 %all-to-all-start.1 = ((bf16[8,32,1152]{2,1,0:T(8,128)(2,1)}), bf16[8,32,1152]{2,1,0:T(8,128)(2,1)}, u32[]{:S(2)}, u32[]{:S(2)}) async-start(bf16[8,32,1152]{2,1,0:T(8,128)(2,1)} %bitcast.6), calls=%async_computation.1 | async-start | bytes 1179648 | tf_op jit(solution)/shard_map/all_to_all | solution.py:666
  43.1 9.8 %attention.1 = (bf16[128,2048]{1,0:T(8,128)(2,1)}, bf16[128,2048]{1,0:T(8,128)(2,1)}, f32[512,256]{1,0:T(8,128)S(1)}, bf16[512,256]{1,0:T(8,128)(2,1)}) custom-call(s32[1]{0:T(128)} %bitcast.me_ref, bf16[128,2048]{1,0:T(8,128)(2,1)} %q_ref, bf16[128,2048]{1,0:T(8,128)(2,1)} %g_ref.1, bf16[512,256]{1,0:T(8,128)(2,1)} %pad_maximum_fusion.1.kv_ref, ...), custom_call_target="tpu_custom_call" | custom-call | flops 3221225472 | bytes 2097152 | tf_op jit(solution)/shard_map/attention/pallas_call | solution.py:565
  52.9 1.4 %convert_add_fusion.1 = f32[2,144,768]{2,1,0:T(8,128)S(1)} fusion(bf16[2,144,768]{2,1,0:T(8,128)(2,1)} %collective-permute-done.5, bf16[2,144,768]{2,1,0:T(8,128)(2,1)} %gate_up_keep.1), kind=kLoop, calls=%fused_computation.1 | loop fusion | flops 663552 | bytes 1769472 | tf_op jit(solution)/shard_map/add | solution.py:626
  54.6 2.1 %collective-permute-start.4 = (bf16[512,256]{1,0:T(8,128)(2,1)}, bf16[512,256]{1,0:T(8,128)(2,1)}, u32[]{:S(2)}, u32[]{:S(2)}) collective-permute-start(bf16[512,256]{1,0:T(8,128)(2,1)} %get-tuple-element.48), channel_id=1, source_target_pairs={{0,1},{1,0},{2,3},{3,2},{4,5},{5,4},{6,7},{7,6},{8,9},{9,8},{10,11... | collective-permute-start | bytes 786440 | tf_op jit(solution)/shard_map/ppermute | solution.py:595
  56.7 2.2 %route_out.1 = bf16[8,2,16,1152]{3,2,1,0:T(8,128)(2,1)} custom-call(s32[2]{0:T(128)S(1)} %pad_add_fusion.order_ref, bf16[144,768]{1,0:T(8,128)(2,1)S(1)} %fusion.5.mine_ref, bf16[144,768]{1,0:T(8,128)(2,1)S(1)} %collective-permute-done.6.other_ref, bf16[2,768,1024]{2,1,0:T(8,128)(2,1)S(1)} %copy-done), custom_call_target="tpu_custom_call" | custom-call | tf_op jit(solution)/shard_map/route_out/pallas_call | solution.py:365
  59.1 2.4 %hidden_grad_send.1 = (bf16[144,768]{1,0:T(8,128)(2,1)}, bf16[144,1024]{1,0:T(8,128)(2,1)S(1)}) custom-call(s32[2]{0:T(128)S(1)} %rev.4.order_ref, bf16[8,2,16,1152]{3,2,1,0:T(8,128)(2,1)} %bitcast.7.recv_ref, bf16[2,768,1024]{2,1,0:T(8,128)(2,1)S(1)} %copy-done), custom_call_target="tpu_custom_call" | custom-call | tf_op jit(solution)/shard_map/hidden_grad_send/pallas_call | solution.py:258
  61.5 5.4 %all-to-all-start.2 = ((bf16[8,32,1152]{2,1,0:T(8,128)(2,1)}), bf16[8,32,1152]{2,1,0:T(8,128)(2,1)}, u32[]{:S(2)}, u32[]{:S(2)}) async-start(bf16[8,32,1152]{2,1,0:T(8,128)(2,1)} %bitcast.74), calls=%async_computation.2 | async-start | bytes 1179648 | tf_op jit(solution)/shard_map/all_to_all | solution.py:666
  66.8 1.6 %hidden_grad_keep.1 = bf16[144,768]{1,0:T(8,128)(2,1)S(1)} custom-call(s32[1]{0:T(128)} %bitcast.1.expert_ref, bf16[144,1024]{1,0:T(8,128)(2,1)S(1)} %get-tuple-element.52.rows_ref, bf16[2,768,1024]{2,1,0:T(8,128)(2,1)S(1)} %copy-done, bf16[144,768]{1,0:T(8,128)(2,1)} %collective-permute-done.7.arrived_ref), custom_call_target="tpu_custom_call" | custom-call | tf_op jit(solution)/shard_map/hidden_grad_keep/pallas_call | solution.py:258
  69.0 1.9 %hold_weights.3.held_ref = bf16[2,1024,768]{2,1,0:T(8,128)(2,1)S(1)} custom-call(s32[1]{0:T(128)} %bitcast.1.expert_ref, bf16[2,1024,768]{2,1,0:T(8,128)(2,1)} %gate_ref.5, bf16[2,1024,768]{2,1,0:T(8,128)(2,1)} %up_ref.7), custom_call_target="tpu_custom_call" | custom-call | tf_op jit(solution)/shard_map/hold_weights/pallas_call | solution.py:258
  73.2 2.7 %collective-permute-done.9 = bf16[144,768]{1,0:T(8,128)(2,1)S(1)} collective-permute-done((bf16[144,768]{1,0:T(8,128)(2,1)S(1)}, bf16[144,768]{1,0:T(8,128)(2,1)S(1)}, u32[]{:S(2)}, u32[]{:S(2)}) %collective-permute-start.9) | collective-permute-done | bytes 221216 | tf_op jit(solution)/shard_map/ppermute | solution.py:595
  76.3 2.7 %collective-permute-start.8 = (bf16[128,256]{1,0:T(8,128)(2,1)S(1)}, bf16[128,256]{1,0:T(8,128)(2,1)S(1)}, u32[]{:S(2)}, u32[]{:S(2)}) collective-permute-start(bf16[128,256]{1,0:T(8,128)(2,1)S(1)} %get-tuple-element.76), channel_id=1, source_target_pairs={{0,4},{1,5},{2,6},{3,7},{4,0},{5,1},{6,2},{7,3},{8,12},{9,13},{10,... | collective-permute-start | bytes 196616 | tf_op jit(solution)/shard_map/ppermute | solution.py:595
  79.0 1.5 %collective-permute-start.11 = (bf16[128,256]{1,0:T(8,128)(2,1)S(1)}, bf16[128,256]{1,0:T(8,128)(2,1)S(1)}, u32[]{:S(2)}, u32[]{:S(2)}) collective-permute-start(bf16[128,256]{1,0:T(8,128)(2,1)S(1)} %get-tuple-element.78), channel_id=1, source_target_pairs={{0,2},{1,3},{2,0},{3,1},{4,6},{5,7},{6,4},{7,5},{8,10},{9,11},{10,... | collective-permute-start | bytes 196616 | tf_op jit(solution)/shard_map/ppermute | solution.py:595
  80.8 4.7 %route_in.1 = bf16[8,2,16,1152]{3,2,1,0:T(8,128)(2,1)} custom-call(s32[2]{0:T(128)S(1)} %pad_add_fusion.order_ref, bf16[2,144,768]{2,1,0:T(8,128)(2,1)S(1)} %pad_maximum_fusion.mine_ref, bf16[2,144,768]{2,1,0:T(8,128)(2,1)S(1)} %collective-permute-done.10.other_ref, bf16[2,1024,768]{2,1,0:T(8,128)(2,1)S(1)} %hold_weights.3.held_ref, ...), custom_call_target="tpu_custom_call" | custom-call | tf_op jit(solution)/shard_map/route_in/pallas_call | solution.py:401
  85.5 1.5 %all-to-all-done.2 = bf16[8,32,1152]{2,1,0:T(8,128)(2,1)} async-done(((bf16[8,32,1152]{2,1,0:T(8,128)(2,1)}), bf16[8,32,1152]{2,1,0:T(8,128)(2,1)}, u32[]{:S(2)}, u32[]{:S(2)}) %all-to-all-start.2) | async-done | bytes 589856 | tf_op jit(solution)/shard_map/all_to_all | solution.py:666
  87.1 4.2 %all-to-all-start.3 = ((bf16[8,32,1152]{2,1,0:T(8,128)(2,1)}), bf16[8,32,1152]{2,1,0:T(8,128)(2,1)S(1)}, u32[]{:S(2)}, u32[]{:S(2)}) async-start(bf16[8,32,1152]{2,1,0:T(8,128)(2,1)} %bitcast.75), calls=%async_computation.3 | async-start | bytes 1179648 | tf_op jit(solution)/shard_map/all_to_all | solution.py:666
  91.3 5.8 %all-gather = bf16[512,256]{1,0:T(8,128)(2,1)S(1)} all-gather(bf16[128,256]{1,0:T(8,128)(2,1)S(1)} %fusion.10), channel_id=2, replica_groups=mesh['ctx'=4,'exp'=8] {'ctx'}, dimensions={0}, use_global_device_ids=true | all-gather | bytes 327680 | tf_op jit(solution)/shard_map/all_gather | solution.py:737
  98.5 2.7 %combine_out.1 = bf16[128,1024]{1,0:T(8,128)(2,1)} custom-call(s32[2,128]{1,0:T(2,128)S(1)} %bitcast.68, f32[2,128]{1,0:T(2,128)S(1)} %bitcast.72, bf16[256,1152]{1,0:T(8,128)(2,1)} %bitcast.24.back_ref), custom_call_target="tpu_custom_call" | custom-call | flops 2249999872 | bytes 1179648 | tf_op jit(solution)/shard_map/combine_out/pallas_call | solution.py:175
  101.2 5.8 %all-to-all-done.3 = bf16[8,32,1152]{2,1,0:T(8,128)(2,1)S(1)} async-done(((bf16[8,32,1152]{2,1,0:T(8,128)(2,1)}), bf16[8,32,1152]{2,1,0:T(8,128)(2,1)S(1)}, u32[]{:S(2)}, u32[]{:S(2)}) %all-to-all-start.3) | async-done | bytes 589856 | tf_op jit(solution)/shard_map/all_to_all | solution.py:666
  107.0 1.5 %combine_in.1 = bf16[128,1024]{1,0:T(8,128)(2,1)} custom-call(s32[2,128]{1,0:T(2,128)S(1)} %bitcast.69, f32[2,128]{1,0:T(2,128)S(1)} %bitcast.73, bf16[256,1152]{1,0:T(8,128)(2,1)S(1)} %bitcast.65), custom_call_target="tpu_custom_call" | custom-call | flops 10000000 | bytes 1179648 | tf_op jit(solution)/shard_map/combine_in/pallas_call | solution.py:175
  (43 shorter events, 7.9 us)
Async XLA Ops:
  1.4 7.8 %collective-permute-start = (bf16[128,256]{1,0:T(8,128)(2,1)S(1)}, bf16[128,256]{1,0:T(8,128)(2,1)S(1)}, u32[]{:S(2)}, u32[]{:S(2)}) collective-permute-start(bf16[128,256]{1,0:T(8,128)(2,1)S(1)} %pad_maximum_fusion.5), channel_id=1, source_target_pairs={{0,4},{1,5},{2,6},{3,7},{4,0},{5,1},{6,2},{7,3},{8,12},{9,13},{10,... | collective-permute-start | bytes 196616 | tf_op jit(solution)/shard_map/ppermute | solution.py:595
  9.2 21.4 %all-to-all-start = ((bf16[8,32,1152]{2,1,0:T(8,128)(2,1)}), bf16[8,32,1152]{2,1,0:T(8,128)(2,1)}, u32[]{:S(2)}, u32[]{:S(2)}) async-start(bf16[8,32,1152]{2,1,0:T(8,128)(2,1)} %bitcast.4), calls=%async_computation | async-start | bytes 1179648 | tf_op jit(solution)/shard_map/all_to_all | solution.py:666
  14.8 13.0 %collective-permute-start.1 = (bf16[256,256]{1,0:T(8,128)(2,1)S(1)}, bf16[256,256]{1,0:T(8,128)(2,1)}, u32[]{:S(2)}, u32[]{:S(2)}) collective-permute-start(bf16[256,256]{1,0:T(8,128)(2,1)S(1)} %pad_maximum_fusion.2), channel_id=1, source_target_pairs={{0,2},{1,3},{2,0},{3,1},{4,6},{5,7},{6,4},{7,5},{8,10},{9,11},{10,... | collective-permute-start | bytes 393224 | tf_op jit(solution)/shard_map/ppermute | solution.py:595
  33.3 1.9 %collective-permute-start.2 = (bf16[2,144,768]{2,1,0:T(8,128)(2,1)S(1)}, bf16[2,144,768]{2,1,0:T(8,128)(2,1)S(1)}, u32[]{:S(2)}, u32[]{:S(2)}) collective-permute-start(bf16[2,144,768]{2,1,0:T(8,128)(2,1)S(1)} %get-tuple-element.43), channel_id=1, source_target_pairs={{0,8},{8,0},{16,24},{24,16},{1,9},{9,1},{17,25},{25,17},{2,10},{10... | collective-permute-start | bytes 1327112 | tf_op jit(solution)/shard_map/ppermute | solution.py:595
  33.4 9.7 %collective-permute-start.3 = (bf16[512,256]{1,0:T(8,128)(2,1)}, bf16[512,256]{1,0:T(8,128)(2,1)S(1)}, u32[]{:S(2)}, u32[]{:S(2)}) collective-permute-start(bf16[512,256]{1,0:T(8,128)(2,1)} %pad_maximum_fusion.1.kv_ref), channel_id=1, source_target_pairs={{0,1},{1,0},{2,3},{3,2},{4,5},{5,4},{6,7},{7,6},{8,9},{9,8},{10,11... | collective-permute-start | bytes 786440 | tf_op jit(solution)/shard_map/ppermute | solution.py:595
  36.5 16.4 %collective-permute-start.5 = (bf16[2,144,768]{2,1,0:T(8,128)(2,1)}, bf16[2,144,768]{2,1,0:T(8,128)(2,1)}, u32[]{:S(2)}, u32[]{:S(2)}) collective-permute-start(bf16[2,144,768]{2,1,0:T(8,128)(2,1)} %gate_up_keep.1), channel_id=1, source_target_pairs={{0,16},{8,24},{16,0},{24,8},{1,17},{9,25},{17,1},{25,9},{2,18},{10... | collective-permute-start | bytes 1327112 | tf_op jit(solution)/shard_map/ppermute | solution.py:595
  38.1 21.0 %all-to-all-start.1 = ((bf16[8,32,1152]{2,1,0:T(8,128)(2,1)}), bf16[8,32,1152]{2,1,0:T(8,128)(2,1)}, u32[]{:S(2)}, u32[]{:S(2)}) async-start(bf16[8,32,1152]{2,1,0:T(8,128)(2,1)} %bitcast.6), calls=%async_computation.1 | async-start | bytes 1179648 | tf_op jit(solution)/shard_map/all_to_all | solution.py:666
  43.1 13.6 %copy-start = (bf16[2,768,1024]{2,1,0:T(8,128)(2,1)S(1)}, bf16[2,768,1024]{2,1,0:T(8,128)(2,1)}, u32[]{:S(2)}) copy-start(bf16[2,768,1024]{2,1,0:T(8,128)(2,1)} %down_ref.5) | copy-start | bytes 9437188
  52.9 3.7 %copy-start.1 = (f32[512,256]{1,0:T(8,128)}, f32[512,256]{1,0:T(8,128)S(1)}, u32[]{:S(2)}) copy-start(f32[512,256]{1,0:T(8,128)S(1)} %get-tuple-element.47) | copy-start | bytes 1572868
  54.5 2.2 %collective-permute-start.6 = (bf16[144,768]{1,0:T(8,128)(2,1)S(1)}, bf16[144,768]{1,0:T(8,128)(2,1)S(1)}, u32[]{:S(2)}, u32[]{:S(2)}) collective-permute-start(bf16[144,768]{1,0:T(8,128)(2,1)S(1)} %fusion.5.mine_ref), channel_id=1, source_target_pairs={{0,8},{8,0},{16,24},{24,16},{1,9},{9,1},{17,25},{25,17},{2,10},{10... | collective-permute-start | bytes 663560 | tf_op jit(solution)/shard_map/ppermute | solution.py:595
  54.6 16.3 %collective-permute-start.4 = (bf16[512,256]{1,0:T(8,128)(2,1)}, bf16[512,256]{1,0:T(8,128)(2,1)}, u32[]{:S(2)}, u32[]{:S(2)}) collective-permute-start(bf16[512,256]{1,0:T(8,128)(2,1)} %get-tuple-element.48), channel_id=1, source_target_pairs={{0,1},{1,0},{2,3},{3,2},{4,5},{5,4},{6,7},{7,6},{8,9},{9,8},{10,11... | collective-permute-start | bytes 786440 | tf_op jit(solution)/shard_map/ppermute | solution.py:595
  61.5 5.4 %collective-permute-start.7 = (bf16[144,768]{1,0:T(8,128)(2,1)}, bf16[144,768]{1,0:T(8,128)(2,1)}, u32[]{:S(2)}, u32[]{:S(2)}) collective-permute-start(bf16[144,768]{1,0:T(8,128)(2,1)} %get-tuple-element.53), channel_id=1, source_target_pairs={{0,8},{8,0},{16,24},{24,16},{1,9},{9,1},{17,25},{25,17},{2,10},{10... | collective-permute-start | bytes 663560 | tf_op jit(solution)/shard_map/ppermute | solution.py:595
  61.5 25.6 %all-to-all-start.2 = ((bf16[8,32,1152]{2,1,0:T(8,128)(2,1)}), bf16[8,32,1152]{2,1,0:T(8,128)(2,1)}, u32[]{:S(2)}, u32[]{:S(2)}) async-start(bf16[8,32,1152]{2,1,0:T(8,128)(2,1)} %bitcast.74), calls=%async_computation.2 | async-start | bytes 1179648 | tf_op jit(solution)/shard_map/all_to_all | solution.py:666
  68.4 3.7 %copy-start.2 = (f32[512,256]{1,0:T(8,128)S(1)}, f32[512,256]{1,0:T(8,128)}, u32[]{:S(2)}) copy-start(f32[512,256]{1,0:T(8,128)} %copy-done.1) | copy-start | bytes 1572868
  68.4 7.5 %collective-permute-start.9 = (bf16[144,768]{1,0:T(8,128)(2,1)S(1)}, bf16[144,768]{1,0:T(8,128)(2,1)S(1)}, u32[]{:S(2)}, u32[]{:S(2)}) collective-permute-start(bf16[144,768]{1,0:T(8,128)(2,1)S(1)} %hidden_grad_keep.1), channel_id=1, source_target_pairs={{0,16},{8,24},{16,0},{24,8},{1,17},{9,25},{17,1},{25,9},{2,18},{10... | collective-permute-start | bytes 663560 | tf_op jit(solution)/shard_map/ppermute | solution.py:595
  76.2 4.6 %collective-permute-start.10 = (bf16[2,144,768]{2,1,0:T(8,128)(2,1)S(1)}, bf16[2,144,768]{2,1,0:T(8,128)(2,1)S(1)}, u32[]{:S(2)}, u32[]{:S(2)}) collective-permute-start(bf16[2,144,768]{2,1,0:T(8,128)(2,1)S(1)} %pad_maximum_fusion.mine_ref), channel_id=1, source_target_pairs={{0,8},{8,0},{16,24},{24,16},{1,9},{9,1},{17,25},{25,17},{2,10},{10... | collective-permute-start | bytes 1327112 | tf_op jit(solution)/shard_map/ppermute | solution.py:595
  76.3 14.9 %collective-permute-start.8 = (bf16[128,256]{1,0:T(8,128)(2,1)S(1)}, bf16[128,256]{1,0:T(8,128)(2,1)S(1)}, u32[]{:S(2)}, u32[]{:S(2)}) collective-permute-start(bf16[128,256]{1,0:T(8,128)(2,1)S(1)} %get-tuple-element.76), channel_id=1, source_target_pairs={{0,4},{1,5},{2,6},{3,7},{4,0},{5,1},{6,2},{7,3},{8,12},{9,13},{10,... | collective-permute-start | bytes 196616 | tf_op jit(solution)/shard_map/ppermute | solution.py:595
  79.0 12.2 %collective-permute-start.11 = (bf16[128,256]{1,0:T(8,128)(2,1)S(1)}, bf16[128,256]{1,0:T(8,128)(2,1)S(1)}, u32[]{:S(2)}, u32[]{:S(2)}) collective-permute-start(bf16[128,256]{1,0:T(8,128)(2,1)S(1)} %get-tuple-element.78), channel_id=1, source_target_pairs={{0,2},{1,3},{2,0},{3,1},{4,6},{5,7},{6,4},{7,5},{8,10},{9,11},{10,... | collective-permute-start | bytes 196616 | tf_op jit(solution)/shard_map/ppermute | solution.py:595
  80.5 18.0 %copy-start.3 = (s32[128,2]{0,1:T(2,128)S(1)}, s32[128,2]{0,1:T(2,128)}, u32[]{:S(2)}) copy-start(s32[128,2]{0,1:T(2,128)} %param.17) | copy-start | bytes 3076
  80.5 18.0 %copy-start.4 = (f32[128,2]{0,1:T(2,128)S(1)}, f32[128,2]{0,1:T(2,128)}, u32[]{:S(2)}) copy-start(f32[128,2]{0,1:T(2,128)} %param.18) | copy-start | bytes 3076
  80.5 10.8 %collective-permute-start.12 = (bf16[128,256]{1,0:T(8,128)(2,1)S(1)}, bf16[128,256]{1,0:T(8,128)(2,1)S(1)}, u32[]{:S(2)}, u32[]{:S(2)}) collective-permute-start(bf16[128,256]{1,0:T(8,128)(2,1)S(1)} %get-tuple-element.77), channel_id=1, source_target_pairs={{0,6},{1,7},{2,4},{3,5},{4,2},{5,3},{6,0},{7,1},{8,14},{9,15},{10,... | collective-permute-start | bytes 196616 | tf_op jit(solution)/shard_map/ppermute | solution.py:595
  87.1 19.9 %all-to-all-start.3 = ((bf16[8,32,1152]{2,1,0:T(8,128)(2,1)}), bf16[8,32,1152]{2,1,0:T(8,128)(2,1)S(1)}, u32[]{:S(2)}, u32[]{:S(2)}) async-start(bf16[8,32,1152]{2,1,0:T(8,128)(2,1)} %bitcast.75), calls=%async_computation.3 | async-start | bytes 1179648 | tf_op jit(solution)/shard_map/all_to_all | solution.py:666

commit v6 on v5

--- a/solution.py
+++ b/solution.py
@@ -471,7 +471,6 @@
     every = range(pairs)
     q = [stacked(q_ref, pair) for pair in every]
     g = [stacked(g_ref, pair) for pair in every]
-    q_t = [jnp.transpose(value) for value in q]
     g_t = [jnp.transpose(value) for value in g]
     top, inverse, row_dot = {}, {}, {}
 
@@ -483,7 +482,7 @@
     def score_stage(pair):
         largest = jnp.full((1, lanes), -jnp.inf, F32)
         for at in chunks:
-            scores = dot(piece(at, 0), q_t[pair])
+            scores = dot(piece(at, 0), q[pair], 1, 1)
             for part in range(0, chunk, tokens):
                 allowed = ahead <= limits[(at + part) // tokens]
                 some = jnp.where(allowed, scores[part : part + tokens], -jnp.inf)
@@ -533,8 +532,8 @@
     @pl.when(step == pl.num_programs(0) - 1)
     def _():
         if last:
-            keep_ref[:, :d] = key_acc[:half, :] * scale
-            keep_ref[:, d:] = value_acc[:half, :]
+            keep_ref[:, :d] = (key_acc[:half, :] * scale).astype(BF16)
+            keep_ref[:, d:] = value_acc[:half, :].astype(BF16)
             send_ref[:, :d] = (key_acc[half:, :] * scale).astype(BF16)
             send_ref[:, d:] = value_acc[half:, :].astype(BF16)
         else:
@@ -559,7 +558,7 @@
     held = pl.BlockSpec(memory_space=pl.ANY)
     wide = jax.ShapeDtypeStruct(queries.shape, BF16)
     if last:
-        final = [jax.ShapeDtypeStruct((half, both), F32), jax.ShapeDtypeStruct((half, both), BF16)]
+        final = [jax.ShapeDtypeStruct((half, both), BF16)] * 2
     else:
         final = [jax.ShapeDtypeStruct((seq, both), F32)]
     return pl.pallas_call(
@@ -713,7 +712,7 @@
     hg_part = hidden_grad_keep(mine, rows, down_proj, hg_recv)
     held = hold(mine, after(gate_proj, hg_part), up_proj)
 
-    kv_sum = kv_keep + after(kv_recv, hg_part).astype(F32)
+    kv_sum = kv_keep.astype(F32) + after(kv_recv, hg_part).astype(F32)
     kv_low = kv_sum.astype(BF16)
     blocks = exp_count // 2
     kv_parts = [

time: 109 us -> 109 us (level)
  no operation moved by 1% of the time
where the time goes in v6:
time: 109 us; the launch traced here: 108 us
  Pallas kernels  37.7 us (35%)
  starting transfers between devices  36.6 us (34%)
  waiting for transfers between devices  19.4 us (18%)
  other arithmetic  7.13 us (7%)
  blocking collectives  5.79 us (5%)
    all_to_all x4, starting transfers between devices, exchange(): return lax.all_to_all(flat, 'exp', split_axis=0, concat_axis=0, tiled=True)  20.1 us
    ppermute x13, starting transfers between devices, swap(): return lax.ppermute(value, axis, [(i, i ^ bit) for i in range(count)])  16.5 us
    pallas_call x6, Pallas kernels, expert_call(): pl.pallas_call(kernel, in_specs=specs, out_specs=[in_vmem] * len(out_shap...  11.8 us
    ppermute x13, waiting for transfers between devices, swap(): return lax.ppermute(value, axis, [(i, i ^ bit) for i in range(count)])  10.6 us
    pallas_call x1, Pallas kernels, attention(): pl.pallas_call(functools.partial(attention_kernel, offsets, tokens, chunk...  9.84 us
    all_to_all x4, waiting for transfers between devices, exchange(): return lax.all_to_all(flat, 'exp', split_axis=0, concat_axis=0, tiled=True)  8.79 us
    all_gather x1, blocking collectives, body(): lax.all_gather(after(kv_total, in_rows), 'ctx', axis=0, tiled=False)  5.79 us
    pallas_call x2, Pallas kernels, dispatch(): pl.pallas_call(functools.partial(dispatch_kernel, slots, weighted), out_s...  4.89 us
  transfers between devices with their start and end apart: 17, of which 8 were waited for; matrix products, arithmetic and copies ran while one was open for 7% of the time, Pallas kernels for 31%

profile of v6, /device:TPU:0, one launch (start us, length us, event | category | flops | bytes accessed | tf_op | source)
XLA Modules:
  0.0 108.4 jit_solution(17069411818714336950)
XLA Ops:
  1.4 4.1 %collective-permute-start = (bf16[128,256]{1,0:T(8,128)(2,1)S(1)}, bf16[128,256]{1,0:T(8,128)(2,1)S(1)}, u32[]{:S(2)}, u32[]{:S(2)}) collective-permute-start(bf16[128,256]{1,0:T(8,128)(2,1)S(1)} %pad_maximum_fusion.5), channel_id=1, source_target_pairs={{0,4},{1,5},{2,6},{3,7},{4,0},{5,1},{6,2},{7,3},{8,12},{9,13},{10,... | collective-permute-start | bytes 196616 | tf_op jit(solution)/shard_map/ppermute | solution.py:594
  5.5 2.4 %dispatch_rows.1 = bf16[256,1152]{1,0:T(8,128)(2,1)} custom-call(s32[2,128]{1,0:T(2,128)} %bitcast.66, f32[2,128]{1,0:T(2,128)} %bitcast.70, bf16[128,1024]{1,0:T(8,128)(2,1)} %rows_ref.1), custom_call_target="tpu_custom_call" | custom-call | flops 134217728 | bytes 1179648 | tf_op jit(solution)/shard_map/dispatch_rows/pallas_call | solution.py:131
  7.9 1.3 %collective-permute-done = bf16[128,256]{1,0:T(8,128)(2,1)S(1)} collective-permute-done((bf16[128,256]{1,0:T(8,128)(2,1)S(1)}, bf16[128,256]{1,0:T(8,128)(2,1)S(1)}, u32[]{:S(2)}, u32[]{:S(2)}) %collective-permute-start) | collective-permute-done | bytes 65568 | tf_op jit(solution)/shard_map/ppermute | solution.py:594
  9.2 5.6 %all-to-all-start = ((bf16[8,32,1152]{2,1,0:T(8,128)(2,1)}), bf16[8,32,1152]{2,1,0:T(8,128)(2,1)}, u32[]{:S(2)}, u32[]{:S(2)}) async-start(bf16[8,32,1152]{2,1,0:T(8,128)(2,1)} %bitcast.4), calls=%async_computation | async-start | bytes 1179648 | tf_op jit(solution)/shard_map/all_to_all | solution.py:665
  14.8 2.0 %collective-permute-start.1 = (bf16[256,256]{1,0:T(8,128)(2,1)S(1)}, bf16[256,256]{1,0:T(8,128)(2,1)}, u32[]{:S(2)}, u32[]{:S(2)}) collective-permute-start(bf16[256,256]{1,0:T(8,128)(2,1)S(1)} %pad_maximum_fusion.2), channel_id=1, source_target_pairs={{0,2},{1,3},{2,0},{3,1},{4,6},{5,7},{6,4},{7,5},{8,10},{9,11},{10,... | collective-permute-start | bytes 393224 | tf_op jit(solution)/shard_map/ppermute | solution.py:594
  17.0 2.5 %dispatch_scaled.1 = bf16[256,1152]{1,0:T(8,128)(2,1)} custom-call(s32[2,128]{1,0:T(2,128)} %bitcast.67, f32[2,128]{1,0:T(2,128)} %bitcast.71, bf16[128,1024]{1,0:T(8,128)(2,1)} %rows_ref.2), custom_call_target="tpu_custom_call" | custom-call | flops 134217728 | bytes 1179648 | tf_op jit(solution)/shard_map/dispatch_scaled/pallas_call | solution.py:131
  19.5 1.9 %hold_weights.2.held_ref = bf16[2,1024,768]{2,1,0:T(8,128)(2,1)S(1)} custom-call(s32[1]{0:T(128)S(6)} %sub.8.expert_ref, bf16[2,1024,768]{2,1,0:T(8,128)(2,1)} %gate_ref.5, bf16[2,1024,768]{2,1,0:T(8,128)(2,1)} %up_ref.7), custom_call_target="tpu_custom_call" | custom-call | tf_op jit(solution)/shard_map/hold_weights/pallas_call | solution.py:258
  21.4 6.3 %collective-permute-done.1 = bf16[256,256]{1,0:T(8,128)(2,1)} collective-permute-done((bf16[256,256]{1,0:T(8,128)(2,1)S(1)}, bf16[256,256]{1,0:T(8,128)(2,1)}, u32[]{:S(2)}, u32[]{:S(2)}) %collective-permute-start.1) | collective-permute-done | bytes 131104 | tf_op jit(solution)/shard_map/ppermute | solution.py:594
  27.8 1.6 %pad_maximum_fusion.1.kv_ref = bf16[512,256]{1,0:T(8,128)(2,1)} fusion(bf16[256,256]{1,0:T(8,128)(2,1)} %collective-permute-done.1, bf16[128,256]{1,0:T(8,128)(2,1)S(1)} %collective-permute-done, bf16[128,128]{1,0:T(8,128)(2,1)S(1)} %get-tuple-element.79, bf16[128,128]{1,0:T(8,128)(2,1)S(1)} %get-tuple-element.80), kind=kLoop, calls=%fused_computation.17 | loop fusion | flops 1048576 | bytes 524288 | tf_op jit(solution)/shard_map/concatenate | solution.py:683
  30.6 2.6 %gate_up_send.1 = (bf16[2,144,768]{2,1,0:T(8,128)(2,1)S(1)}, bf16[2,1024,768]{2,1,0:T(8,128)(2,1)S(1)}, bf16[144,1024]{1,0:T(8,128)(2,1)S(1)}) custom-call(s32[2]{0:T(128)S(1)} %rev.4.order_ref, bf16[8,2,16,1152]{3,2,1,0:T(8,128)(2,1)} %bitcast.5.recv_ref, bf16[2,1024,768]{2,1,0:T(8,128)(2,1)S(1)} %hold_weights.2.held_ref, bf16[2,1024,768]{2,1,0:T(8,128)(2,1)} %gate_ref.5, ...), custom_call_target="tpu_custom_call" | custom-call | tf_op jit(solution)/shard_map/gate_up_send/pallas_call | solution.py:258
  33.4 1.5 %collective-permute-start.3 = (bf16[512,256]{1,0:T(8,128)(2,1)}, bf16[512,256]{1,0:T(8,128)(2,1)S(1)}, u32[]{:S(2)}, u32[]{:S(2)}) collective-permute-start(bf16[512,256]{1,0:T(8,128)(2,1)} %pad_maximum_fusion.1.kv_ref), channel_id=1, source_target_pairs={{0,1},{1,0},{2,3},{3,2},{4,5},{5,4},{6,7},{7,6},{8,9},{9,8},{10,11... | collective-permute-start | bytes 786440 | tf_op jit(solution)/shard_map/ppermute | solution.py:594
  35.1 1.4 %gate_up_keep.1 = bf16[2,144,768]{2,1,0:T(8,128)(2,1)} custom-call(bf16[144,1024]{1,0:T(8,128)(2,1)S(1)} %get-tuple-element.41.rows_ref, bf16[2,1024,768]{2,1,0:T(8,128)(2,1)S(1)} %get-tuple-element.42.held_ref, bf16[2,144,768]{2,1,0:T(8,128)(2,1)S(1)} %collective-permute-done.2.arrived_ref), custom_call_target="tpu_custom_call" | custom-call | tf_op jit(solution)/shard_map/gate_up_keep/pallas_call | solution.py:258
  36.5 1.5 %collective-permute-start.5 = (bf16[2,144,768]{2,1,0:T(8,128)(2,1)}, bf16[2,144,768]{2,1,0:T(8,128)(2,1)}, u32[]{:S(2)}, u32[]{:S(2)}) collective-permute-start(bf16[2,144,768]{2,1,0:T(8,128)(2,1)} %gate_up_keep.1), channel_id=1, source_target_pairs={{0,16},{8,24},{16,0},{24,8},{1,17},{9,25},{17,1},{25,9},{2,18},{10... | collective-permute-start | bytes 1327112 | tf_op jit(solution)/shard_map/ppermute | solution.py:594
  38.1 5.0 %all-to-all-start.1 = ((bf16[8,32,1152]{2,1,0:T(8,128)(2,1)}), bf16[8,32,1152]{2,1,0:T(8,128)(2,1)}, u32[]{:S(2)}, u32[]{:S(2)}) async-start(bf16[8,32,1152]{2,1,0:T(8,128)(2,1)} %bitcast.6), calls=%async_computation.1 | async-start | bytes 1179648 | tf_op jit(solution)/shard_map/all_to_all | solution.py:665
  43.1 9.8 %attention.1 = (bf16[128,2048]{1,0:T(8,128)(2,1)}, bf16[128,2048]{1,0:T(8,128)(2,1)}, bf16[512,256]{1,0:T(8,128)(2,1)S(1)}, bf16[512,256]{1,0:T(8,128)(2,1)}) custom-call(s32[1]{0:T(128)} %bitcast.me_ref, bf16[128,2048]{1,0:T(8,128)(2,1)} %q_ref, bf16[128,2048]{1,0:T(8,128)(2,1)} %g_ref.1, bf16[512,256]{1,0:T(8,128)(2,1)} %pad_maximum_fusion.1.kv_ref, ...), custom_call_target="tpu_custom_call" | custom-call | flops 3221225472 | bytes 2097152 | tf_op jit(solution)/shard_map/attention/pallas_call | solution.py:564
  52.9 1.3 %convert_add_fusion.1 = f32[2,144,768]{2,1,0:T(8,128)S(1)} fusion(bf16[2,144,768]{2,1,0:T(8,128)(2,1)} %collective-permute-done.5, bf16[2,144,768]{2,1,0:T(8,128)(2,1)} %gate_up_keep.1), kind=kLoop, calls=%fused_computation.1 | loop fusion | flops 663552 | bytes 1769472 | tf_op jit(solution)/shard_map/add | solution.py:625
  54.5 2.1 %collective-permute-start.4 = (bf16[512,256]{1,0:T(8,128)(2,1)}, bf16[512,256]{1,0:T(8,128)(2,1)}, u32[]{:S(2)}, u32[]{:S(2)}) collective-permute-start(bf16[512,256]{1,0:T(8,128)(2,1)} %get-tuple-element.48), channel_id=1, source_target_pairs={{0,1},{1,0},{2,3},{3,2},{4,5},{5,4},{6,7},{7,6},{8,9},{9,8},{10,11... | collective-permute-start | bytes 786440 | tf_op jit(solution)/shard_map/ppermute | solution.py:594
  56.6 2.2 %route_out.1 = bf16[8,2,16,1152]{3,2,1,0:T(8,128)(2,1)} custom-call(s32[2]{0:T(128)S(1)} %pad_add_fusion.order_ref, bf16[144,768]{1,0:T(8,128)(2,1)S(1)} %fusion.5.mine_ref, bf16[144,768]{1,0:T(8,128)(2,1)S(1)} %collective-permute-done.6.other_ref, bf16[2,768,1024]{2,1,0:T(8,128)(2,1)S(1)} %copy-done), custom_call_target="tpu_custom_call" | custom-call | tf_op jit(solution)/shard_map/route_out/pallas_call | solution.py:365
  59.1 2.4 %hidden_grad_send.1 = (bf16[144,768]{1,0:T(8,128)(2,1)}, bf16[144,1024]{1,0:T(8,128)(2,1)S(1)}) custom-call(s32[2]{0:T(128)S(1)} %rev.4.order_ref, bf16[8,2,16,1152]{3,2,1,0:T(8,128)(2,1)} %bitcast.7.recv_ref, bf16[2,768,1024]{2,1,0:T(8,128)(2,1)S(1)} %copy-done), custom_call_target="tpu_custom_call" | custom-call | tf_op jit(solution)/shard_map/hidden_grad_send/pallas_call | solution.py:258
  61.5 5.3 %all-to-all-start.2 = ((bf16[8,32,1152]{2,1,0:T(8,128)(2,1)}), bf16[8,32,1152]{2,1,0:T(8,128)(2,1)}, u32[]{:S(2)}, u32[]{:S(2)}) async-start(bf16[8,32,1152]{2,1,0:T(8,128)(2,1)} %bitcast.74), calls=%async_computation.2 | async-start | bytes 1179648 | tf_op jit(solution)/shard_map/all_to_all | solution.py:665
  66.7 1.6 %hidden_grad_keep.1 = bf16[144,768]{1,0:T(8,128)(2,1)S(1)} custom-call(s32[1]{0:T(128)} %bitcast.1.expert_ref, bf16[144,1024]{1,0:T(8,128)(2,1)S(1)} %get-tuple-element.52.rows_ref, bf16[2,768,1024]{2,1,0:T(8,128)(2,1)S(1)} %copy-done, bf16[144,768]{1,0:T(8,128)(2,1)} %collective-permute-done.7.arrived_ref), custom_call_target="tpu_custom_call" | custom-call | tf_op jit(solution)/shard_map/hidden_grad_keep/pallas_call | solution.py:258
  68.9 1.9 %hold_weights.3.held_ref = bf16[2,1024,768]{2,1,0:T(8,128)(2,1)S(1)} custom-call(s32[1]{0:T(128)} %bitcast.1.expert_ref, bf16[2,1024,768]{2,1,0:T(8,128)(2,1)} %gate_ref.5, bf16[2,1024,768]{2,1,0:T(8,128)(2,1)} %up_ref.7), custom_call_target="tpu_custom_call" | custom-call | tf_op jit(solution)/shard_map/hold_weights/pallas_call | solution.py:258
  73.1 2.7 %collective-permute-done.9 = bf16[144,768]{1,0:T(8,128)(2,1)S(1)} collective-permute-done((bf16[144,768]{1,0:T(8,128)(2,1)S(1)}, bf16[144,768]{1,0:T(8,128)(2,1)S(1)}, u32[]{:S(2)}, u32[]{:S(2)}) %collective-permute-start.9) | collective-permute-done | bytes 221216 | tf_op jit(solution)/shard_map/ppermute | solution.py:594
  76.2 2.7 %collective-permute-start.8 = (bf16[128,256]{1,0:T(8,128)(2,1)S(1)}, bf16[128,256]{1,0:T(8,128)(2,1)S(1)}, u32[]{:S(2)}, u32[]{:S(2)}) collective-permute-start(bf16[128,256]{1,0:T(8,128)(2,1)S(1)} %get-tuple-element.76), channel_id=1, source_target_pairs={{0,4},{1,5},{2,6},{3,7},{4,0},{5,1},{6,2},{7,3},{8,12},{9,13},{10,... | collective-permute-start | bytes 196616 | tf_op jit(solution)/shard_map/ppermute | solution.py:594
  78.9 1.5 %collective-permute-start.11 = (bf16[128,256]{1,0:T(8,128)(2,1)S(1)}, bf16[128,256]{1,0:T(8,128)(2,1)S(1)}, u32[]{:S(2)}, u32[]{:S(2)}) collective-permute-start(bf16[128,256]{1,0:T(8,128)(2,1)S(1)} %get-tuple-element.78), channel_id=1, source_target_pairs={{0,2},{1,3},{2,0},{3,1},{4,6},{5,7},{6,4},{7,5},{8,10},{9,11},{10,... | collective-permute-start | bytes 196616 | tf_op jit(solution)/shard_map/ppermute | solution.py:594
  80.7 4.7 %route_in.1 = bf16[8,2,16,1152]{3,2,1,0:T(8,128)(2,1)} custom-call(s32[2]{0:T(128)S(1)} %pad_add_fusion.order_ref, bf16[2,144,768]{2,1,0:T(8,128)(2,1)S(1)} %pad_maximum_fusion.mine_ref, bf16[2,144,768]{2,1,0:T(8,128)(2,1)S(1)} %collective-permute-done.10.other_ref, bf16[2,1024,768]{2,1,0:T(8,128)(2,1)S(1)} %hold_weights.3.held_ref, ...), custom_call_target="tpu_custom_call" | custom-call | tf_op jit(solution)/shard_map/route_in/pallas_call | solution.py:401
  85.5 1.5 %all-to-all-done.2 = bf16[8,32,1152]{2,1,0:T(8,128)(2,1)} async-done(((bf16[8,32,1152]{2,1,0:T(8,128)(2,1)}), bf16[8,32,1152]{2,1,0:T(8,128)(2,1)}, u32[]{:S(2)}, u32[]{:S(2)}) %all-to-all-start.2) | async-done | bytes 589856 | tf_op jit(solution)/shard_map/all_to_all | solution.py:665
  87.0 4.2 %all-to-all-start.3 = ((bf16[8,32,1152]{2,1,0:T(8,128)(2,1)}), bf16[8,32,1152]{2,1,0:T(8,128)(2,1)S(1)}, u32[]{:S(2)}, u32[]{:S(2)}) async-start(bf16[8,32,1152]{2,1,0:T(8,128)(2,1)} %bitcast.75), calls=%async_computation.3 | async-start | bytes 1179648 | tf_op jit(solution)/shard_map/all_to_all | solution.py:665
  91.3 5.8 %all-gather = bf16[512,256]{1,0:T(8,128)(2,1)S(1)} all-gather(bf16[128,256]{1,0:T(8,128)(2,1)S(1)} %fusion.10), channel_id=2, replica_groups=mesh['ctx'=4,'exp'=8] {'ctx'}, dimensions={0}, use_global_device_ids=true | all-gather | bytes 327680 | tf_op jit(solution)/shard_map/all_gather | solution.py:736
  98.5 2.7 %combine_out.1 = bf16[128,1024]{1,0:T(8,128)(2,1)} custom-call(s32[2,128]{1,0:T(2,128)S(1)} %bitcast.68, f32[2,128]{1,0:T(2,128)S(1)} %bitcast.72, bf16[256,1152]{1,0:T(8,128)(2,1)} %bitcast.24.back_ref), custom_call_target="tpu_custom_call" | custom-call | flops 2249999872 | bytes 1179648 | tf_op jit(solution)/shard_map/combine_out/pallas_call | solution.py:175
  101.1 5.8 %all-to-all-done.3 = bf16[8,32,1152]{2,1,0:T(8,128)(2,1)S(1)} async-done(((bf16[8,32,1152]{2,1,0:T(8,128)(2,1)}), bf16[8,32,1152]{2,1,0:T(8,128)(2,1)S(1)}, u32[]{:S(2)}, u32[]{:S(2)}) %all-to-all-start.3) | async-done | bytes 589856 | tf_op jit(solution)/shard_map/all_to_all | solution.py:665
  106.9 1.5 %combine_in.1 = bf16[128,1024]{1,0:T(8,128)(2,1)} custom-call(s32[2,128]{1,0:T(2,128)S(1)} %bitcast.69, f32[2,128]{1,0:T(2,128)S(1)} %bitcast.73, bf16[256,1152]{1,0:T(8,128)(2,1)S(1)} %bitcast.65), custom_call_target="tpu_custom_call" | custom-call | flops 10000000 | bytes 1179648 | tf_op jit(solution)/shard_map/combine_in/pallas_call | solution.py:175
  (43 shorter events, 8.0 us)
Async XLA Ops:
  1.4 7.8 %collective-permute-start = (bf16[128,256]{1,0:T(8,128)(2,1)S(1)}, bf16[128,256]{1,0:T(8,128)(2,1)S(1)}, u32[]{:S(2)}, u32[]{:S(2)}) collective-permute-start(bf16[128,256]{1,0:T(8,128)(2,1)S(1)} %pad_maximum_fusion.5), channel_id=1, source_target_pairs={{0,4},{1,5},{2,6},{3,7},{4,0},{5,1},{6,2},{7,3},{8,12},{9,13},{10,... | collective-permute-start | bytes 196616 | tf_op jit(solution)/shard_map/ppermute | solution.py:594
  9.2 21.4 %all-to-all-start = ((bf16[8,32,1152]{2,1,0:T(8,128)(2,1)}), bf16[8,32,1152]{2,1,0:T(8,128)(2,1)}, u32[]{:S(2)}, u32[]{:S(2)}) async-start(bf16[8,32,1152]{2,1,0:T(8,128)(2,1)} %bitcast.4), calls=%async_computation | async-start | bytes 1179648 | tf_op jit(solution)/shard_map/all_to_all | solution.py:665
  14.8 13.0 %collective-permute-start.1 = (bf16[256,256]{1,0:T(8,128)(2,1)S(1)}, bf16[256,256]{1,0:T(8,128)(2,1)}, u32[]{:S(2)}, u32[]{:S(2)}) collective-permute-start(bf16[256,256]{1,0:T(8,128)(2,1)S(1)} %pad_maximum_fusion.2), channel_id=1, source_target_pairs={{0,2},{1,3},{2,0},{3,1},{4,6},{5,7},{6,4},{7,5},{8,10},{9,11},{10,... | collective-permute-start | bytes 393224 | tf_op jit(solution)/shard_map/ppermute | solution.py:594
  33.3 1.9 %collective-permute-start.2 = (bf16[2,144,768]{2,1,0:T(8,128)(2,1)S(1)}, bf16[2,144,768]{2,1,0:T(8,128)(2,1)S(1)}, u32[]{:S(2)}, u32[]{:S(2)}) collective-permute-start(bf16[2,144,768]{2,1,0:T(8,128)(2,1)S(1)} %get-tuple-element.43), channel_id=1, source_target_pairs={{0,8},{8,0},{16,24},{24,16},{1,9},{9,1},{17,25},{25,17},{2,10},{10... | collective-permute-start | bytes 1327112 | tf_op jit(solution)/shard_map/ppermute | solution.py:594
  33.4 9.7 %collective-permute-start.3 = (bf16[512,256]{1,0:T(8,128)(2,1)}, bf16[512,256]{1,0:T(8,128)(2,1)S(1)}, u32[]{:S(2)}, u32[]{:S(2)}) collective-permute-start(bf16[512,256]{1,0:T(8,128)(2,1)} %pad_maximum_fusion.1.kv_ref), channel_id=1, source_target_pairs={{0,1},{1,0},{2,3},{3,2},{4,5},{5,4},{6,7},{7,6},{8,9},{9,8},{10,11... | collective-permute-start | bytes 786440 | tf_op jit(solution)/shard_map/ppermute | solution.py:594
  36.5 16.4 %collective-permute-start.5 = (bf16[2,144,768]{2,1,0:T(8,128)(2,1)}, bf16[2,144,768]{2,1,0:T(8,128)(2,1)}, u32[]{:S(2)}, u32[]{:S(2)}) collective-permute-start(bf16[2,144,768]{2,1,0:T(8,128)(2,1)} %gate_up_keep.1), channel_id=1, source_target_pairs={{0,16},{8,24},{16,0},{24,8},{1,17},{9,25},{17,1},{25,9},{2,18},{10... | collective-permute-start | bytes 1327112 | tf_op jit(solution)/shard_map/ppermute | solution.py:594
  38.1 21.0 %all-to-all-start.1 = ((bf16[8,32,1152]{2,1,0:T(8,128)(2,1)}), bf16[8,32,1152]{2,1,0:T(8,128)(2,1)}, u32[]{:S(2)}, u32[]{:S(2)}) async-start(bf16[8,32,1152]{2,1,0:T(8,128)(2,1)} %bitcast.6), calls=%async_computation.1 | async-start | bytes 1179648 | tf_op jit(solution)/shard_map/all_to_all | solution.py:665
  43.1 13.5 %copy-start = (bf16[2,768,1024]{2,1,0:T(8,128)(2,1)S(1)}, bf16[2,768,1024]{2,1,0:T(8,128)(2,1)}, u32[]{:S(2)}) copy-start(bf16[2,768,1024]{2,1,0:T(8,128)(2,1)} %down_ref.5) | copy-start | bytes 9437188
  52.9 3.6 %copy-start.1 = (bf16[512,256]{1,0:T(8,128)(2,1)}, bf16[512,256]{1,0:T(8,128)(2,1)S(1)}, u32[]{:S(2)}) copy-start(bf16[512,256]{1,0:T(8,128)(2,1)S(1)} %get-tuple-element.47) | copy-start | bytes 786436
  54.4 2.2 %collective-permute-start.6 = (bf16[144,768]{1,0:T(8,128)(2,1)S(1)}, bf16[144,768]{1,0:T(8,128)(2,1)S(1)}, u32[]{:S(2)}, u32[]{:S(2)}) collective-permute-start(bf16[144,768]{1,0:T(8,128)(2,1)S(1)} %fusion.5.mine_ref), channel_id=1, source_target_pairs={{0,8},{8,0},{16,24},{24,16},{1,9},{9,1},{17,25},{25,17},{2,10},{10... | collective-permute-start | bytes 663560 | tf_op jit(solution)/shard_map/ppermute | solution.py:594
  54.5 16.3 %collective-permute-start.4 = (bf16[512,256]{1,0:T(8,128)(2,1)}, bf16[512,256]{1,0:T(8,128)(2,1)}, u32[]{:S(2)}, u32[]{:S(2)}) collective-permute-start(bf16[512,256]{1,0:T(8,128)(2,1)} %get-tuple-element.48), channel_id=1, source_target_pairs={{0,1},{1,0},{2,3},{3,2},{4,5},{5,4},{6,7},{7,6},{8,9},{9,8},{10,11... | collective-permute-start | bytes 786440 | tf_op jit(solution)/shard_map/ppermute | solution.py:594
  61.5 5.3 %collective-permute-start.7 = (bf16[144,768]{1,0:T(8,128)(2,1)}, bf16[144,768]{1,0:T(8,128)(2,1)}, u32[]{:S(2)}, u32[]{:S(2)}) collective-permute-start(bf16[144,768]{1,0:T(8,128)(2,1)} %get-tuple-element.53), channel_id=1, source_target_pairs={{0,8},{8,0},{16,24},{24,16},{1,9},{9,1},{17,25},{25,17},{2,10},{10... | collective-permute-start | bytes 663560 | tf_op jit(solution)/shard_map/ppermute | solution.py:594
  61.5 25.5 %all-to-all-start.2 = ((bf16[8,32,1152]{2,1,0:T(8,128)(2,1)}), bf16[8,32,1152]{2,1,0:T(8,128)(2,1)}, u32[]{:S(2)}, u32[]{:S(2)}) async-start(bf16[8,32,1152]{2,1,0:T(8,128)(2,1)} %bitcast.74), calls=%async_computation.2 | async-start | bytes 1179648 | tf_op jit(solution)/shard_map/all_to_all | solution.py:665
  68.3 3.7 %copy-start.2 = (bf16[512,256]{1,0:T(8,128)(2,1)S(1)}, bf16[512,256]{1,0:T(8,128)(2,1)}, u32[]{:S(2)}) copy-start(bf16[512,256]{1,0:T(8,128)(2,1)} %copy-done.1) | copy-start | bytes 786436
  68.3 7.5 %collective-permute-start.9 = (bf16[144,768]{1,0:T(8,128)(2,1)S(1)}, bf16[144,768]{1,0:T(8,128)(2,1)S(1)}, u32[]{:S(2)}, u32[]{:S(2)}) collective-permute-start(bf16[144,768]{1,0:T(8,128)(2,1)S(1)} %hidden_grad_keep.1), channel_id=1, source_target_pairs={{0,16},{8,24},{16,0},{24,8},{1,17},{9,25},{17,1},{25,9},{2,18},{10... | collective-permute-start | bytes 663560 | tf_op jit(solution)/shard_map/ppermute | solution.py:594
  76.1 4.6 %collective-permute-start.10 = (bf16[2,144,768]{2,1,0:T(8,128)(2,1)S(1)}, bf16[2,144,768]{2,1,0:T(8,128)(2,1)S(1)}, u32[]{:S(2)}, u32[]{:S(2)}) collective-permute-start(bf16[2,144,768]{2,1,0:T(8,128)(2,1)S(1)} %pad_maximum_fusion.mine_ref), channel_id=1, source_target_pairs={{0,8},{8,0},{16,24},{24,16},{1,9},{9,1},{17,25},{25,17},{2,10},{10... | collective-permute-start | bytes 1327112 | tf_op jit(solution)/shard_map/ppermute | solution.py:594
  76.2 15.0 %collective-permute-start.8 = (bf16[128,256]{1,0:T(8,128)(2,1)S(1)}, bf16[128,256]{1,0:T(8,128)(2,1)S(1)}, u32[]{:S(2)}, u32[]{:S(2)}) collective-permute-start(bf16[128,256]{1,0:T(8,128)(2,1)S(1)} %get-tuple-element.76), channel_id=1, source_target_pairs={{0,4},{1,5},{2,6},{3,7},{4,0},{5,1},{6,2},{7,3},{8,12},{9,13},{10,... | collective-permute-start | bytes 196616 | tf_op jit(solution)/shard_map/ppermute | solution.py:594
  78.9 12.3 %collective-permute-start.11 = (bf16[128,256]{1,0:T(8,128)(2,1)S(1)}, bf16[128,256]{1,0:T(8,128)(2,1)S(1)}, u32[]{:S(2)}, u32[]{:S(2)}) collective-permute-start(bf16[128,256]{1,0:T(8,128)(2,1)S(1)} %get-tuple-element.78), channel_id=1, source_target_pairs={{0,2},{1,3},{2,0},{3,1},{4,6},{5,7},{6,4},{7,5},{8,10},{9,11},{10,... | collective-permute-start | bytes 196616 | tf_op jit(solution)/shard_map/ppermute | solution.py:594
  80.4 18.0 %copy-start.3 = (s32[128,2]{0,1:T(2,128)S(1)}, s32[128,2]{0,1:T(2,128)}, u32[]{:S(2)}) copy-start(s32[128,2]{0,1:T(2,128)} %param.17) | copy-start | bytes 3076
  80.4 18.0 %copy-start.4 = (f32[128,2]{0,1:T(2,128)S(1)}, f32[128,2]{0,1:T(2,128)}, u32[]{:S(2)}) copy-start(f32[128,2]{0,1:T(2,128)} %param.18) | copy-start | bytes 3076
  80.4 10.8 %collective-permute-start.12 = (bf16[128,256]{1,0:T(8,128)(2,1)S(1)}, bf16[128,256]{1,0:T(8,128)(2,1)S(1)}, u32[]{:S(2)}, u32[]{:S(2)}) collective-permute-start(bf16[128,256]{1,0:T(8,128)(2,1)S(1)} %get-tuple-element.77), channel_id=1, source_target_pairs={{0,6},{1,7},{2,4},{3,5},{4,2},{5,3},{6,0},{7,1},{8,14},{9,15},{10,... | collective-permute-start | bytes 196616 | tf_op jit(solution)/shard_map/ppermute | solution.py:594
  87.0 19.9 %all-to-all-start.3 = ((bf16[8,32,1152]{2,1,0:T(8,128)(2,1)}), bf16[8,32,1152]{2,1,0:T(8,128)(2,1)S(1)}, u32[]{:S(2)}, u32[]{:S(2)}) async-start(bf16[8,32,1152]{2,1,0:T(8,128)(2,1)} %bitcast.75), calls=%async_computation.3 | async-start | bytes 1179648 | tf_op jit(solution)/shard_map/all_to_all | solution.py:665
